TPU v7x, 32 devices: a whole 2x2x4 slice. The times are simulated.
32 devices in a mesh: slab: 8 (over z, y), grp: 4 (over x, core).
Axes of the slice: x: 2, y: 2, z: 4, core: 2. Of those that a mesh axis runs over, the one named last changes fastest.
Arguments:
- tiles: bfloat16 [96, 27, 36864], P(('slab', 'grp')), may hold values from -0.0390625 to 0.0390625
- neighbours: int32 [96, 27], P('slab'), may hold values from 0 to 95, as said below
- t_cur: bfloat16 [96, 192, 512], P('slab', None, 'grp'), may hold values from -6 to 6
- t_prev: float32 [96, 192, 512], P('slab', None, 'grp'), may hold values from -6 to 6
- probes: float32 [96, 192, 512], P('slab', None, 'grp'), may hold values from -18 to 18
Outputs:
- t_next: float32 [96, 192, 512], P('slab', None, 'grp')
- moments: float32 [2, 512], P(None, 'grp')
Inputs may be any that keep to these rules, and one draw needn't show every extreme that they name: Block b lies in slab b // 12; each of its neighbours lies in the same slab or in one of the two slabs beside it, the last slab being beside the first.
All inputs are finite; a program needn't handle non-finite values.
Results may differ from a plain program's by a relative error of at most 0.0003.
Values may be sent and summed in bfloat16 or wider, within the bound.
No kernel may reach another device: no remote copies, remote signals or barrier semaphores. Data moves between devices by JAX's collectives and lax.ppermute only.
A program may use at most 192 MiB of HBM per device.

v0:
```python
import math

import jax
import jax.numpy as jnp
from jax import lax
from jax.sharding import PartitionSpec as P


def with_halo(value, sides, width):
    for axis, dim in sides:
        size, length = (lax.axis_size(axis), value.shape[dim])
        up = [(i, (i + 1) % size) for i in range(size)]
        down = [(j, i) for i, j in up]
        last = lax.slice_in_dim(value, length - width, length, axis=dim)
        leading = lax.slice_in_dim(value, 0, width, axis=dim)
        before = lax.ppermute(last, axis, up)
        after = lax.ppermute(leading, axis, down)
        value = jnp.concatenate([before, value, after], axis=dim)
    return value


def apply_rows(tile_rows, padded, locals_rows):
    width = padded.shape[1]
    squares = tile_rows.reshape(tile_rows.shape[:2] + (width, width))
    near = jnp.take(padded, locals_rows.reshape(-1), axis=0)
    near = near.reshape(locals_rows.shape + padded.shape[1:])
    return jnp.einsum("bkrc,bkcp->brp", squares, near, preferred_element_type=jnp.float32)


def shards(tiles, neighbours, t_cur, t_prev, probes):
    blocks_slab = t_cur.shape[0]
    slab_count = lax.axis_size("slab")
    my_slab = lax.axis_index("slab")
    slab_near = neighbours // blocks_slab
    local_ids = (slab_near - my_slab + 1) % slab_count * blocks_slab + neighbours % blocks_slab
    rows_dev = tiles.shape[0]
    mine = lax.dynamic_slice_in_dim(local_ids, lax.axis_index("grp") * rows_dev, rows_dev, 0)
    whole = lax.all_gather(t_cur, "grp", axis=2, tiled=True)
    padded = with_halo(whole, (("slab", 0),), blocks_slab)
    rows_image = apply_rows(tiles, padded, mine)
    image = lax.all_to_all(rows_image, "grp", split_axis=2, concat_axis=0, tiled=True)
    t_next = 2.0 * image - t_prev
    first = jnp.sum(probes * t_next, axis=(0, 1))
    second = jnp.sum(t_cur.astype(jnp.float32) * t_next, axis=(0, 1))
    first, second = lax.psum((first, second), "slab")
    factor = 1.0 / math.sqrt(slab_count * blocks_slab * t_cur.shape[1])
    moments = jnp.stack([first, second]) * factor
    return (t_next, moments)


def solution(mesh):
    placed = (
        P(("slab", "grp"), None, None),
        P("slab", None),
        P("slab", None, "grp"),
        P("slab", None, "grp"),
        P("slab", None, "grp"),
    )
    return jax.shard_map(
        shards,
        mesh=mesh,
        in_specs=placed,
        out_specs=(P("slab", None, "grp"), P(None, "grp")),
        check_vma=False,
    )
```

profile of v0, /device:TPU:0, one launch (start us, length us, event | category | flops | bytes accessed | tf_op | source)
XLA Modules:
  0.0 230.7 jit_solution(10757656988305396355)
XLA Ops:
  7.2 0.0 all-gather.2.cloned.1.call-start
  7.2 0.7 all-gather.2.cloned.1.call-update
  7.9 28.7 %all-gather.2.cloned.1.call-done = bf16[12,192,512]{2,1,0:T(8,128)(2,1)} async-done(((bf16[12,192,128]{2,1,0:T(8,128)(2,1)}), bf16[12,192,512]{2,1,0:T(8,128)(2,1)}) %all-gather.2.cloned.1.call-update) | async-done | bytes 2359312 | tf_op jit(solution)/shard_map/all_gather | solution.py:38
  36.6 1.5 collective-permute-start
  38.1 3.2 %collective-permute-start.1 = (bf16[12,192,512]{2,1,0:T(8,128)(2,1)}, bf16[12,192,512]{2,1,0:T(8,128)(2,1)}, u32[]{:S(2)}, u32[]{:S(2)}) collective-permute-start(bf16[12,192,512]{2,1,0:T(8,128)(2,1)} %all-gather.2.cloned.1.call-done), channel_id=1, source_target_pairs={{4,0},{8,4},{12,8},{16,12},{20,16},{24,20},{28,24},{0,28},{5,1},{9... | collective-permute-start | bytes 7077896 | tf_op jit(solution)/shard_map/ppermute | solution.py:17
  41.4 0.7 broadcast_compare_fusion
  42.1 0.7 fusion.16
  42.8 0.1 reshape.51
  42.9 0.0 copy-start
  42.9 12.2 %reshape.52 = bf16[3,27,192,192]{3,2,1,0:T(8,128)(2,1)} reshape(bf16[3,27,36864]{2,1,0:T(8,128)(2,1)} %param.5) | data formatting | bytes 11943936 | tf_op jit(solution)/shard_map/reshape | solution.py:24
  55.2 84.8 %collective-permute-done = bf16[12,192,512]{2,1,0:T(8,128)(2,1)} collective-permute-done((bf16[12,192,512]{2,1,0:T(8,128)(2,1)}, bf16[12,192,512]{2,1,0:T(8,128)(2,1)}, u32[]{:S(2)}, u32[]{:S(2)}) %collective-permute-start) | collective-permute-done | bytes 2359328 | tf_op jit(solution)/shard_map/ppermute | solution.py:16
  139.9 2.2 collective-permute-done.1
  142.1 0.0 copy-done
  142.1 5.8 %pad_maximum_fusion = bf16[36,192,512]{2,1,0:T(8,128)(2,1)} fusion(bf16[12,192,512]{2,1,0:T(8,128)(2,1)} %collective-permute-done.1, bf16[12,192,512]{2,1,0:T(8,128)(2,1)S(1)} %copy-done, bf16[12,192,512]{2,1,0:T(8,128)(2,1)} %collective-permute-done), kind=kLoop, calls=%fused_computation.5 | loop fusion | flops 7077888 | bytes 14155776 | tf_op jit(solution)/shard_map/concatenate | solution.py:18
  148.0 11.3 %gather_fusion = bf16[81,192,512]{2,1,0:T(8,128)(2,1)} fusion(bf16[36,192,512]{2,1,0:T(8,128)(2,1)} %pad_maximum_fusion, s32[1024]{0:T(1024)S(1)} %pad_clamp_fusion), kind=kCustom, calls=%fused_computation | custom fusion | bytes 31850820 | tf_op jit(solution)/shard_map/jit(_take)/gather | solution.py:25
  159.3 10.4 %fusion.4 = f32[3,192,512]{2,1,0:T(8,128)S(1)} fusion(bf16[3,27,192,192]{3,2,1,0:T(8,128)(2,1)} %reshape.52, bf16[3,27,192,512]{3,2,1,0:T(8,128)(2,1)} %bitcast.17, pred[3,27]{1,0:T(4,128)(4,1)S(1)} %get-tuple-element.7), kind=kOutput, calls=%fused_computation.6 | convolution fusion | flops 3065610240 | bytes 23076944 | tf_op jit(solution)/shard_map/bkrc,bkcp->brp/dot_general | solution.py:27
  169.7 0.9 copy.8
  170.7 28.2 %all_to_all.4 = f32[3,192,512]{1,0,2:T(4,128)S(1)} all-to-all(f32[3,192,512]{1,0,2:T(4,128)S(1)} %copy.8), channel_id=1, replica_groups=mesh['slab'=8,'grp'=4] {'grp'}, dimensions={2} | all-to-all | bytes 2359296 | tf_op jit(solution)/shard_map/all_to_all | solution.py:41
  198.8 0.5 broadcast_multiply_fusion
  199.3 0.7 copy.9
  200.0 3.1 %multiply_reduce_fusion.1 = (f32[128]{0:T(128)S(1)}, f32[128]{0:T(128)S(1)}, f32[12,192,128]{2,1,0:T(8,128)}) fusion(f32[12,192,128]{2,1,0:T(8,128)} %param.9, bf16[12,192,128]{2,1,0:T(8,128)(2,1)} %param.7, f32[12,192,128]{2,1,0:T(8,128)} %param.8, f32[4,3,192,128]{3,2,1,0:T(8,128)S(1)} %copy.9), kind=kLoop, calls=%fused_computation.9 | loop fusion | flops 1769216 | bytes 5309440 | tf_op jit(solution)/shard_map/reduce_sum | solution.py:43
  203.1 20.2 %all-reduce = (f32[1,128]{1,0:T(1,128)S(1)}, f32[1,128]{1,0:T(1,128)S(1)}) all-reduce(f32[1,128]{1,0:T(1,128)S(1)} %bitcast.20, f32[1,128]{1,0:T(1,128)S(1)} %bitcast.19), channel_id=1, replica_groups=mesh['slab'=8,'grp'=4] {'slab'}, use_global_device_ids=true, to_apply=%region_3.4 | all-reduce | flops 256 | bytes 2048 | tf_op jit(solution)/shard_map/psum | solution.py:45
  223.3 0.6 maximum_multiply_fusion
  (3 shorter events, 0.0 us)
Async XLA Ops:
  7.2 29.5 %all-gather.2.cloned.1.call-start = ((), (), s32[]{:S(2)}) async-start(), calls=%async_computation.1 | async-start | bytes 2949120 | tf_op jit(solution)/shard_map/all_gather | solution.py:38
  36.6 103.3 %collective-permute-start = (bf16[12,192,512]{2,1,0:T(8,128)(2,1)}, bf16[12,192,512]{2,1,0:T(8,128)(2,1)}, u32[]{:S(2)}, u32[]{:S(2)}) collective-permute-start(bf16[12,192,512]{2,1,0:T(8,128)(2,1)} %all-gather.2.cloned.1.call-done), channel_id=1, source_target_pairs={{0,4},{4,8},{8,12},{12,16},{16,20},{20,24},{24,28},{28,0},{1,5},{5... | collective-permute-start | bytes 7077896 | tf_op jit(solution)/shard_map/ppermute | solution.py:16
  38.1 104.0 %collective-permute-start.1 = (bf16[12,192,512]{2,1,0:T(8,128)(2,1)}, bf16[12,192,512]{2,1,0:T(8,128)(2,1)}, u32[]{:S(2)}, u32[]{:S(2)}) collective-permute-start(bf16[12,192,512]{2,1,0:T(8,128)(2,1)} %all-gather.2.cloned.1.call-done), channel_id=1, source_target_pairs={{4,0},{8,4},{12,8},{16,12},{20,16},{24,20},{28,24},{0,28},{5,1},{9... | collective-permute-start | bytes 7077896 | tf_op jit(solution)/shard_map/ppermute | solution.py:17
  42.9 99.2 %copy-start = (bf16[12,192,512]{2,1,0:T(8,128)(2,1)S(1)}, bf16[12,192,512]{2,1,0:T(8,128)(2,1)}, u32[]{:S(2)}) copy-start(bf16[12,192,512]{2,1,0:T(8,128)(2,1)} %all-gather.2.cloned.1.call-done) | copy-start | bytes 7077892
Sparse Core Ops, SparseCore 0:
  9.5 27.0 all-gather.1
where the time goes:
time: 231 us
  waiting for transfers between devices  116 us (50%)
  blocking collectives  48.3 us (21%)
  local copies, waits for them, and re-layouts  25.3 us (11%)
  between operations  14.1 us (6%)
  other arithmetic  11.4 us (5%)
  matrix products  10.4 us (5%)
  starting transfers between devices  4.76 us (2%)
    ppermute x1, waiting for transfers between devices, with_halo(): before = lax.ppermute(last, axis, up)  84.8 us
    all_gather x1, waiting for transfers between devices, shards(): whole = lax.all_gather(t_cur, 'grp', axis=2, tiled=True)  28.7 us
    all_to_all x1, blocking collectives, shards(): lax.all_to_all(rows_image, 'grp', split_axis=2, concat_axis=0, tiled=True)  28.2 us
    psum x1, blocking collectives, shards(): first, second = lax.psum((first, second), 'slab')  20.2 us
    reshape x1, local copies, waits for them, and re-layouts, apply_rows(): squares = tile_rows.reshape(tile_rows.shape[:2] + (width, width))  12.2 us
    gather x1, local copies, waits for them, and re-layouts, apply_rows(): near = jnp.take(padded, locals_rows.reshape(-1), axis=0)  11.3 us
    dot_general x1, matrix products, apply_rows(): jnp.einsum('bkrc,bkcp->brp', squares, near, preferred_element_type=jnp.fl...  10.4 us
    concatenate x1, other arithmetic, with_halo(): value = jnp.concatenate([before, value, after], axis=dim)  5.85 us
  transfers between devices with their start and end apart: 3, of which 3 were waited for; matrix products, arithmetic and copies ran while one was open for 6% of the time, Pallas kernels for 0%

commit v1 on v0

v1 whole, which is shorter than its diff:
```python
import functools
import math

import jax
import jax.numpy as jnp
from jax import lax
from jax.experimental import pallas as pl
from jax.experimental.pallas import tpu as pltpu
from jax.sharding import PartitionSpec as P

VMEM_LIMIT = 48 * 1024 * 1024


def image_kernel(ids, core, own_tiles, sib_tiles, *rest):
    nears, (own_img, oth_img, near) = rest[:6], rest[6:]
    step = pl.program_id(0)
    blocks, rows, cols = nears[0].shape
    pad = near.shape[1] - rows - 64
    neigh, half, wide = own_tiles.shape[1:]

    @pl.when(step == 0)
    def _():
        near[:, :64, :] = jnp.zeros((near.shape[0], 64, near.shape[2]), near.dtype)
        near[:, 64 + rows :, :] = jnp.zeros((near.shape[0], pad, near.shape[2]), near.dtype)
        for n, ref in enumerate(nears):
            at = (n % 3) * blocks
            side = (n // 3) * cols
            near[at : at + blocks, 64 : 64 + rows, side : side + cols] = ref[...]

    lane = lax.broadcasted_iota(jnp.int32, (half, 128), 1)

    def work(tiles):
        even = jnp.zeros((half, 2 * cols), jnp.float32)
        odd = jnp.zeros((half, 2 * cols), jnp.float32)
        for k in range(neigh):
            vec = near.at[ids[step * neigh + k]]
            tile = tiles[0, k]
            mid = tile[:, 128:256]
            none = jnp.zeros_like(mid)
            left = jnp.concatenate([tile[:, :128], jnp.where(lane < 64, mid, none)], axis=1)
            right = jnp.concatenate([jnp.where(lane < 64, none, mid), tile[:, 256:]], axis=1)
            even = even + jnp.dot(left, vec[64:, :], preferred_element_type=jnp.float32)
            odd = odd + jnp.dot(right, vec[: rows + 64, :], preferred_element_type=jnp.float32)
        for ref, side in ((own_img, 0), (oth_img, cols)):
            ref[0, pl.ds(0, half, 2), :] = even[:, side : side + cols]
            ref[0, pl.ds(1, half, 2), :] = odd[:, side : side + cols]

    @pl.when(step < own_tiles_steps(core))
    def _():
        work(own_tiles)

    @pl.when(step >= own_tiles_steps(core))
    def _():
        work(sib_tiles)


def own_tiles_steps(core):
    return core[1]


def images(ids, core, own_tiles, sib_tiles, nears):
    per, neigh, half, wide = own_tiles.shape
    blocks, rows, cols = nears[0].shape
    place = lambda b, ids, core: (jnp.where(b < per, core[0], 1 - core[0]) * per + b % per, 0, 0)
    tile = (1, neigh, half, wide)
    whole = pl.BlockSpec((blocks, rows, cols), lambda b, ids, core: (0, 0, 0))
    out = jax.ShapeDtypeStruct((2 * per, rows, cols), jnp.float32)
    return pl.pallas_call(
        image_kernel,
        grid_spec=pltpu.PrefetchScalarGridSpec(
            num_scalar_prefetch=2,
            grid=(2 * per,),
            in_specs=[
                pl.BlockSpec(tile, lambda b, ids, core: (jnp.minimum(b, per - 1), 0, 0, 0)),
                pl.BlockSpec(tile, lambda b, ids, core: (jnp.maximum(b - per, 0), 0, 0, 0)),
            ]
            + [whole] * 6,
            out_specs=[pl.BlockSpec((1, rows, cols), place)] * 2,
            scratch_shapes=[pltpu.VMEM((3 * blocks, rows + 128, 2 * cols), jnp.bfloat16)],
        ),
        out_shape=[out, out],
        compiler_params=pltpu.CompilerParams(vmem_limit_bytes=VMEM_LIMIT),
        name="images",
    )(ids, core, own_tiles, sib_tiles, *nears)


def next_kernel(side, own_img, oth_img, prev, probes, cur, out, sums):
    step = pl.program_id(0)

    def work(img):
        value = 2.0 * img[...] - prev[...]
        out[...] = value
        first = probes[...] * value
        second = cur[...].astype(jnp.float32) * value
        for n, term in enumerate((first, second)):
            part = jnp.sum(term.reshape(-1, 8, term.shape[-1]), axis=0)
            at = pl.ds(8 * n, 8)
            sums[at, :] = jnp.where(step == 0, part, sums[at, :] + part)

    @pl.when(step < pl.num_programs(0) // 2)
    def _():
        work(own_img)

    @pl.when(step >= pl.num_programs(0) // 2)
    def _():
        work(oth_img)


def next_vectors(side, own_img, oth_img, prev, probes, cur):
    half, rows, cols = own_img.shape
    parts = 2
    size = half // parts
    block = (size, rows, cols)
    spot = lambda i, side: (jnp.where(i < parts, side[0], 1 - side[0]) * parts + i % parts, 0, 0)
    return pl.pallas_call(
        next_kernel,
        grid_spec=pltpu.PrefetchScalarGridSpec(
            num_scalar_prefetch=1,
            grid=(2 * parts,),
            in_specs=[
                pl.BlockSpec(block, lambda i, side: (jnp.minimum(i, parts - 1), 0, 0)),
                pl.BlockSpec(block, lambda i, side: (jnp.maximum(i - parts, 0), 0, 0)),
            ]
            + [pl.BlockSpec(block, spot)] * 3,
            out_specs=[pl.BlockSpec(block, spot), pl.BlockSpec((16, cols), lambda i, side: (0, 0))],
        ),
        out_shape=[
            jax.ShapeDtypeStruct(prev.shape, jnp.float32),
            jax.ShapeDtypeStruct((16, cols), jnp.float32),
        ],
        compiler_params=pltpu.CompilerParams(vmem_limit_bytes=VMEM_LIMIT),
        name="next_vectors",
    )(side, own_img, oth_img, prev, probes, cur)


def sum_over(value, axis):
    size = lax.axis_size(axis)
    if size & (size - 1):
        return lax.psum(value, axis)
    hop = 1
    while hop < size:
        value = value + lax.ppermute(value, axis, [(i, i ^ hop) for i in range(size)])
        hop *= 2
    return value


def shards(tiles, neighbours, t_cur, t_prev, probes):
    blocks, rows, cols = t_cur.shape
    per, neigh = tiles.shape[:2]
    slabs, lanes = lax.axis_size("slab"), lax.axis_size("grp")
    slab, lane = lax.axis_index("slab"), lax.axis_index("grp")
    side, core = lane // 2, lane % 2
    across = functools.partial(lax.ppermute, axis_name="grp", perm=[(i, i ^ 2) for i in range(lanes)])
    sibling = functools.partial(lax.ppermute, axis_name="grp", perm=[(i, i ^ 1) for i in range(lanes)])
    pair = functools.partial(lax.ppermute, axis_name="slab", perm=[(i, i ^ 1) for i in range(slabs)])
    along = functools.partial(
        lax.ppermute,
        axis_name="slab",
        perm=[(i, (i + 2 if i % 2 == 0 else i - 2) % slabs) for i in range(slabs)],
    )

    oth = across(t_cur)
    near_own = pair(t_cur)
    squares = tiles.reshape(per, neigh, rows // 2, 2 * rows)
    sib_squares = sibling(squares)
    near_oth = pair(oth)
    far_own = along(near_own)
    far_oth = along(near_oth)

    owner = neighbours // blocks
    kind = jnp.where(owner == slab, 0, jnp.where(owner == slab ^ 1, 1, 2))
    local = (kind * blocks + neighbours % blocks).astype(jnp.int32)
    mine = lax.dynamic_slice_in_dim(local, lane * per, per, 0)
    theirs = lax.dynamic_slice_in_dim(local, (lane ^ 1) * per, per, 0)
    ids = jnp.concatenate([mine, theirs]).reshape(-1)

    own_img, oth_img = images(
        ids,
        jnp.stack([core, jnp.int32(per)]).astype(jnp.int32),
        squares,
        sib_squares,
        (t_cur, near_own, far_own, oth, near_oth, far_oth),
    )
    back = across(oth_img)
    t_next, sums = next_vectors(side.astype(jnp.int32)[None], own_img, back, t_prev, probes, t_cur)
    sums = jnp.sum(sums.reshape(2, 8, cols), axis=1)
    factor = 1.0 / math.sqrt(slabs * blocks * rows)
    moments = sum_over(sums, "slab") * factor
    return (t_next, moments)


def solution(mesh):
    placed = (
        P(("slab", "grp"), None, None),
        P("slab", None),
        P("slab", None, "grp"),
        P("slab", None, "grp"),
        P("slab", None, "grp"),
    )
    return jax.shard_map(
        shards,
        mesh=mesh,
        in_specs=placed,
        out_specs=(P("slab", None, "grp"), P(None, "grp")),
        check_vma=False,
    )
```

time: 231 us -> 101 us (0.44)
  waiting for transfers between devices: 116 us -> 61.5 us
  blocking collectives: 48.3 us -> 0 us
  Pallas kernels: 0 us -> 14.9 us
  local copies, waits for them, and re-layouts: 25.3 us -> 10.4 us
  between operations: 14.1 us -> 0.68 us
  other arithmetic: 11.4 us -> 0.69 us
  matrix products: 10.4 us -> 0 us
  starting transfers between devices: 4.76 us -> 12.5 us
    all_gather x1 -> x0, waiting for transfers between devices: 28.7 us -> none  [shards(): whole = lax.all_gather(t_cur, 'grp', axis=2, tiled=True)]
    all_to_all x1 -> x0, blocking collectives: 28.2 us -> none  [shards(): lax.all_to_all(rows_image, 'grp', split_axis=2, concat_axis=0, tiled=True)]
    ppermute x2 -> x10, waiting for transfers between devices: 87 us -> 61.5 us  [the longest x1 13.2 us: shards(): far_oth = along(near_oth)]
    psum x1 -> x0, blocking collectives: 20.2 us -> none  [shards(): first, second = lax.psum((first, second), 'slab')]
    pallas_call x0 -> x2, Pallas kernels: none -> 14.9 us  [the longest x1 13.2 us: images(): pl.pallas_call(image_kernel, grid_spec=pltpu.PrefetchScalarGridSpec(num_s...]
    gather x1 -> x0, local copies, waits for them, and re-layouts: 11.3 us -> none  [apply_rows(): near = jnp.take(padded, locals_rows.reshape(-1), axis=0)]
    dot_general x1 -> x0, matrix products: 10.4 us -> none  [apply_rows(): jnp.einsum('bkrc,bkcp->brp', squares, near, preferred_element_type=jnp.fl...]
    ppermute x2 -> x10, starting transfers between devices: 4.72 us -> 12.5 us  [the longest x1 2.49 us: shards(): oth = across(t_cur)]
  transfers between devices with their start and end apart: 3 -> 10, of which waited for: 3 -> 8; matrix products, arithmetic and copies ran while one was open for 6% -> 0% of each run, Pallas kernels for 0% -> 0%
where the time goes in v1:
time: 101 us
  waiting for transfers between devices  61.5 us (61%)
  Pallas kernels  14.9 us (15%)
  starting transfers between devices  12.5 us (12%)
  local copies, waits for them, and re-layouts  10.4 us (10%)
    pallas_call x1, Pallas kernels, images(): pl.pallas_call(image_kernel, grid_spec=pltpu.PrefetchScalarGridSpec(num_s...  13.2 us
    ppermute x1, waiting for transfers between devices, shards(): far_oth = along(near_oth)  13.2 us
    ppermute x1, waiting for transfers between devices, shards(): oth = across(t_cur)  12.5 us
    ppermute x1, waiting for transfers between devices, shards(): back = across(oth_img)  12.3 us
    ppermute x1, waiting for transfers between devices, shards(): near_oth = pair(oth)  12 us
    ppermute x3, waiting for transfers between devices, sum_over(): lax.ppermute(value, axis, [(i, i ^ hop) for i in range(size)])  9.95 us
    reshape x1, local copies, waits for them, and re-layouts, shards(): squares = tiles.reshape(per, neigh, rows // 2, 2 * rows)  8.38 us
    ppermute x1, starting transfers between devices, shards(): oth = across(t_cur)  2.49 us
  transfers between devices with their start and end apart: 10, of which 8 were waited for; matrix products, arithmetic and copies ran while one was open for 0% of the time, Pallas kernels for 0%

profile of v1, /device:TPU:0, one launch (start us, length us, event | category | flops | bytes accessed | tf_op | source)
XLA Modules:
  0.0 100.7 jit_solution(1180847104449826313)
XLA Ops:
  0.6 0.0 copy-start
  0.6 0.0 copy-start.5
  0.6 8.4 %reshape.14.own_tiles = bf16[3,27,96,384]{3,2,1,0:T(8,128)(2,1)} reshape(bf16[3,27,36864]{2,1,0:T(8,128)(2,1)} %param.5) | data formatting | bytes 11943936 | tf_op jit(solution)/shard_map/reshape | solution.py:164
  9.0 0.5 collective-permute-start
  9.5 0.0 copy-done
  9.5 2.5 %collective-permute-start.3 = (bf16[12,192,128]{2,1,0:T(8,128)(2,1)S(1)}, bf16[12,192,128]{2,1,0:T(8,128)(2,1)S(1)}, u32[]{:S(2)}, u32[]{:S(2)}) collective-permute-start(bf16[12,192,128]{2,1,0:T(8,128)(2,1)S(1)} %copy-done), channel_id=1, source_target_pairs={{0,2},{1,3},{2,0},{3,1},{4,6},{5,7},{6,4},{7,5},{8,10},{9,11},{10,... | collective-permute-start | bytes 1769480 | tf_op jit(solution)/shard_map/ppermute | solution.py:162
  12.0 1.5 %collective-permute-start.1 = (bf16[12,192,128]{2,1,0:T(8,128)(2,1)S(1)}, bf16[12,192,128]{2,1,0:T(8,128)(2,1)}, u32[]{:S(2)}, u32[]{:S(2)}) collective-permute-start(bf16[12,192,128]{2,1,0:T(8,128)(2,1)S(1)} %copy-done), channel_id=1, source_target_pairs={{0,4},{4,0},{8,12},{12,8},{16,20},{20,16},{24,28},{28,24},{1,5},{5... | collective-permute-start | bytes 1769480 | tf_op jit(solution)/shard_map/ppermute | solution.py:163
  13.5 12.5 %collective-permute-done.3.rest_3_ = bf16[12,192,128]{2,1,0:T(8,128)(2,1)S(1)} collective-permute-done((bf16[12,192,128]{2,1,0:T(8,128)(2,1)S(1)}, bf16[12,192,128]{2,1,0:T(8,128)(2,1)S(1)}, u32[]{:S(2)}, u32[]{:S(2)}) %collective-permute-start.3) | collective-permute-done | bytes 589856 | tf_op jit(solution)/shard_map/ppermute | solution.py:162
  26.0 1.8 %collective-permute-start.4 = (bf16[12,192,128]{2,1,0:T(8,128)(2,1)S(1)}, bf16[12,192,128]{2,1,0:T(8,128)(2,1)}, u32[]{:S(2)}, u32[]{:S(2)}) collective-permute-start(bf16[12,192,128]{2,1,0:T(8,128)(2,1)S(1)} %collective-permute-done.3.rest_3_), channel_id=1, source_target_pairs={{0,4},{4,0},{8,12},{12,8},{16,20},{20,16},{24,28},{28,24},{1,5},{5... | collective-permute-start | bytes 1769480 | tf_op jit(solution)/shard_map/ppermute | solution.py:166
  27.7 0.0 collective-permute-done.1.rest_1_
  27.7 1.6 %collective-permute-start.2 = (bf16[12,192,128]{2,1,0:T(8,128)(2,1)}, bf16[12,192,128]{2,1,0:T(8,128)(2,1)}, u32[]{:S(2)}, u32[]{:S(2)}) collective-permute-start(bf16[12,192,128]{2,1,0:T(8,128)(2,1)} %collective-permute-done.1.rest_1_), channel_id=1, source_target_pairs={{0,8},{4,28},{8,16},{12,4},{16,24},{20,12},{24,0},{28,20},{1,9},{5... | collective-permute-start | bytes 1769480 | tf_op jit(solution)/shard_map/ppermute | solution.py:167
  29.3 12.0 %collective-permute-done.4.rest_4_ = bf16[12,192,128]{2,1,0:T(8,128)(2,1)} collective-permute-done((bf16[12,192,128]{2,1,0:T(8,128)(2,1)S(1)}, bf16[12,192,128]{2,1,0:T(8,128)(2,1)}, u32[]{:S(2)}, u32[]{:S(2)}) %collective-permute-start.4) | collective-permute-done | bytes 589856 | tf_op jit(solution)/shard_map/ppermute | solution.py:166
  41.3 1.6 %collective-permute-start.5 = (bf16[12,192,128]{2,1,0:T(8,128)(2,1)}, bf16[12,192,128]{2,1,0:T(8,128)(2,1)}, u32[]{:S(2)}, u32[]{:S(2)}) collective-permute-start(bf16[12,192,128]{2,1,0:T(8,128)(2,1)} %collective-permute-done.4.rest_4_), channel_id=1, source_target_pairs={{0,8},{4,28},{8,16},{12,4},{16,24},{20,12},{24,0},{28,20},{1,9},{5... | collective-permute-start | bytes 1769480 | tf_op jit(solution)/shard_map/ppermute | solution.py:168
  43.0 0.0 copy-done.5
  43.0 0.1 reshape.13.ids
  43.1 0.1 pad_add_fusion.1.core
  43.2 0.0 copy-start.1
  43.2 0.0 copy-start.2
  43.2 1.5 %collective-permute-done.2.rest_2_ = bf16[12,192,128]{2,1,0:T(8,128)(2,1)} collective-permute-done((bf16[12,192,128]{2,1,0:T(8,128)(2,1)}, bf16[12,192,128]{2,1,0:T(8,128)(2,1)}, u32[]{:S(2)}, u32[]{:S(2)}) %collective-permute-start.2) | collective-permute-done | bytes 589856 | tf_op jit(solution)/shard_map/ppermute | solution.py:167
  44.7 13.2 %collective-permute-done.5.rest_5_ = bf16[12,192,128]{2,1,0:T(8,128)(2,1)} collective-permute-done((bf16[12,192,128]{2,1,0:T(8,128)(2,1)}, bf16[12,192,128]{2,1,0:T(8,128)(2,1)}, u32[]{:S(2)}, u32[]{:S(2)}) %collective-permute-start.5) | collective-permute-done | bytes 589856 | tf_op jit(solution)/shard_map/ppermute | solution.py:168
  57.9 0.0 collective-permute-done.sib_tiles
  57.9 13.2 %images.1 = (f32[6,192,128]{2,1,0:T(8,128)S(1)}, f32[6,192,128]{2,1,0:T(8,128)}) custom-call(s32[162]{0:T(256)S(1)} %reshape.13.ids, s32[2]{0:T(128)S(1)} %pad_add_fusion.1.core, bf16[3,27,96,384]{3,2,1,0:T(8,128)(2,1)} %reshape.14.own_tiles, bf16[3,27,96,384]{3,2,1,0:T(8,128)(2,1)} %collective-permute-done.sib_tiles, bf16[12,192,128]{2,1,0:T(8,128)(2,1)S(1)} %copy-done, ...), custom_call_target="tpu_custom_call" | custom-call | tf_op jit(solution)/shard_map/images/pallas_call | solution.py:68
  71.1 0.0 copy-start.3
  71.1 0.8 copy-done.3
  71.9 1.4 %collective-permute-start.6 = (f32[6,192,128]{2,1,0:T(8,128)}, f32[6,192,128]{2,1,0:T(8,128)S(1)}, u32[]{:S(2)}, u32[]{:S(2)}) collective-permute-start(f32[6,192,128]{2,1,0:T(8,128)} %get-tuple-element.7), channel_id=1, source_target_pairs={{0,2},{1,3},{2,0},{3,1},{4,6},{5,7},{6,4},{7,5},{8,10},{9,11},{10,... | collective-permute-start | bytes 1769480 | tf_op jit(solution)/shard_map/ppermute | solution.py:184
  73.2 12.3 %collective-permute-done.6.oth_img = f32[6,192,128]{2,1,0:T(8,128)S(1)} collective-permute-done((f32[6,192,128]{2,1,0:T(8,128)}, f32[6,192,128]{2,1,0:T(8,128)S(1)}, u32[]{:S(2)}, u32[]{:S(2)}) %collective-permute-start.6) | collective-permute-done | bytes 589856 | tf_op jit(solution)/shard_map/ppermute | solution.py:184
  85.6 0.0 copy-done.1
  85.6 0.0 copy-done.2
  85.6 0.0 copy-start.4
  85.6 1.1 %copy-done.4 = f32[6,192,128]{2,1,0:T(8,128)S(1)} copy-done((f32[6,192,128]{2,1,0:T(8,128)S(1)}, f32[6,192,128]{2,1,0:T(8,128)}, u32[]{:S(2)}) %copy-start.4) | copy-done | bytes 589848
  86.7 1.7 %next_vectors.1 = (f32[12,192,128]{2,1,0:T(8,128)}, f32[16,128]{1,0:T(8,128)S(1)}) custom-call(s32[1]{0:T(128)} %bitcast.side, f32[6,192,128]{2,1,0:T(8,128)S(1)} %copy-done.4, f32[6,192,128]{2,1,0:T(8,128)S(1)} %collective-permute-done.6.oth_img, f32[12,192,128]{2,1,0:T(8,128)S(1)} %copy-done.1, f32[12,192,128]{2,1,0:T(8,128)S(1)} %copy-done.2, ...), custom_call_target="tpu_custom_call" | custom-call | tf_op jit(solution)/shard_map/next_vectors/pallas_call | solution.py:115
  88.4 0.5 collective-permute-start.7
  88.9 3.1 %collective-permute-done.7 = f32[2,128]{1,0:T(2,128)S(1)} collective-permute-done((f32[2,128]{1,0:T(2,128)S(1)}, f32[2,128]{1,0:T(2,128)S(1)}, u32[]{:S(2)}, u32[]{:S(2)}) %collective-permute-start.7) | collective-permute-done | bytes 1056 | tf_op jit(solution)/shard_map/ppermute | solution.py:142
  92.0 0.0 collective-permute-start.8
  92.0 3.6 %collective-permute-done.8 = f32[2,128]{1,0:T(2,128)S(1)} collective-permute-done((f32[2,128]{1,0:T(2,128)S(1)}, f32[2,128]{1,0:T(2,128)S(1)}, u32[]{:S(2)}, u32[]{:S(2)}) %collective-permute-start.8) | collective-permute-done | bytes 1056 | tf_op jit(solution)/shard_map/ppermute | solution.py:142
  95.6 1.2 %collective-permute-start.9 = (f32[2,128]{1,0:T(2,128)S(1)}, f32[2,128]{1,0:T(2,128)S(1)}, u32[]{:S(2)}, u32[]{:S(2)}) collective-permute-start(f32[2,128]{1,0:T(2,128)S(1)} %add.36), channel_id=1, source_target_pairs={{0,16},{4,20},{8,24},{12,28},{16,0},{20,4},{24,8},{28,12},{1,17},{... | collective-permute-start | bytes 3080 | tf_op jit(solution)/shard_map/ppermute | solution.py:142
  96.8 3.2 %collective-permute-done.9 = f32[2,128]{1,0:T(2,128)S(1)} collective-permute-done((f32[2,128]{1,0:T(2,128)S(1)}, f32[2,128]{1,0:T(2,128)S(1)}, u32[]{:S(2)}, u32[]{:S(2)}) %collective-permute-start.9) | collective-permute-done | bytes 1056 | tf_op jit(solution)/shard_map/ppermute | solution.py:142
  100.1 0.6 add_multiply_fusion
  (6 shorter events, 0.1 us)
Async XLA Ops:
  0.6 8.9 %copy-start = (bf16[12,192,128]{2,1,0:T(8,128)(2,1)S(1)}, bf16[12,192,128]{2,1,0:T(8,128)(2,1)}, u32[]{:S(2)}) copy-start(bf16[12,192,128]{2,1,0:T(8,128)(2,1)} %cur.1) | copy-start | bytes 1769476
  0.6 42.3 %copy-start.5 = (s32[12,27]{1,0:T(8,128)S(1)}, s32[12,27]{1,0:T(8,128)}, u32[]{:S(2)}) copy-start(s32[12,27]{1,0:T(8,128)} %param.6) | copy-start | bytes 3892
  9.0 48.9 %collective-permute-start = (bf16[3,27,96,384]{3,2,1,0:T(8,128)(2,1)}, bf16[3,27,96,384]{3,2,1,0:T(8,128)(2,1)}, u32[]{:S(2)}, u32[]{:S(2)}) collective-permute-start(bf16[3,27,96,384]{3,2,1,0:T(8,128)(2,1)} %reshape.14.own_tiles), channel_id=1, source_target_pairs={{0,1},{1,0},{2,3},{3,2},{4,5},{5,4},{6,7},{7,6},{8,9},{9,8},{10,11... | collective-permute-start | bytes 17915912 | tf_op jit(solution)/shard_map/ppermute | solution.py:165
  9.5 16.5 %collective-permute-start.3 = (bf16[12,192,128]{2,1,0:T(8,128)(2,1)S(1)}, bf16[12,192,128]{2,1,0:T(8,128)(2,1)S(1)}, u32[]{:S(2)}, u32[]{:S(2)}) collective-permute-start(bf16[12,192,128]{2,1,0:T(8,128)(2,1)S(1)} %copy-done), channel_id=1, source_target_pairs={{0,2},{1,3},{2,0},{3,1},{4,6},{5,7},{6,4},{7,5},{8,10},{9,11},{10,... | collective-permute-start | bytes 1769480 | tf_op jit(solution)/shard_map/ppermute | solution.py:162
  12.0 15.8 %collective-permute-start.1 = (bf16[12,192,128]{2,1,0:T(8,128)(2,1)S(1)}, bf16[12,192,128]{2,1,0:T(8,128)(2,1)}, u32[]{:S(2)}, u32[]{:S(2)}) collective-permute-start(bf16[12,192,128]{2,1,0:T(8,128)(2,1)S(1)} %copy-done), channel_id=1, source_target_pairs={{0,4},{4,0},{8,12},{12,8},{16,20},{20,16},{24,28},{28,24},{1,5},{5... | collective-permute-start | bytes 1769480 | tf_op jit(solution)/shard_map/ppermute | solution.py:163
  26.0 15.4 %collective-permute-start.4 = (bf16[12,192,128]{2,1,0:T(8,128)(2,1)S(1)}, bf16[12,192,128]{2,1,0:T(8,128)(2,1)}, u32[]{:S(2)}, u32[]{:S(2)}) collective-permute-start(bf16[12,192,128]{2,1,0:T(8,128)(2,1)S(1)} %collective-permute-done.3.rest_3_), channel_id=1, source_target_pairs={{0,4},{4,0},{8,12},{12,8},{16,20},{20,16},{24,28},{28,24},{1,5},{5... | collective-permute-start | bytes 1769480 | tf_op jit(solution)/shard_map/ppermute | solution.py:166
  27.7 17.0 %collective-permute-start.2 = (bf16[12,192,128]{2,1,0:T(8,128)(2,1)}, bf16[12,192,128]{2,1,0:T(8,128)(2,1)}, u32[]{:S(2)}, u32[]{:S(2)}) collective-permute-start(bf16[12,192,128]{2,1,0:T(8,128)(2,1)} %collective-permute-done.1.rest_1_), channel_id=1, source_target_pairs={{0,8},{4,28},{8,16},{12,4},{16,24},{20,12},{24,0},{28,20},{1,9},{5... | collective-permute-start | bytes 1769480 | tf_op jit(solution)/shard_map/ppermute | solution.py:167
  41.3 16.5 %collective-permute-start.5 = (bf16[12,192,128]{2,1,0:T(8,128)(2,1)}, bf16[12,192,128]{2,1,0:T(8,128)(2,1)}, u32[]{:S(2)}, u32[]{:S(2)}) collective-permute-start(bf16[12,192,128]{2,1,0:T(8,128)(2,1)} %collective-permute-done.4.rest_4_), channel_id=1, source_target_pairs={{0,8},{4,28},{8,16},{12,4},{16,24},{20,12},{24,0},{28,20},{1,9},{5... | collective-permute-start | bytes 1769480 | tf_op jit(solution)/shard_map/ppermute | solution.py:168
  43.2 42.4 %copy-start.1 = (f32[12,192,128]{2,1,0:T(8,128)S(1)}, f32[12,192,128]{2,1,0:T(8,128)}, u32[]{:S(2)}) copy-start(f32[12,192,128]{2,1,0:T(8,128)} %prev.1) | copy-start | bytes 3538948
  43.2 42.4 %copy-start.2 = (f32[12,192,128]{2,1,0:T(8,128)S(1)}, f32[12,192,128]{2,1,0:T(8,128)}, u32[]{:S(2)}) copy-start(f32[12,192,128]{2,1,0:T(8,128)} %probes.1) | copy-start | bytes 3538948
  71.1 0.8 copy-start.3
  71.9 13.7 %collective-permute-start.6 = (f32[6,192,128]{2,1,0:T(8,128)}, f32[6,192,128]{2,1,0:T(8,128)S(1)}, u32[]{:S(2)}, u32[]{:S(2)}) collective-permute-start(f32[6,192,128]{2,1,0:T(8,128)} %get-tuple-element.7), channel_id=1, source_target_pairs={{0,2},{1,3},{2,0},{3,1},{4,6},{5,7},{6,4},{7,5},{8,10},{9,11},{10,... | collective-permute-start | bytes 1769480 | tf_op jit(solution)/shard_map/ppermute | solution.py:184
  85.6 1.1 %copy-start.4 = (f32[6,192,128]{2,1,0:T(8,128)S(1)}, f32[6,192,128]{2,1,0:T(8,128)}, u32[]{:S(2)}) copy-start(f32[6,192,128]{2,1,0:T(8,128)} %copy-done.3) | copy-start | bytes 1769476
  88.4 3.6 %collective-permute-start.7 = (f32[2,128]{1,0:T(2,128)S(1)}, f32[2,128]{1,0:T(2,128)S(1)}, u32[]{:S(2)}, u32[]{:S(2)}) collective-permute-start(f32[2,128]{1,0:T(2,128)S(1)} %bitcast_reduce_fusion), channel_id=1, source_target_pairs={{0,4},{4,0},{8,12},{12,8},{16,20},{20,16},{24,28},{28,24},{1,5},{5... | collective-permute-start | bytes 3080 | tf_op jit(solution)/shard_map/ppermute | solution.py:142
  92.0 3.6 %collective-permute-start.8 = (f32[2,128]{1,0:T(2,128)S(1)}, f32[2,128]{1,0:T(2,128)S(1)}, u32[]{:S(2)}, u32[]{:S(2)}) collective-permute-start(f32[2,128]{1,0:T(2,128)S(1)} %add.35), channel_id=1, source_target_pairs={{0,8},{4,12},{8,0},{12,4},{16,24},{20,28},{24,16},{28,20},{1,9},{5... | collective-permute-start | bytes 3080 | tf_op jit(solution)/shard_map/ppermute | solution.py:142
  95.6 4.5 %collective-permute-start.9 = (f32[2,128]{1,0:T(2,128)S(1)}, f32[2,128]{1,0:T(2,128)S(1)}, u32[]{:S(2)}, u32[]{:S(2)}) collective-permute-start(f32[2,128]{1,0:T(2,128)S(1)} %add.36), channel_id=1, source_target_pairs={{0,16},{4,20},{8,24},{12,28},{16,0},{20,4},{24,8},{28,12},{1,17},{... | collective-permute-start | bytes 3080 | tf_op jit(solution)/shard_map/ppermute | solution.py:142

commit v2 on v0

v2 whole, which is shorter than its diff:
```python
import functools
import math

import jax
import jax.numpy as jnp
from jax import lax
from jax.experimental import pallas as pl
from jax.experimental.pallas import tpu as pltpu
from jax.sharding import PartitionSpec as P

GRANT = 20 * 1024 * 1024
BLOCKS = 6
PAD = 64
LIGHT = pl.CostEstimate(flops=1, bytes_accessed=1, transcendentals=0)
HEAVY = pl.CostEstimate(flops=1, bytes_accessed=18_000_000, transcendentals=0)
VMEM = pl.BlockSpec(memory_space=pltpu.VMEM)
SMEM = pl.BlockSpec(memory_space=pltpu.SMEM)
HBM = pl.BlockSpec(memory_space=pltpu.HBM)
ANY = pl.BlockSpec(memory_space=pl.ANY)
DMA = pltpu.SemaphoreType.DMA


def in_vmem(arrays):
    return [pltpu.with_memory_space_constraint(a, pltpu.VMEM) for a in arrays]


def in_smem(table):
    return pltpu.with_memory_space_constraint(table, pltpu.SMEM)


def in_hbm(arrays):
    return [pltpu.with_memory_space_constraint(a, pltpu.HBM) for a in arrays]


def params():
    return pltpu.CompilerParams(vmem_limit_bytes=GRANT)


def copy(src, dst, sem):
    made = pltpu.make_async_copy(src, dst, sem)
    made.start()
    return made


def meets_kernel(neighbours, out, table, sem):
    blocks, neigh = neighbours.shape
    slab, lane = lax.axis_index("slab"), lax.axis_index("grp")
    per = BLOCKS // 2
    table[...] = jnp.zeros_like(table)
    for side, first in enumerate((lane * per, (lane ^ 1) * per)):
        for n in range(per):
            table[pl.ds(side * per + n, 1), :neigh] = neighbours[pl.ds(first + n, 1), :]
    mine = table[...]
    owner = mine // blocks
    kind = jnp.where(owner == slab, 0, jnp.where(owner == (slab ^ 1), 1, 2))
    table[...] = kind * blocks + mine - owner * blocks
    copy(table, out, sem).wait()


def meets(neighbours):
    return pl.pallas_call(
        meets_kernel,
        in_specs=[VMEM],
        out_specs=SMEM,
        out_shape=pltpu.SMEM((8, 128), jnp.int32),
        scratch_shapes=[pltpu.VMEM((8, 128), jnp.int32), DMA],
        compiler_params=params(),
        cost_estimate=LIGHT,
        name="meets",
    )(neighbours)


def square_part(src, held, low):
    neigh, wide = src.shape[0], held.shape[2]
    piece = [src[:, pl.ds(pl.multiple_of(j * wide, wide), wide)] for j in range(16)]
    held[:, pl.ds(low, 16), :] = jnp.transpose(jnp.stack(piece, axis=0), (1, 0, 2))


def square_kernel(parts, tiles, held, raw, sems):
    count, _, half, wide = held.shape
    each = parts // count
    size = half // each
    loads = []
    for n in range(parts):
        src = tiles.at[n // each, :, pl.ds((n % each) * size * wide, size * wide)]
        loads.append(copy(src, raw.at[n], sems.at[n]))
    for n in range(parts):
        loads[n].wait()

        @pl.loop(0, size // 16)
        def _(step):
            low = pl.multiple_of((n % each) * size + step * 16, 16)
            src = raw.at[n, :, pl.ds(pl.multiple_of(step * 16 * wide, 128), 16 * wide)]
            square_part(src, held.at[n // each], low)


def held_kernel(tiles, held):
    count, _, half, wide = held.shape

    @pl.loop(0, count * (half // 16))
    def _(step):
        b, part = step // (half // 16), step % (half // 16)
        src = tiles.at[b, :, pl.ds(pl.multiple_of(part * 16 * wide, 128), 16 * wide)]
        square_part(src, held.at[b], pl.multiple_of(part * 16, 16))


def squares(tiles, rows, resident):
    count, neigh = tiles.shape[:2]
    half, wide = rows // 2, 2 * rows
    parts = 3 * count
    raw = [pltpu.VMEM((parts, neigh, rows * rows // 3), tiles.dtype), DMA((parts,))]
    return pl.pallas_call(
        held_kernel if resident else functools.partial(square_kernel, parts),
        in_specs=[VMEM if resident else HBM],
        out_specs=VMEM,
        out_shape=pltpu.VMEM((count, neigh, half, wide), tiles.dtype),
        scratch_shapes=[] if resident else raw,
        compiler_params=params(),
        cost_estimate=HEAVY,
        name="squares",
    )(*(in_vmem([tiles]) if resident else in_hbm([tiles])))


def start_near(chunks, near, sems):
    copies, at = [], 0
    for n, chunk in enumerate(chunks):
        copies.append(copy(chunk, near.at[pl.ds(at, chunk.shape[0])], sems.at[n]))
        at += chunk.shape[0]
    return copies


def multiply(tiles, table, row, near):
    count, half, wide = tiles.shape
    rows = wide // 2
    lane = lax.broadcasted_iota(jnp.int32, (half, 128), 1)
    even = odd = None
    for k in range(count):
        vec = near[table[row, k]]
        tile = tiles[k]
        mid = tile[:, 128:256]
        none = jnp.zeros_like(mid)
        left = jnp.concatenate([tile[:, :128], jnp.where(lane < PAD, mid, none)], axis=1)
        right = jnp.concatenate([jnp.where(lane < PAD, none, mid), tile[:, 256:]], axis=1)
        one = jnp.concatenate([vec, vec[:PAD]], axis=0)
        two = jnp.concatenate([vec[rows - PAD :], vec], axis=0)
        one = jnp.dot(left, one, preferred_element_type=jnp.float32)
        two = jnp.dot(right, two, preferred_element_type=jnp.float32)
        even = one if even is None else even + one
        odd = two if odd is None else odd + two
    return even, odd


def each_block(held, body):
    first = 0
    for square in held:
        start = first

        @pl.loop(0, square.shape[0])
        def _(n):
            body(start + n, square.at[n])

        first += square.shape[0]


def place(b):
    per = BLOCKS // 2
    core = lax.axis_index("grp") % 2
    return jnp.where(b < per, core * per + b, (1 - core) * per + b - per)


def near_scratch(chunks):
    return pltpu.VMEM((sum(c.shape[0] for c in chunks),) + chunks[0].shape[1:], chunks[0].dtype)


def other_kernel(n_chunks, table, first, second, *refs):
    chunks = refs[:n_chunks]
    out, near, image, near_sems, out_sems = refs[-5:]
    half = first.shape[2]
    for load in start_near(chunks, near, near_sems):
        load.wait()

    def body(b, tiles):
        even, odd = multiply(tiles, table, b, near)
        image[b, pl.ds(0, half, 2), :] = even
        image[b, pl.ds(1, half, 2), :] = odd
        copy(image.at[b], out.at[place(b)], out_sems.at[b])

    each_block((first, second), body)
    for b in range(BLOCKS):
        pltpu.make_async_copy(image.at[b], out.at[place(b)], out_sems.at[b]).wait()


def other_images(table, held, chunks, after):
    rows, cols = chunks[0].shape[1:]
    return pl.pallas_call(
        functools.partial(other_kernel, len(chunks)),
        in_specs=[SMEM] + [VMEM] * 2 + [ANY] * (len(chunks) + len(after)),
        out_specs=HBM,
        out_shape=pltpu.HBM((BLOCKS, rows, cols), jnp.float32),
        scratch_shapes=[
            near_scratch(chunks),
            pltpu.VMEM((BLOCKS, rows, cols), jnp.float32),
            DMA((len(chunks),)),
            DMA((BLOCKS,)),
        ],
        compiler_params=params(),
        cost_estimate=HEAVY,
        name="other_images",
    )(in_smem(table), *in_vmem(held), *chunks, *after)


def add_sums(factor, value, probes, cur, sums):
    for n, term in enumerate((probes * value, cur.astype(jnp.float32) * value)):
        part = jnp.sum(term.reshape(-1, 8, term.shape[-1]), axis=0) * factor
        sums[pl.ds(8 * n, 8), :] += part


def own_kernel(n_chunks, factor, table, first_held, second_held, *refs):
    chunks, rows_in = refs[:n_chunks], refs[n_chunks : n_chunks + 3]
    out, sums, near, held, image, prev, probes, cur, near_sems, held_sems, row_sems, out_sems = refs[-12:]
    half = first_held.shape[2]
    loads = start_near(chunks, near, near_sems)
    slots = held.shape[0]

    def load(n, square):
        return pltpu.make_async_copy(square, held.at[n % slots], held_sems.at[n % slots])

    def load_next(n):
        count = first_held.shape[0]
        pl.when(n < count)(lambda: load(n, first_held.at[jnp.minimum(n, count - 1)]).start())
        more = (n >= count) & (n < BLOCKS)
        pl.when(more)(lambda: load(n, second_held.at[jnp.clip(n - count, 0, BLOCKS - count - 1)]).start())

    for n in range(slots - 1):
        load_next(n)
    first = (lax.axis_index("grp") // 2) * BLOCKS
    for n, (src, dst) in enumerate(zip(rows_in, (prev, probes, cur))):
        loads.append(copy(src.at[pl.ds(first, BLOCKS)], dst, row_sems.at[n]))
    sums[...] = jnp.zeros_like(sums)
    for made in loads:
        made.wait()

    @pl.loop(0, BLOCKS)
    def _(b):
        load_next(b + slots - 1)
        load(b, first_held.at[0]).wait()
        at = place(b)
        even, odd = multiply(held.at[b % slots], table, b, near)
        image[b, pl.ds(0, half, 2), :] = even
        image[b, pl.ds(1, half, 2), :] = odd
        value = 2.0 * image[b] - prev[at]
        image[b] = value
        copy(image.at[b], out.at[first + at], out_sems.at[b])
        add_sums(factor, value, probes[at], cur[at], sums)

    for b in range(BLOCKS):
        pltpu.make_async_copy(image.at[b], out.at[first + place(b)], out_sems.at[b]).wait()


def own_rows(table, held, chunks, factor, prev, probes, cur, after):
    rows, cols = cur.shape[1:]
    part = (BLOCKS, rows, cols)
    return pl.pallas_call(
        functools.partial(own_kernel, len(chunks), factor),
        in_specs=[SMEM] + [HBM] * 2 + [ANY] * (len(chunks) + 3 + len(after)),
        out_specs=[HBM, VMEM],
        out_shape=[
            jax.ShapeDtypeStruct(prev.shape, jnp.float32),
            jax.ShapeDtypeStruct((16, cols), jnp.float32),
        ],
        scratch_shapes=[
            near_scratch(chunks),
            pltpu.VMEM((3,) + held[0].shape[1:], held[0].dtype),
            pltpu.VMEM(part, jnp.float32),
            pltpu.VMEM(part, jnp.float32),
            pltpu.VMEM(part, jnp.float32),
            pltpu.VMEM(part, cur.dtype),
            DMA((len(chunks),)),
            DMA((3,)),
            DMA((3,)),
            DMA((BLOCKS,)),
        ],
        compiler_params=params(),
        cost_estimate=HEAVY,
        name="own_rows",
    )(in_smem(table), *in_hbm(held), *chunks, prev, probes, cur, *after)


def final_kernel(factor, side, image, prev, probes, cur, _, sums_in, out, sums, acc):
    step = pl.program_id(0)

    @pl.when(step == 0)
    def _():
        acc[...] = sums_in[...]

    value = 2.0 * image[...] - prev[...]
    out[...] = value
    add_sums(factor, value, probes[...], cur[...], acc)

    @pl.when(step == pl.num_programs(0) - 1)
    def _():
        for n in range(2):
            sums[pl.ds(n, 1), :] = jnp.sum(acc[pl.ds(8 * n, 8), :], axis=0, keepdims=True)


def other_rows(side, factor, image, prev, probes, cur, t_next, sums):
    half, rows, cols = image.shape
    steps = 3
    block = (half // steps, rows, cols)
    spot = pl.BlockSpec(block, lambda i, side: ((1 - side[0]) * steps + i, 0, 0))
    return pl.pallas_call(
        functools.partial(final_kernel, factor),
        grid_spec=pltpu.PrefetchScalarGridSpec(
            num_scalar_prefetch=1,
            grid=(steps,),
            in_specs=[pl.BlockSpec(block, lambda i, side: (i, 0, 0))]
            + [spot] * 3
            + [pl.BlockSpec(memory_space=pl.ANY), pl.BlockSpec((16, cols), lambda i, side: (0, 0))],
            out_specs=[spot, pl.BlockSpec((2, cols), lambda i, side: (0, 0))],
            scratch_shapes=[pltpu.VMEM((16, cols), jnp.float32)],
        ),
        out_shape=[
            jax.ShapeDtypeStruct(prev.shape, jnp.float32),
            jax.ShapeDtypeStruct((2, cols), jnp.float32),
        ],
        input_output_aliases={5: 0},
        compiler_params=params(),
        cost_estimate=LIGHT,
        name="other_rows",
    )(side, image, prev, probes, cur, t_next, sums)


def gate(value, *after):
    return pl.pallas_call(
        lambda *refs: None,
        in_specs=[ANY] * (1 + len(after)),
        out_specs=ANY,
        out_shape=jax.ShapeDtypeStruct(value.shape, value.dtype),
        input_output_aliases={0: 0},
        compiler_params=params(),
        cost_estimate=LIGHT,
        name="gate",
    )(value, *after)


def sum_over(value, axis):
    size = lax.axis_size(axis)
    if size & (size - 1):
        return lax.psum(value, axis)
    hop = 1
    while hop < size:
        value = value + lax.ppermute(value, axis, [(i, i ^ hop) for i in range(size)])
        hop *= 2
    return value


def shards(tiles, neighbours, t_cur, t_prev, probes):
    blocks, rows, cols = t_cur.shape
    per = tiles.shape[0]
    slabs, lanes = lax.axis_size("slab"), lax.axis_size("grp")
    side = (lax.axis_index("grp") // 2).astype(jnp.int32)[None]
    factor = 1.0 / math.sqrt(slabs * blocks * rows)
    across = functools.partial(lax.ppermute, axis_name="grp", perm=[(i, i ^ 2) for i in range(lanes)])
    sibling = functools.partial(lax.ppermute, axis_name="grp", perm=[(i, i ^ 1) for i in range(lanes)])
    pair = functools.partial(lax.ppermute, axis_name="slab", perm=[(i, i ^ 1) for i in range(slabs)])
    along = functools.partial(
        lax.ppermute,
        axis_name="slab",
        perm=[(i, (i + 2 if i % 2 == 0 else i - 2) % slabs) for i in range(slabs)],
    )

    tiles, t_prev, probes, fixed = in_hbm([tiles, t_prev, probes, t_cur])
    half = blocks // 2
    low, high = t_cur[:half], t_cur[half:]

    sib_tiles = sibling(tiles)
    oth = [across(low), across(high)]
    near_high = pair(high)
    table = meets(neighbours)
    held = [squares(tiles, rows, False)]
    near_oth = [pair(gate(oth[0], *held)), pair(oth[1])]
    far_high = along(near_high)
    far_oth = [along(near_oth[0]), across(far_high)]
    held.append(squares(sib_tiles, rows, True))
    near_low = pair(gate(low, held[1]))
    far_low = along(near_low)

    images = other_images(table, held, [*oth, *near_oth, *far_oth], ())
    back = across(images)
    own = [fixed, near_low, near_high, far_low, far_high]
    t_next, sums = own_rows(table, held, own, factor, t_prev, probes, fixed, in_hbm([images]))
    t_next, sums = other_rows(side, factor, back, t_prev, probes, fixed, t_next, sums)
    return (t_next, sum_over(sums, "slab"))


def solution(mesh):
    placed = (
        P(("slab", "grp"), None, None),
        P("slab", None),
        P("slab", None, "grp"),
        P("slab", None, "grp"),
        P("slab", None, "grp"),
    )
    return jax.shard_map(
        shards,
        mesh=mesh,
        in_specs=placed,
        out_specs=(P("slab", None, "grp"), P(None, "grp")),
        check_vma=False,
    )
```

time: 231 us -> 72.5 us (0.31)
  waiting for transfers between devices: 116 us -> 27.7 us
  blocking collectives: 48.3 us -> 0 us
  local copies, waits for them, and re-layouts: 25.3 us -> 1.12 us
  Pallas kernels: 0 us -> 23.9 us
  starting transfers between devices: 4.76 us -> 18.2 us
  between operations: 14.1 us -> 0.76 us
  other arithmetic: 11.4 us -> 0.57 us
  matrix products: 10.4 us -> 0 us
    ppermute x2 -> x15, waiting for transfers between devices: 87 us -> 27.7 us  [the longest x3 10.9 us: sum_over(): lax.ppermute(value, axis, [(i, i ^ hop) for i in range(size)])]
    all_gather x1 -> x0, waiting for transfers between devices: 28.7 us -> none  [shards(): whole = lax.all_gather(t_cur, 'grp', axis=2, tiled=True)]
    all_to_all x1 -> x0, blocking collectives: 28.2 us -> none  [shards(): lax.all_to_all(rows_image, 'grp', split_axis=2, concat_axis=0, tiled=True)]
    pallas_call x0 -> x8, Pallas kernels: none -> 23.9 us  [the longest x1 8.94 us: own_rows(): pl.pallas_call(functools.partial(own_kernel, len(chunks), factor), in_spe...]
    psum x1 -> x0, blocking collectives: 20.2 us -> none  [shards(): first, second = lax.psum((first, second), 'slab')]
    ppermute x2 -> x15, starting transfers between devices: 4.72 us -> 18.2 us  [the longest x2 3.8 us: shards(): near_oth = [pair(gate(oth[0], *held)), pair(oth[1])]]
    reshape x2 -> x0, local copies, waits for them, and re-layouts: 12.3 us -> none  [the longest x1 12.2 us: apply_rows(): squares = tile_rows.reshape(tile_rows.shape[:2] + (width, width))]
    gather x1 -> x0, local copies, waits for them, and re-layouts: 11.3 us -> none  [apply_rows(): near = jnp.take(padded, locals_rows.reshape(-1), axis=0)]
  transfers between devices with their start and end apart: 3 -> 15, of which waited for: 3 -> 10; matrix products, arithmetic and copies ran while one was open for 6% -> 2% of each run, Pallas kernels for 0% -> 29%
where the time goes in v2:
time: 72.5 us; the launch traced here: 72.3 us
  waiting for transfers between devices  27.7 us (38%)
  Pallas kernels  23.9 us (33%)
  starting transfers between devices  18.2 us (25%)
  local copies, waits for them, and re-layouts  1.12 us (2%)
  between operations  0.76 us (1%)
    ppermute x3, waiting for transfers between devices, sum_over(): lax.ppermute(value, axis, [(i, i ^ hop) for i in range(size)])  10.9 us
    pallas_call x1, Pallas kernels, own_rows(): pl.pallas_call(functools.partial(own_kernel, len(chunks), factor), in_spe...  8.94 us
    ppermute x1, waiting for transfers between devices, shards(): far_low = along(near_low)  8.37 us
    pallas_call x1, Pallas kernels, other_images(): pl.pallas_call(functools.partial(other_kernel, len(chunks)), in_specs=[SM...  6.28 us
    ppermute x2, waiting for transfers between devices, shards(): oth = [across(low), across(high)]  5 us
    pallas_call x2, Pallas kernels, squares(): pl.pallas_call(held_kernel if resident else functools.partial(square_kern...  4.88 us
    ppermute x2, starting transfers between devices, shards(): near_oth = [pair(gate(oth[0], *held)), pair(oth[1])]  3.8 us
    pallas_call x1, Pallas kernels, other_rows(): pl.pallas_call(functools.partial(final_kernel, factor), grid_spec=pltpu.P...  3.18 us
  transfers between devices with their start and end apart: 15, of which 10 were waited for; matrix products, arithmetic and copies ran while one was open for 2% of the time, Pallas kernels for 29%

profile of v2, /device:TPU:0, one launch (start us, length us, event | category | flops | bytes accessed | tf_op | source)
XLA Modules:
  0.0 72.3 jit_solution(15197679490926500475)
XLA Ops:
  0.6 0.5 collective-permute-start
  1.1 1.1 %fusion = (bf16[6,192,128]{2,1,0:T(8,128)(2,1)S(1)}, bf16[6,192,128]{2,1,0:T(8,128)(2,1)S(1)}) fusion(bf16[12,192,128]{2,1,0:T(8,128)(2,1)} %cur.1), kind=kLoop, calls=%fused_computation | loop fusion | bytes 1179648 | tf_op jit(solution)/shard_map/slice | solution.py:374
  2.2 2.6 %collective-permute-start.1 = (bf16[6,192,128]{2,1,0:T(8,128)(2,1)S(1)}, bf16[6,192,128]{2,1,0:T(8,128)(2,1)S(1)}, u32[]{:S(2)}, u32[]{:S(2)}) collective-permute-start(bf16[6,192,128]{2,1,0:T(8,128)(2,1)S(1)} %get-tuple-element.11.refs_0_), channel_id=1, source_target_pairs={{0,2},{1,3},{2,0},{3,1},{4,6},{5,7},{6,4},{7,5},{8,10},{9,11},{10,... | collective-permute-start | bytes 884744 | tf_op jit(solution)/shard_map/ppermute | solution.py:377
  4.8 1.5 %collective-permute-start.6 = (bf16[6,192,128]{2,1,0:T(8,128)(2,1)S(1)}, bf16[6,192,128]{2,1,0:T(8,128)(2,1)S(1)}, u32[]{:S(2)}, u32[]{:S(2)}) collective-permute-start(bf16[6,192,128]{2,1,0:T(8,128)(2,1)S(1)} %get-tuple-element.10), channel_id=1, source_target_pairs={{0,4},{4,0},{8,12},{12,8},{16,20},{20,16},{24,28},{28,24},{1,5},{5... | collective-permute-start | bytes 884744 | tf_op jit(solution)/shard_map/ppermute | solution.py:378
  6.3 0.5 collective-permute-start.2
  6.9 3.2 %squares.2.refs_1_.first.first_held = bf16[3,27,96,384]{3,2,1,0:T(8,128)(2,1)S(1)} custom-call(bf16[3,27,36864]{2,1,0:T(8,128)(2,1)} %tiles.1), custom_call_target="tpu_custom_call" | custom-call | flops 1 | bytes 18000000 | tf_op jit(solution)/shard_map/squares/pallas_call | solution.py:112
  10.1 0.0 copy-start
  10.1 2.5 %collective-permute-done.1.refs_0_ = bf16[6,192,128]{2,1,0:T(8,128)(2,1)S(1)} collective-permute-done((bf16[6,192,128]{2,1,0:T(8,128)(2,1)S(1)}, bf16[6,192,128]{2,1,0:T(8,128)(2,1)S(1)}, u32[]{:S(2)}, u32[]{:S(2)}) %collective-permute-start.1) | collective-permute-done | bytes 294944 | tf_op jit(solution)/shard_map/ppermute | solution.py:377
  12.7 0.0 copy-start.2
  12.7 2.0 %collective-permute-start.3 = (bf16[6,192,128]{2,1,0:T(8,128)(2,1)S(1)}, bf16[6,192,128]{2,1,0:T(8,128)(2,1)S(1)}, u32[]{:S(2)}, u32[]{:S(2)}) collective-permute-start(bf16[6,192,128]{2,1,0:T(8,128)(2,1)S(1)} %gate.2), channel_id=1, source_target_pairs={{0,4},{4,0},{8,12},{12,8},{16,20},{20,16},{24,28},{28,24},{1,5},{5... | collective-permute-start | bytes 884744 | tf_op jit(solution)/shard_map/ppermute | solution.py:381
  14.8 0.0 collective-permute-done.6.refs_2_
  14.8 1.6 %collective-permute-start.7 = (bf16[6,192,128]{2,1,0:T(8,128)(2,1)S(1)}, bf16[6,192,128]{2,1,0:T(8,128)(2,1)S(1)}, u32[]{:S(2)}, u32[]{:S(2)}) collective-permute-start(bf16[6,192,128]{2,1,0:T(8,128)(2,1)S(1)} %collective-permute-done.6.refs_2_), channel_id=1, source_target_pairs={{0,8},{4,28},{8,16},{12,4},{16,24},{20,12},{24,0},{28,20},{1,9},{5... | collective-permute-start | bytes 884744 | tf_op jit(solution)/shard_map/ppermute | solution.py:382
  16.3 2.5 %collective-permute-done.2.refs_1_ = bf16[6,192,128]{2,1,0:T(8,128)(2,1)S(1)} collective-permute-done((bf16[6,192,128]{2,1,0:T(8,128)(2,1)S(1)}, bf16[6,192,128]{2,1,0:T(8,128)(2,1)S(1)}, u32[]{:S(2)}, u32[]{:S(2)}) %collective-permute-start.2) | collective-permute-done | bytes 294944 | tf_op jit(solution)/shard_map/ppermute | solution.py:377
  18.8 1.8 %collective-permute-start.4 = (bf16[6,192,128]{2,1,0:T(8,128)(2,1)S(1)}, bf16[6,192,128]{2,1,0:T(8,128)(2,1)S(1)}, u32[]{:S(2)}, u32[]{:S(2)}) collective-permute-start(bf16[6,192,128]{2,1,0:T(8,128)(2,1)S(1)} %collective-permute-done.2.refs_1_), channel_id=1, source_target_pairs={{0,4},{4,0},{8,12},{12,8},{16,20},{20,16},{24,28},{28,24},{1,5},{5... | collective-permute-start | bytes 884744 | tf_op jit(solution)/shard_map/ppermute | solution.py:381
  20.6 0.9 %collective-permute-done.3.refs_2_ = bf16[6,192,128]{2,1,0:T(8,128)(2,1)S(1)} collective-permute-done((bf16[6,192,128]{2,1,0:T(8,128)(2,1)S(1)}, bf16[6,192,128]{2,1,0:T(8,128)(2,1)S(1)}, u32[]{:S(2)}, u32[]{:S(2)}) %collective-permute-start.3) | collective-permute-done | bytes 294944 | tf_op jit(solution)/shard_map/ppermute | solution.py:381
  21.5 1.6 %collective-permute-start.5 = (bf16[6,192,128]{2,1,0:T(8,128)(2,1)S(1)}, bf16[6,192,128]{2,1,0:T(8,128)(2,1)S(1)}, u32[]{:S(2)}, u32[]{:S(2)}) collective-permute-start(bf16[6,192,128]{2,1,0:T(8,128)(2,1)S(1)} %collective-permute-done.3.refs_2_), channel_id=1, source_target_pairs={{0,8},{4,28},{8,16},{12,4},{16,24},{20,12},{24,0},{28,20},{1,9},{5... | collective-permute-start | bytes 884744 | tf_op jit(solution)/shard_map/ppermute | solution.py:383
  23.1 1.5 %collective-permute-done.7.refs_4_ = bf16[6,192,128]{2,1,0:T(8,128)(2,1)S(1)} collective-permute-done((bf16[6,192,128]{2,1,0:T(8,128)(2,1)S(1)}, bf16[6,192,128]{2,1,0:T(8,128)(2,1)S(1)}, u32[]{:S(2)}, u32[]{:S(2)}) %collective-permute-start.7) | collective-permute-done | bytes 294944 | tf_op jit(solution)/shard_map/ppermute | solution.py:382
  24.6 1.5 %collective-permute-start.8 = (bf16[6,192,128]{2,1,0:T(8,128)(2,1)S(1)}, bf16[6,192,128]{2,1,0:T(8,128)(2,1)S(1)}, u32[]{:S(2)}, u32[]{:S(2)}) collective-permute-start(bf16[6,192,128]{2,1,0:T(8,128)(2,1)S(1)} %collective-permute-done.7.refs_4_), channel_id=1, source_target_pairs={{0,2},{1,3},{2,0},{3,1},{4,6},{5,7},{6,4},{7,5},{8,10},{9,11},{10,... | collective-permute-start | bytes 884744 | tf_op jit(solution)/shard_map/ppermute | solution.py:383
  26.1 0.0 collective-permute-done.tiles
  26.1 1.6 %squares.3.second.refs_1_.second_held = bf16[3,27,96,384]{3,2,1,0:T(8,128)(2,1)S(1)} custom-call(bf16[3,27,36864]{2,1,0:T(8,128)(2,1)S(1)} %collective-permute-done.tiles), custom_call_target="tpu_custom_call" | custom-call | flops 1 | bytes 18000000 | tf_op jit(solution)/shard_map/squares/pallas_call | solution.py:112
  27.7 0.0 copy-done.2
  27.8 0.0 copy-start.1
  27.8 0.6 meets.1.table
  28.4 2.1 %collective-permute-start.10 = (bf16[6,192,128]{2,1,0:T(8,128)(2,1)S(1)}, bf16[6,192,128]{2,1,0:T(8,128)(2,1)S(1)}, u32[]{:S(2)}, u32[]{:S(2)}) collective-permute-start(bf16[6,192,128]{2,1,0:T(8,128)(2,1)S(1)} %gate.3), channel_id=1, source_target_pairs={{0,4},{4,0},{8,12},{12,8},{16,20},{20,16},{24,28},{28,24},{1,5},{5... | collective-permute-start | bytes 884744 | tf_op jit(solution)/shard_map/ppermute | solution.py:385
  30.5 0.0 collective-permute-done.4.refs_3_
  30.5 0.4 collective-permute-done.5.refs_4_
  30.9 0.7 collective-permute-done.8.refs_5_
  31.6 0.0 copy-done
  31.6 6.3 %other_images.1.refs_8_ = f32[6,192,128]{2,1,0:T(8,128)} custom-call(s32[8,128]{1,0:T(8,128)S(4)} %meets.1.table, bf16[3,27,96,384]{3,2,1,0:T(8,128)(2,1)S(1)} %squares.2.refs_1_.first.first_held, bf16[3,27,96,384]{3,2,1,0:T(8,128)(2,1)S(1)} %squares.3.second.refs_1_.second_held, bf16[6,192,128]{2,1,0:T(8,128)(2,1)S(1)} %collective-permute-done.1.refs_0_, ...), custom_call_target="tpu_custom_call" | custom-call | flops 1 | bytes 18000000 | tf_op jit(solution)/shard_map/other_images/pallas_call | solution.py:195
  37.9 0.0 copy-done.1
  37.9 1.6 %collective-permute-start.9 = (f32[6,192,128]{2,1,0:T(8,128)}, f32[6,192,128]{2,1,0:T(8,128)S(1)}, u32[]{:S(2)}, u32[]{:S(2)}) collective-permute-start(f32[6,192,128]{2,1,0:T(8,128)} %other_images.1.refs_8_), channel_id=1, source_target_pairs={{0,2},{1,3},{2,0},{3,1},{4,6},{5,7},{6,4},{7,5},{8,10},{9,11},{10,... | collective-permute-start | bytes 1769480 | tf_op jit(solution)/shard_map/ppermute | solution.py:389
  39.5 0.0 collective-permute-done.10.refs_1_
  39.5 0.1 collective-permute-start.11
  39.7 8.4 %collective-permute-done.11.refs_3_ = bf16[6,192,128]{2,1,0:T(8,128)(2,1)S(1)} collective-permute-done((bf16[6,192,128]{2,1,0:T(8,128)(2,1)S(1)}, bf16[6,192,128]{2,1,0:T(8,128)(2,1)S(1)}, u32[]{:S(2)}, u32[]{:S(2)}) %collective-permute-start.11) | collective-permute-done | bytes 294944 | tf_op jit(solution)/shard_map/ppermute | solution.py:386
  48.0 8.9 %own_rows.1 = (f32[12,192,128]{2,1,0:T(8,128)}, f32[16,128]{1,0:T(8,128)S(1)}) custom-call(s32[8,128]{1,0:T(8,128)S(4)} %meets.1.table, bf16[3,27,96,384]{3,2,1,0:T(8,128)(2,1)} %copy-done, bf16[3,27,96,384]{3,2,1,0:T(8,128)(2,1)} %copy-done.1, bf16[12,192,128]{2,1,0:T(8,128)(2,1)} %cur.1, bf16[6,192,128]{2,1,0:T(8,128)(2,1)S(1)} %collective-permute-done.10.refs_1_, ...), custom_call_target="tpu_custom_call" | custom-call | flops 1 | bytes 18000000 | tf_op jit(solution)/shard_map/own_rows/pallas_call | solution.py:263
  57.0 0.0 collective-permute-done.9.image
  57.0 3.2 %other_rows.1 = (f32[12,192,128]{2,1,0:T(8,128)}, f32[2,128]{1,0:T(2,128)S(1)}) custom-call(s32[1]{0:T(128)} %bitcast.side, f32[6,192,128]{2,1,0:T(8,128)S(1)} %collective-permute-done.9.image, f32[12,192,128]{2,1,0:T(8,128)} %prev.1, f32[12,192,128]{2,1,0:T(8,128)} %probes.1, bf16[12,192,128]{2,1,0:T(8,128)(2,1)} %cur.1, ...), custom_call_target="tpu_custom_call", output_to_operand_aliasing={{0}: (5, {})} | custom-call | flops 1 | bytes 1 | tf_op jit(solution)/shard_map/other_rows/pallas_call | solution.py:311
  60.2 0.2 collective-permute-start.12
  60.3 3.4 %collective-permute-done.12 = f32[2,128]{1,0:T(2,128)S(1)} collective-permute-done((f32[2,128]{1,0:T(2,128)S(1)}, f32[2,128]{1,0:T(2,128)S(1)}, u32[]{:S(2)}, u32[]{:S(2)}) %collective-permute-start.12) | collective-permute-done | bytes 1056 | tf_op jit(solution)/shard_map/ppermute | solution.py:352
  63.7 0.0 collective-permute-start.13
  63.7 3.6 %collective-permute-done.13 = f32[2,128]{1,0:T(2,128)S(1)} collective-permute-done((f32[2,128]{1,0:T(2,128)S(1)}, f32[2,128]{1,0:T(2,128)S(1)}, u32[]{:S(2)}, u32[]{:S(2)}) %collective-permute-start.13) | collective-permute-done | bytes 1056 | tf_op jit(solution)/shard_map/ppermute | solution.py:352
  67.3 0.6 collective-permute-start.14
  67.9 3.9 %collective-permute-done.14 = f32[2,128]{1,0:T(2,128)S(1)} collective-permute-done((f32[2,128]{1,0:T(2,128)S(1)}, f32[2,128]{1,0:T(2,128)S(1)}, u32[]{:S(2)}, u32[]{:S(2)}) %collective-permute-start.14) | collective-permute-done | bytes 1056 | tf_op jit(solution)/shard_map/ppermute | solution.py:352
  71.8 0.6 add.12
  (5 shorter events, 0.0 us)
Async XLA Ops:
  0.6 25.5 %collective-permute-start = (bf16[3,27,36864]{2,1,0:T(8,128)(2,1)}, bf16[3,27,36864]{2,1,0:T(8,128)(2,1)S(1)}, u32[]{:S(2)}, u32[]{:S(2)}) collective-permute-start(bf16[3,27,36864]{2,1,0:T(8,128)(2,1)} %tiles.1), channel_id=1, source_target_pairs={{0,1},{1,0},{2,3},{3,2},{4,5},{5,4},{6,7},{7,6},{8,9},{9,8},{10,11... | collective-permute-start | bytes 17915912 | tf_op jit(solution)/shard_map/ppermute | solution.py:376
  2.2 10.4 %collective-permute-start.1 = (bf16[6,192,128]{2,1,0:T(8,128)(2,1)S(1)}, bf16[6,192,128]{2,1,0:T(8,128)(2,1)S(1)}, u32[]{:S(2)}, u32[]{:S(2)}) collective-permute-start(bf16[6,192,128]{2,1,0:T(8,128)(2,1)S(1)} %get-tuple-element.11.refs_0_), channel_id=1, source_target_pairs={{0,2},{1,3},{2,0},{3,1},{4,6},{5,7},{6,4},{7,5},{8,10},{9,11},{10,... | collective-permute-start | bytes 884744 | tf_op jit(solution)/shard_map/ppermute | solution.py:377
  4.8 9.9 %collective-permute-start.6 = (bf16[6,192,128]{2,1,0:T(8,128)(2,1)S(1)}, bf16[6,192,128]{2,1,0:T(8,128)(2,1)S(1)}, u32[]{:S(2)}, u32[]{:S(2)}) collective-permute-start(bf16[6,192,128]{2,1,0:T(8,128)(2,1)S(1)} %get-tuple-element.10), channel_id=1, source_target_pairs={{0,4},{4,0},{8,12},{12,8},{16,20},{20,16},{24,28},{28,24},{1,5},{5... | collective-permute-start | bytes 884744 | tf_op jit(solution)/shard_map/ppermute | solution.py:378
  6.3 12.5 %collective-permute-start.2 = (bf16[6,192,128]{2,1,0:T(8,128)(2,1)S(1)}, bf16[6,192,128]{2,1,0:T(8,128)(2,1)S(1)}, u32[]{:S(2)}, u32[]{:S(2)}) collective-permute-start(bf16[6,192,128]{2,1,0:T(8,128)(2,1)S(1)} %get-tuple-element.10), channel_id=1, source_target_pairs={{0,2},{1,3},{2,0},{3,1},{4,6},{5,7},{6,4},{7,5},{8,10},{9,11},{10,... | collective-permute-start | bytes 884744 | tf_op jit(solution)/shard_map/ppermute | solution.py:377
  10.1 21.5 %copy-start = (bf16[3,27,96,384]{3,2,1,0:T(8,128)(2,1)}, bf16[3,27,96,384]{3,2,1,0:T(8,128)(2,1)S(1)}, u32[]{:S(2)}) copy-start(bf16[3,27,96,384]{3,2,1,0:T(8,128)(2,1)S(1)} %squares.2.refs_1_.first.first_held) | copy-start | bytes 17915908
  12.7 15.0 %copy-start.2 = (s32[12,27]{1,0:T(8,128)S(1)}, s32[12,27]{1,0:T(8,128)}, u32[]{:S(2)}) copy-start(s32[12,27]{1,0:T(8,128)} %neighbours.1) | copy-start | bytes 3892
  12.7 8.7 %collective-permute-start.3 = (bf16[6,192,128]{2,1,0:T(8,128)(2,1)S(1)}, bf16[6,192,128]{2,1,0:T(8,128)(2,1)S(1)}, u32[]{:S(2)}, u32[]{:S(2)}) collective-permute-start(bf16[6,192,128]{2,1,0:T(8,128)(2,1)S(1)} %gate.2), channel_id=1, source_target_pairs={{0,4},{4,0},{8,12},{12,8},{16,20},{20,16},{24,28},{28,24},{1,5},{5... | collective-permute-start | bytes 884744 | tf_op jit(solution)/shard_map/ppermute | solution.py:381
  14.8 9.8 %collective-permute-start.7 = (bf16[6,192,128]{2,1,0:T(8,128)(2,1)S(1)}, bf16[6,192,128]{2,1,0:T(8,128)(2,1)S(1)}, u32[]{:S(2)}, u32[]{:S(2)}) collective-permute-start(bf16[6,192,128]{2,1,0:T(8,128)(2,1)S(1)} %collective-permute-done.6.refs_2_), channel_id=1, source_target_pairs={{0,8},{4,28},{8,16},{12,4},{16,24},{20,12},{24,0},{28,20},{1,9},{5... | collective-permute-start | bytes 884744 | tf_op jit(solution)/shard_map/ppermute | solution.py:382
  18.8 11.7 %collective-permute-start.4 = (bf16[6,192,128]{2,1,0:T(8,128)(2,1)S(1)}, bf16[6,192,128]{2,1,0:T(8,128)(2,1)S(1)}, u32[]{:S(2)}, u32[]{:S(2)}) collective-permute-start(bf16[6,192,128]{2,1,0:T(8,128)(2,1)S(1)} %collective-permute-done.2.refs_1_), channel_id=1, source_target_pairs={{0,4},{4,0},{8,12},{12,8},{16,20},{20,16},{24,28},{28,24},{1,5},{5... | collective-permute-start | bytes 884744 | tf_op jit(solution)/shard_map/ppermute | solution.py:381
  21.5 9.5 %collective-permute-start.5 = (bf16[6,192,128]{2,1,0:T(8,128)(2,1)S(1)}, bf16[6,192,128]{2,1,0:T(8,128)(2,1)S(1)}, u32[]{:S(2)}, u32[]{:S(2)}) collective-permute-start(bf16[6,192,128]{2,1,0:T(8,128)(2,1)S(1)} %collective-permute-done.3.refs_2_), channel_id=1, source_target_pairs={{0,8},{4,28},{8,16},{12,4},{16,24},{20,12},{24,0},{28,20},{1,9},{5... | collective-permute-start | bytes 884744 | tf_op jit(solution)/shard_map/ppermute | solution.py:383
  24.6 7.1 %collective-permute-start.8 = (bf16[6,192,128]{2,1,0:T(8,128)(2,1)S(1)}, bf16[6,192,128]{2,1,0:T(8,128)(2,1)S(1)}, u32[]{:S(2)}, u32[]{:S(2)}) collective-permute-start(bf16[6,192,128]{2,1,0:T(8,128)(2,1)S(1)} %collective-permute-done.7.refs_4_), channel_id=1, source_target_pairs={{0,2},{1,3},{2,0},{3,1},{4,6},{5,7},{6,4},{7,5},{8,10},{9,11},{10,... | collective-permute-start | bytes 884744 | tf_op jit(solution)/shard_map/ppermute | solution.py:383
  27.8 10.2 %copy-start.1 = (bf16[3,27,96,384]{3,2,1,0:T(8,128)(2,1)}, bf16[3,27,96,384]{3,2,1,0:T(8,128)(2,1)S(1)}, u32[]{:S(2)}) copy-start(bf16[3,27,96,384]{3,2,1,0:T(8,128)(2,1)S(1)} %squares.3.second.refs_1_.second_held) | copy-start | bytes 17915908
  28.4 11.1 %collective-permute-start.10 = (bf16[6,192,128]{2,1,0:T(8,128)(2,1)S(1)}, bf16[6,192,128]{2,1,0:T(8,128)(2,1)S(1)}, u32[]{:S(2)}, u32[]{:S(2)}) collective-permute-start(bf16[6,192,128]{2,1,0:T(8,128)(2,1)S(1)} %gate.3), channel_id=1, source_target_pairs={{0,4},{4,0},{8,12},{12,8},{16,20},{20,16},{24,28},{28,24},{1,5},{5... | collective-permute-start | bytes 884744 | tf_op jit(solution)/shard_map/ppermute | solution.py:385
  37.9 19.0 %collective-permute-start.9 = (f32[6,192,128]{2,1,0:T(8,128)}, f32[6,192,128]{2,1,0:T(8,128)S(1)}, u32[]{:S(2)}, u32[]{:S(2)}) collective-permute-start(f32[6,192,128]{2,1,0:T(8,128)} %other_images.1.refs_8_), channel_id=1, source_target_pairs={{0,2},{1,3},{2,0},{3,1},{4,6},{5,7},{6,4},{7,5},{8,10},{9,11},{10,... | collective-permute-start | bytes 1769480 | tf_op jit(solution)/shard_map/ppermute | solution.py:389
  39.5 8.5 %collective-permute-start.11 = (bf16[6,192,128]{2,1,0:T(8,128)(2,1)S(1)}, bf16[6,192,128]{2,1,0:T(8,128)(2,1)S(1)}, u32[]{:S(2)}, u32[]{:S(2)}) collective-permute-start(bf16[6,192,128]{2,1,0:T(8,128)(2,1)S(1)} %collective-permute-done.10.refs_1_), channel_id=1, source_target_pairs={{0,8},{4,28},{8,16},{12,4},{16,24},{20,12},{24,0},{28,20},{1,9},{5... | collective-permute-start | bytes 884744 | tf_op jit(solution)/shard_map/ppermute | solution.py:386
  60.2 3.6 %collective-permute-start.12 = (f32[2,128]{1,0:T(2,128)S(1)}, f32[2,128]{1,0:T(2,128)S(1)}, u32[]{:S(2)}, u32[]{:S(2)}) collective-permute-start(f32[2,128]{1,0:T(2,128)S(1)} %get-tuple-element.9), channel_id=1, source_target_pairs={{0,4},{4,0},{8,12},{12,8},{16,20},{20,16},{24,28},{28,24},{1,5},{5... | collective-permute-start | bytes 3080 | tf_op jit(solution)/shard_map/ppermute | solution.py:352
  63.7 3.6 %collective-permute-start.13 = (f32[2,128]{1,0:T(2,128)S(1)}, f32[2,128]{1,0:T(2,128)S(1)}, u32[]{:S(2)}, u32[]{:S(2)}) collective-permute-start(f32[2,128]{1,0:T(2,128)S(1)} %add.10), channel_id=1, source_target_pairs={{0,8},{4,12},{8,0},{12,4},{16,24},{20,28},{24,16},{28,20},{1,9},{5... | collective-permute-start | bytes 3080 | tf_op jit(solution)/shard_map/ppermute | solution.py:352
  67.3 4.5 %collective-permute-start.14 = (f32[2,128]{1,0:T(2,128)S(1)}, f32[2,128]{1,0:T(2,128)S(1)}, u32[]{:S(2)}, u32[]{:S(2)}) collective-permute-start(f32[2,128]{1,0:T(2,128)S(1)} %add.11), channel_id=1, source_target_pairs={{0,16},{4,20},{8,24},{12,28},{16,0},{20,4},{24,8},{28,12},{1,17},{... | collective-permute-start | bytes 3080 | tf_op jit(solution)/shard_map/ppermute | solution.py:352

commit v3 on v2

--- a/solution.py
+++ b/solution.py
@@ -11,7 +11,9 @@
 GRANT = 20 * 1024 * 1024
 BLOCKS = 6
 PAD = 64
+LEVELS = 32760.0
 LIGHT = pl.CostEstimate(flops=1, bytes_accessed=1, transcendentals=0)
+LONG = pl.CostEstimate(flops=1, bytes_accessed=1_000_000_000, transcendentals=0)
 HEAVY = pl.CostEstimate(flops=1, bytes_accessed=18_000_000, transcendentals=0)
 VMEM = pl.BlockSpec(memory_space=pltpu.VMEM)
 SMEM = pl.BlockSpec(memory_space=pltpu.SMEM)
@@ -172,22 +174,42 @@
     return pltpu.VMEM((sum(c.shape[0] for c in chunks),) + chunks[0].shape[1:], chunks[0].dtype)
 
 
+def largest(power, size):
+    return size * jnp.exp2(power - 14.0)
+
+
 def other_kernel(n_chunks, table, first, second, *refs):
     chunks = refs[:n_chunks]
-    out, near, image, near_sems, out_sems = refs[-5:]
-    half = first.shape[2]
+    out, near, image, coded, scales, near_sems, out_sems = refs[-7:]
+    half, rows = first.shape[2], image.shape[0]
+    scales[...] = jnp.zeros_like(scales)
     for load in start_near(chunks, near, near_sems):
         load.wait()
 
+    def send(b):
+        rows_out = out.at[pl.ds(pl.multiple_of(place(b) * rows, rows), rows)]
+        return pltpu.make_async_copy(coded.at[b], rows_out, out_sems.at[b])
+
     def body(b, tiles):
         even, odd = multiply(tiles, table, b, near)
-        image[b, pl.ds(0, half, 2), :] = even
-        image[b, pl.ds(1, half, 2), :] = odd
-        copy(image.at[b], out.at[place(b)], out_sems.at[b])
+        image[pl.ds(0, half, 2), :] = even
+        image[pl.ds(1, half, 2), :] = odd
+        value = image[...]
+        top = jnp.maximum(jnp.max(jnp.abs(value), axis=0, keepdims=True), 1e-30)
+        power = jnp.ceil(jnp.log2(top))
+        size = jnp.ceil(top * jnp.exp2(14.0 - power))
+        scales[pl.ds(place(b), 1), :] = power
+        scales[pl.ds(8 + place(b), 1), :] = size
+        value = jnp.round(value * (LEVELS / largest(power, size)))
+        coded[b] = value.astype(jnp.int32).astype(jnp.int16)
+        send(b).start()
 
     each_block((first, second), body)
+    coded[BLOCKS, :16, :] = scales[...].astype(jnp.int32).astype(jnp.int16)
+    last = copy(coded.at[BLOCKS, pl.ds(0, 16)], out.at[pl.ds(BLOCKS * rows, 16)], out_sems.at[BLOCKS])
     for b in range(BLOCKS):
-        pltpu.make_async_copy(image.at[b], out.at[place(b)], out_sems.at[b]).wait()
+        send(b).wait()
+    last.wait()
 
 
 def other_images(table, held, chunks, after):
@@ -196,15 +218,17 @@
         functools.partial(other_kernel, len(chunks)),
         in_specs=[SMEM] + [VMEM] * 2 + [ANY] * (len(chunks) + len(after)),
         out_specs=HBM,
-        out_shape=pltpu.HBM((BLOCKS, rows, cols), jnp.float32),
+        out_shape=pltpu.HBM((BLOCKS * rows + 16, cols), jnp.int16),
         scratch_shapes=[
             near_scratch(chunks),
-            pltpu.VMEM((BLOCKS, rows, cols), jnp.float32),
+            pltpu.VMEM((rows, cols), jnp.float32),
+            pltpu.VMEM((BLOCKS + 1, rows, cols), jnp.int16),
+            pltpu.VMEM((16, cols), jnp.float32),
             DMA((len(chunks),)),
-            DMA((BLOCKS,)),
+            DMA((BLOCKS + 1,)),
         ],
         compiler_params=params(),
-        cost_estimate=HEAVY,
+        cost_estimate=LONG,
         name="other_images",
     )(in_smem(table), *in_vmem(held), *chunks, *after)
 
@@ -217,7 +241,8 @@
 
 def own_kernel(n_chunks, factor, table, first_held, second_held, *refs):
     chunks, rows_in = refs[:n_chunks], refs[n_chunks : n_chunks + 3]
-    out, sums, near, held, image, prev, probes, cur, near_sems, held_sems, row_sems, out_sems = refs[-12:]
+    out, sums, *later = refs[n_chunks + 4 : n_chunks + 9]
+    near, held, image, prev, probes, cur, near_sems, held_sems, row_sems, later_sems, out_sems = refs[-11:]
     half = first_held.shape[2]
     loads = start_near(chunks, near, near_sems)
     slots = held.shape[0]
@@ -234,8 +259,9 @@
     for n in range(slots - 1):
         load_next(n)
     first = (lax.axis_index("grp") // 2) * BLOCKS
+    mine = []
     for n, (src, dst) in enumerate(zip(rows_in, (prev, probes, cur))):
-        loads.append(copy(src.at[pl.ds(first, BLOCKS)], dst, row_sems.at[n]))
+        mine.append(copy(src.at[pl.ds(first, BLOCKS)], dst, row_sems.at[n]))
     sums[...] = jnp.zeros_like(sums)
     for made in loads:
         made.wait()
@@ -246,6 +272,14 @@
         load(b, first_held.at[0]).wait()
         at = place(b)
         even, odd = multiply(held.at[b % slots], table, b, near)
+
+        @pl.when(b == 0)
+        def _():
+            for made in mine:
+                made.wait()
+            for n, (src, dst) in enumerate(zip(rows_in, later)):
+                copy(src.at[pl.ds(BLOCKS - first, BLOCKS)], dst, later_sems.at[n])
+
         image[b, pl.ds(0, half, 2), :] = even
         image[b, pl.ds(1, half, 2), :] = odd
         value = 2.0 * image[b] - prev[at]
@@ -253,6 +287,8 @@
         copy(image.at[b], out.at[first + at], out_sems.at[b])
         add_sums(factor, value, probes[at], cur[at], sums)
 
+    for n, (src, dst) in enumerate(zip(rows_in, later)):
+        pltpu.make_async_copy(src.at[pl.ds(BLOCKS - first, BLOCKS)], dst, later_sems.at[n]).wait()
     for b in range(BLOCKS):
         pltpu.make_async_copy(image.at[b], out.at[first + place(b)], out_sems.at[b]).wait()
 
@@ -263,10 +299,13 @@
     return pl.pallas_call(
         functools.partial(own_kernel, len(chunks), factor),
         in_specs=[SMEM] + [HBM] * 2 + [ANY] * (len(chunks) + 3 + len(after)),
-        out_specs=[HBM, VMEM],
+        out_specs=[HBM] + [VMEM] * 4,
         out_shape=[
-            jax.ShapeDtypeStruct(prev.shape, jnp.float32),
-            jax.ShapeDtypeStruct((16, cols), jnp.float32),
+            pltpu.HBM(prev.shape, jnp.float32),
+            pltpu.VMEM((16, cols), jnp.float32),
+            pltpu.VMEM(part, jnp.float32),
+            pltpu.VMEM(part, jnp.float32),
+            pltpu.VMEM(part, cur.dtype),
         ],
         scratch_shapes=[
             near_scratch(chunks),
@@ -278,69 +317,61 @@
             DMA((len(chunks),)),
             DMA((3,)),
             DMA((3,)),
+            DMA((3,)),
             DMA((BLOCKS,)),
         ],
         compiler_params=params(),
-        cost_estimate=HEAVY,
+        cost_estimate=LONG,
         name="own_rows",
     )(in_smem(table), *in_hbm(held), *chunks, prev, probes, cur, *after)
 
 
-def final_kernel(factor, side, image, prev, probes, cur, _, sums_in, out, sums, acc):
-    step = pl.program_id(0)
-
-    @pl.when(step == 0)
-    def _():
-        acc[...] = sums_in[...]
-
-    value = 2.0 * image[...] - prev[...]
-    out[...] = value
-    add_sums(factor, value, probes[...], cur[...], acc)
-
-    @pl.when(step == pl.num_programs(0) - 1)
-    def _():
-        for n in range(2):
-            sums[pl.ds(n, 1), :] = jnp.sum(acc[pl.ds(8 * n, 8), :], axis=0, keepdims=True)
-
-
-def other_rows(side, factor, image, prev, probes, cur, t_next, sums):
-    half, rows, cols = image.shape
-    steps = 3
-    block = (half // steps, rows, cols)
-    spot = pl.BlockSpec(block, lambda i, side: ((1 - side[0]) * steps + i, 0, 0))
+def final_kernel(factor, coded, prev, probes, cur, sums_in, _, out, sums, value, acc, sem):
+    rows = prev.shape[1]
+    scales = coded[pl.ds(BLOCKS * rows, 16), :].astype(jnp.int32).astype(jnp.float32)
+    step = largest(scales[:8], scales[8:]) * (1.0 / LEVELS)
+    for b in range(BLOCKS):
+        image = coded[pl.ds(b * rows, rows), :].astype(jnp.int32).astype(jnp.float32) * step[b : b + 1]
+        value[b] = 2.0 * image - prev[b]
+    first = (1 - lax.axis_index("grp") // 2) * BLOCKS
+    send = copy(value, out.at[pl.ds(first, BLOCKS)], sem)
+    acc[...] = sums_in[...]
+    for b in range(BLOCKS):
+        add_sums(factor, value[b], probes[b], cur[b], acc)
+    for n in range(2):
+        sums[pl.ds(n, 1), :] = jnp.sum(acc[pl.ds(8 * n, 8), :], axis=0, keepdims=True)
+    send.wait()
+
+
+def other_rows(factor, coded, prev, probes, cur, t_next, sums):
+    cols = cur.shape[2]
     return pl.pallas_call(
         functools.partial(final_kernel, factor),
-        grid_spec=pltpu.PrefetchScalarGridSpec(
-            num_scalar_prefetch=1,
-            grid=(steps,),
-            in_specs=[pl.BlockSpec(block, lambda i, side: (i, 0, 0))]
-            + [spot] * 3
-            + [pl.BlockSpec(memory_space=pl.ANY), pl.BlockSpec((16, cols), lambda i, side: (0, 0))],
-            out_specs=[spot, pl.BlockSpec((2, cols), lambda i, side: (0, 0))],
-            scratch_shapes=[pltpu.VMEM((16, cols), jnp.float32)],
-        ),
+        in_specs=[VMEM] * 5 + [HBM],
+        out_specs=[HBM, VMEM],
         out_shape=[
-            jax.ShapeDtypeStruct(prev.shape, jnp.float32),
+            pltpu.HBM(t_next.shape, jnp.float32),
             jax.ShapeDtypeStruct((2, cols), jnp.float32),
         ],
+        scratch_shapes=[pltpu.VMEM(prev.shape, jnp.float32), pltpu.VMEM((16, cols), jnp.float32), DMA],
         input_output_aliases={5: 0},
         compiler_params=params(),
         cost_estimate=LIGHT,
         name="other_rows",
-    )(side, image, prev, probes, cur, t_next, sums)
+    )(*in_vmem([coded, prev, probes, cur, sums]), *in_hbm([t_next]))
 
 
 def gate(value, *after):
     return pl.pallas_call(
         lambda *refs: None,
-        in_specs=[ANY] * (1 + len(after)),
+        in_specs=[ANY] + [SMEM if a.dtype == jnp.int32 else ANY for a in after],
         out_specs=ANY,
         out_shape=jax.ShapeDtypeStruct(value.shape, value.dtype),
         input_output_aliases={0: 0},
         compiler_params=params(),
         cost_estimate=LIGHT,
         name="gate",
-    )(value, *after)
+    )(value, *[in_smem(a) if a.dtype == jnp.int32 else a for a in after])
 
 
 def sum_over(value, axis):
@@ -358,7 +389,6 @@
     blocks, rows, cols = t_cur.shape
     per = tiles.shape[0]
     slabs, lanes = lax.axis_size("slab"), lax.axis_size("grp")
-    side = (lax.axis_index("grp") // 2).astype(jnp.int32)[None]
     factor = 1.0 / math.sqrt(slabs * blocks * rows)
     across = functools.partial(lax.ppermute, axis_name="grp", perm=[(i, i ^ 2) for i in range(lanes)])
     sibling = functools.partial(lax.ppermute, axis_name="grp", perm=[(i, i ^ 1) for i in range(lanes)])
@@ -378,18 +408,19 @@
     near_high = pair(high)
     table = meets(neighbours)
     held = [squares(tiles, rows, False)]
-    near_oth = [pair(gate(oth[0], *held)), pair(oth[1])]
+    held.append(squares(sib_tiles, rows, True))
+    near_oth = [pair(gate(oth[0], held[0], table)), pair(oth[1])]
     far_high = along(near_high)
     far_oth = [along(near_oth[0]), across(far_high)]
-    held.append(squares(sib_tiles, rows, True))
     near_low = pair(gate(low, held[1]))
-    far_low = along(near_low)
+    far_low = across(far_oth[0])
 
     images = other_images(table, held, [*oth, *near_oth, *far_oth], ())
+    images = gate(images, near_low, far_low)
     back = across(images)
     own = [fixed, near_low, near_high, far_low, far_high]
-    t_next, sums = own_rows(table, held, own, factor, t_prev, probes, fixed, in_hbm([images]))
-    t_next, sums = other_rows(side, factor, back, t_prev, probes, fixed, t_next, sums)
+    t_next, sums, *later = own_rows(table, held, own, factor, t_prev, probes, fixed, in_hbm([images]))
+    t_next, sums = other_rows(factor, back, *later, t_next, sums)
     return (t_next, sum_over(sums, "slab"))
 
 

time: 72.5 us -> 65.4 us (0.902)
  waiting for transfers between devices: 27.7 us -> 19.6 us
  starting transfers between devices: 18.2 us -> 21.2 us
  Pallas kernels: 23.9 us -> 21.9 us
    ppermute x3, waiting for transfers between devices: 9.27 us -> 3.99 us  [the longest x2 3.99 us: shards(): near_oth = [pair(gate(oth[0], held[0], table)), pair(oth[1])]]
    ppermute x2, waiting for transfers between devices: 5 us -> 2.22 us  [shards(): oth = [across(low), across(high)]]
    pallas_call x3 -> x4, Pallas kernels: 3.18 us -> 0.94 us  [the longest x1 0.94 us: other_rows(): pl.pallas_call(functools.partial(final_kernel, factor), in_specs=[VMEM] *...]
    ppermute x3, starting transfers between devices: 3.95 us -> 5.91 us  [the longest x2 5.38 us: shards(): near_oth = [pair(gate(oth[0], held[0], table)), pair(oth[1])]]
    ppermute x2, waiting for transfers between devices: 1.13 us -> 2.97 us  [shards(): far_oth = [along(near_oth[0]), across(far_high)]]
    ppermute x1, waiting for transfers between devices: 1.48 us -> 0.04 us  [shards(): far_high = along(near_high)]
    ppermute x1, starting transfers between devices: 2.09 us -> 0.7 us  [shards(): near_low = pair(gate(low, held[1]))]
    ppermute x1, starting transfers between devices: 1.55 us -> 2.55 us  [shards(): back = across(images)]
  transfers between devices with their start and end apart: 15 -> 15, of which waited for: 10 -> 7; matrix products, arithmetic and copies ran while one was open for 2% -> 2% of each run, Pallas kernels for 29% -> 32%
where the time goes in v3:
time: 65.4 us; the launch traced here: 65.2 us
  Pallas kernels  21.9 us (33%)
  starting transfers between devices  21.2 us (32%)
  waiting for transfers between devices  19.6 us (30%)
  local copies, waits for them, and re-layouts  1.12 us (2%)
  between operations  0.77 us (1%)
    ppermute x3, waiting for transfers between devices, sum_over(): lax.ppermute(value, axis, [(i, i ^ hop) for i in range(size)])  10.4 us
    pallas_call x1, Pallas kernels, own_rows(): pl.pallas_call(functools.partial(own_kernel, len(chunks), factor), in_spe...  8.83 us
    pallas_call x1, Pallas kernels, other_images(): pl.pallas_call(functools.partial(other_kernel, len(chunks)), in_specs=[SM...  6.65 us
    ppermute x2, starting transfers between devices, shards(): near_oth = [pair(gate(oth[0], held[0], table)), pair(oth[1])]  5.38 us
    pallas_call x2, Pallas kernels, squares(): pl.pallas_call(held_kernel if resident else functools.partial(square_kern...  4.88 us
    ppermute x2, starting transfers between devices, shards(): oth = [across(low), across(high)]  4.06 us
    ppermute x2, waiting for transfers between devices, shards(): near_oth = [pair(gate(oth[0], held[0], table)), pair(oth[1])]  3.99 us
    ppermute x2, starting transfers between devices, shards(): far_oth = [along(near_oth[0]), across(far_high)]  3.08 us
  transfers between devices with their start and end apart: 15, of which 7 were waited for; matrix products, arithmetic and copies ran while one was open for 2% of the time, Pallas kernels for 32%

profile of v3, /device:TPU:0, one launch (start us, length us, event | category | flops | bytes accessed | tf_op | source)
XLA Modules:
  0.0 65.2 jit_solution(16856701441595323768)
XLA Ops:
  0.6 0.5 collective-permute-start
  1.1 1.1 %fusion = (bf16[6,192,128]{2,1,0:T(8,128)(2,1)S(1)}, bf16[6,192,128]{2,1,0:T(8,128)(2,1)S(1)}) fusion(bf16[12,192,128]{2,1,0:T(8,128)(2,1)} %refs_7_.1), kind=kLoop, calls=%fused_computation | loop fusion | bytes 1179648 | tf_op jit(solution)/shard_map/slice | solution.py:404
  2.2 2.6 %collective-permute-start.1 = (bf16[6,192,128]{2,1,0:T(8,128)(2,1)S(1)}, bf16[6,192,128]{2,1,0:T(8,128)(2,1)S(1)}, u32[]{:S(2)}, u32[]{:S(2)}) collective-permute-start(bf16[6,192,128]{2,1,0:T(8,128)(2,1)S(1)} %get-tuple-element.17.refs_0_), channel_id=1, source_target_pairs={{0,2},{1,3},{2,0},{3,1},{4,6},{5,7},{6,4},{7,5},{8,10},{9,11},{10,... | collective-permute-start | bytes 884744 | tf_op jit(solution)/shard_map/ppermute | solution.py:407
  4.8 0.0 copy-start.2
  4.8 1.5 %collective-permute-start.6 = (bf16[6,192,128]{2,1,0:T(8,128)(2,1)S(1)}, bf16[6,192,128]{2,1,0:T(8,128)(2,1)S(1)}, u32[]{:S(2)}, u32[]{:S(2)}) collective-permute-start(bf16[6,192,128]{2,1,0:T(8,128)(2,1)S(1)} %get-tuple-element.16), channel_id=1, source_target_pairs={{0,4},{4,0},{8,12},{12,8},{16,20},{20,16},{24,28},{28,24},{1,5},{5... | collective-permute-start | bytes 884744 | tf_op jit(solution)/shard_map/ppermute | solution.py:408
  6.3 3.2 %squares.2.refs_1_.first.first_held = bf16[3,27,96,384]{3,2,1,0:T(8,128)(2,1)S(1)} custom-call(bf16[3,27,36864]{2,1,0:T(8,128)(2,1)} %tiles.1), custom_call_target="tpu_custom_call" | custom-call | flops 1 | bytes 18000000 | tf_op jit(solution)/shard_map/squares/pallas_call | solution.py:114
  9.6 0.0 copy-done.2
  9.6 0.0 copy-start
  9.6 0.6 meets.1.refs_2_.table
  10.3 2.2 %collective-permute-done.1.refs_0_ = bf16[6,192,128]{2,1,0:T(8,128)(2,1)S(1)} collective-permute-done((bf16[6,192,128]{2,1,0:T(8,128)(2,1)S(1)}, bf16[6,192,128]{2,1,0:T(8,128)(2,1)S(1)}, u32[]{:S(2)}, u32[]{:S(2)}) %collective-permute-start.1) | collective-permute-done | bytes 294944 | tf_op jit(solution)/shard_map/ppermute | solution.py:407
  12.5 1.8 %collective-permute-start.3 = (bf16[6,192,128]{2,1,0:T(8,128)(2,1)S(1)}, bf16[6,192,128]{2,1,0:T(8,128)(2,1)S(1)}, u32[]{:S(2)}, u32[]{:S(2)}) collective-permute-start(bf16[6,192,128]{2,1,0:T(8,128)(2,1)S(1)} %gate.3), channel_id=1, source_target_pairs={{0,4},{4,0},{8,12},{12,8},{16,20},{20,16},{24,28},{28,24},{1,5},{5... | collective-permute-start | bytes 884744 | tf_op jit(solution)/shard_map/ppermute | solution.py:412
  14.3 1.5 %collective-permute-start.2 = (bf16[6,192,128]{2,1,0:T(8,128)(2,1)S(1)}, bf16[6,192,128]{2,1,0:T(8,128)(2,1)S(1)}, u32[]{:S(2)}, u32[]{:S(2)}) collective-permute-start(bf16[6,192,128]{2,1,0:T(8,128)(2,1)S(1)} %get-tuple-element.16), channel_id=1, source_target_pairs={{0,2},{1,3},{2,0},{3,1},{4,6},{5,7},{6,4},{7,5},{8,10},{9,11},{10,... | collective-permute-start | bytes 884744 | tf_op jit(solution)/shard_map/ppermute | solution.py:407
  15.8 0.0 collective-permute-done.6.refs_2_
  15.8 1.6 %collective-permute-start.7 = (bf16[6,192,128]{2,1,0:T(8,128)(2,1)S(1)}, bf16[6,192,128]{2,1,0:T(8,128)(2,1)S(1)}, u32[]{:S(2)}, u32[]{:S(2)}) collective-permute-start(bf16[6,192,128]{2,1,0:T(8,128)(2,1)S(1)} %collective-permute-done.6.refs_2_), channel_id=1, source_target_pairs={{0,8},{4,28},{8,16},{12,4},{16,24},{20,12},{24,0},{28,20},{1,9},{5... | collective-permute-start | bytes 884744 | tf_op jit(solution)/shard_map/ppermute | solution.py:413
  17.4 4.0 %collective-permute-done.3.refs_2_ = bf16[6,192,128]{2,1,0:T(8,128)(2,1)S(1)} collective-permute-done((bf16[6,192,128]{2,1,0:T(8,128)(2,1)S(1)}, bf16[6,192,128]{2,1,0:T(8,128)(2,1)S(1)}, u32[]{:S(2)}, u32[]{:S(2)}) %collective-permute-start.3) | collective-permute-done | bytes 294944 | tf_op jit(solution)/shard_map/ppermute | solution.py:412
  21.4 1.6 %collective-permute-start.5 = (bf16[6,192,128]{2,1,0:T(8,128)(2,1)S(1)}, bf16[6,192,128]{2,1,0:T(8,128)(2,1)S(1)}, u32[]{:S(2)}, u32[]{:S(2)}) collective-permute-start(bf16[6,192,128]{2,1,0:T(8,128)(2,1)S(1)} %collective-permute-done.3.refs_2_), channel_id=1, source_target_pairs={{0,8},{4,28},{8,16},{12,4},{16,24},{20,12},{24,0},{28,20},{1,9},{5... | collective-permute-start | bytes 884744 | tf_op jit(solution)/shard_map/ppermute | solution.py:414
  23.0 0.0 collective-permute-done.2.refs_1_
  23.0 3.5 %collective-permute-start.4 = (bf16[6,192,128]{2,1,0:T(8,128)(2,1)S(1)}, bf16[6,192,128]{2,1,0:T(8,128)(2,1)S(1)}, u32[]{:S(2)}, u32[]{:S(2)}) collective-permute-start(bf16[6,192,128]{2,1,0:T(8,128)(2,1)S(1)} %collective-permute-done.2.refs_1_), channel_id=1, source_target_pairs={{0,4},{4,0},{8,12},{12,8},{16,20},{20,16},{24,28},{28,24},{1,5},{5... | collective-permute-start | bytes 884744 | tf_op jit(solution)/shard_map/ppermute | solution.py:412
  26.6 0.0 collective-permute-done.7.refs_4_
  26.6 1.5 %collective-permute-start.8 = (bf16[6,192,128]{2,1,0:T(8,128)(2,1)S(1)}, bf16[6,192,128]{2,1,0:T(8,128)(2,1)S(1)}, u32[]{:S(2)}, u32[]{:S(2)}) collective-permute-start(bf16[6,192,128]{2,1,0:T(8,128)(2,1)S(1)} %collective-permute-done.7.refs_4_), channel_id=1, source_target_pairs={{0,2},{1,3},{2,0},{3,1},{4,6},{5,7},{6,4},{7,5},{8,10},{9,11},{10,... | collective-permute-start | bytes 884744 | tf_op jit(solution)/shard_map/ppermute | solution.py:414
  28.1 0.0 collective-permute-done.tiles
  28.1 1.6 %squares.3.second.refs_1_.second_held = bf16[3,27,96,384]{3,2,1,0:T(8,128)(2,1)S(1)} custom-call(bf16[3,27,36864]{2,1,0:T(8,128)(2,1)S(1)} %collective-permute-done.tiles), custom_call_target="tpu_custom_call" | custom-call | flops 1 | bytes 18000000 | tf_op jit(solution)/shard_map/squares/pallas_call | solution.py:114
  29.7 0.0 copy-start.1
  29.7 2.4 %collective-permute-done.5.refs_4_ = bf16[6,192,128]{2,1,0:T(8,128)(2,1)S(1)} collective-permute-done((bf16[6,192,128]{2,1,0:T(8,128)(2,1)S(1)}, bf16[6,192,128]{2,1,0:T(8,128)(2,1)S(1)}, u32[]{:S(2)}, u32[]{:S(2)}) %collective-permute-start.5) | collective-permute-done | bytes 294944 | tf_op jit(solution)/shard_map/ppermute | solution.py:414
  32.1 0.5 collective-permute-start.10
  32.6 0.7 %collective-permute-start.9 = (bf16[6,192,128]{2,1,0:T(8,128)(2,1)S(1)}, bf16[6,192,128]{2,1,0:T(8,128)(2,1)S(1)}, u32[]{:S(2)}, u32[]{:S(2)}) collective-permute-start(bf16[6,192,128]{2,1,0:T(8,128)(2,1)S(1)} %gate.4), channel_id=1, source_target_pairs={{0,4},{4,0},{8,12},{12,8},{16,20},{20,16},{24,28},{28,24},{1,5},{5... | collective-permute-start | bytes 884744 | tf_op jit(solution)/shard_map/ppermute | solution.py:415
  33.3 0.0 collective-permute-done.4.refs_3_
  33.3 0.6 collective-permute-done.8.refs_5_
  33.9 0.0 copy-done
  33.9 6.6 %other_images.1.refs_0_ = s16[1168,128]{1,0:T(8,128)(2,1)} custom-call(s32[8,128]{1,0:T(8,128)S(4)} %meets.1.refs_2_.table, bf16[3,27,96,384]{3,2,1,0:T(8,128)(2,1)S(1)} %squares.2.refs_1_.first.first_held, bf16[3,27,96,384]{3,2,1,0:T(8,128)(2,1)S(1)} %squares.3.second.refs_1_.second_held, bf16[6,192,128]{2,1,0:T(8,128)(2,1)S(1)} %collective-permute-done.1.refs_0_, ...), custom_call_target="tpu_custom_call" | custom-call | flops 1 | bytes 1000000000 | tf_op jit(solution)/shard_map/other_images/pallas_call | solution.py:217
  40.6 0.0 copy-done.1
  40.6 0.0 collective-permute-done.10.refs_2_.refs_3_
  40.6 0.0 collective-permute-done.9.refs_1_
  40.6 2.5 %collective-permute-start.11 = (s16[1168,128]{1,0:T(8,128)(2,1)}, s16[1168,128]{1,0:T(8,128)(2,1)S(1)}, u32[]{:S(2)}, u32[]{:S(2)}) collective-permute-start(s16[1168,128]{1,0:T(8,128)(2,1)} %gate.5.refs_8_), channel_id=1, source_target_pairs={{0,2},{1,3},{2,0},{3,1},{4,6},{5,7},{6,4},{7,5},{8,10},{9,11},{10,... | collective-permute-start | bytes 897032 | tf_op jit(solution)/shard_map/ppermute | solution.py:420
  43.2 8.8 %own_rows.1 = (f32[12,192,128]{2,1,0:T(8,128)}, f32[16,128]{1,0:T(8,128)S(1)}, f32[6,192,128]{2,1,0:T(8,128)S(1)}, f32[6,192,128]{2,1,0:T(8,128)S(1)}, bf16[6,192,128]{2,1,0:T(8,128)(2,1)S(1)}) custom-call(s32[8,128]{1,0:T(8,128)S(4)} %meets.1.refs_2_.table, bf16[3,27,96,384]{3,2,1,0:T(8,128)(2,1)} %copy-done, bf16[3,27,96,384]{3,2,1,0:T(8,128)(2,1)} %copy-done.1, ...), custom_call_target="tpu_custom_call" | custom-call | flops 1 | bytes 1000000000 | tf_op jit(solution)/shard_map/own_rows/pallas_call | solution.py:299
  52.0 0.0 collective-permute-done.11.coded
  52.0 0.9 %other_rows.1 = (f32[12,192,128]{2,1,0:T(8,128)}, f32[2,128]{1,0:T(2,128)S(1)}) custom-call(s16[1168,128]{1,0:T(8,128)(2,1)S(1)} %collective-permute-done.11.coded, f32[6,192,128]{2,1,0:T(8,128)S(1)} %get-tuple-element.9.prev, f32[6,192,128]{2,1,0:T(8,128)S(1)} %get-tuple-element.10.probes, ...), custom_call_target="tpu_custom_call", output_to_operand_aliasing={{0}: (5, {})} | custom-call | flops 1 | bytes 1 | tf_op jit(solution)/shard_map/other_rows/pallas_call | solution.py:348
  53.0 1.0 %collective-permute-start.12 = (f32[2,128]{1,0:T(2,128)S(1)}, f32[2,128]{1,0:T(2,128)S(1)}, u32[]{:S(2)}, u32[]{:S(2)}) collective-permute-start(f32[2,128]{1,0:T(2,128)S(1)} %get-tuple-element.15), channel_id=1, source_target_pairs={{0,4},{4,0},{8,12},{12,8},{16,20},{20,16},{24,28},{28,24},{1,5},{5... | collective-permute-start | bytes 3080 | tf_op jit(solution)/shard_map/ppermute | solution.py:383
  53.9 2.7 %collective-permute-done.12 = f32[2,128]{1,0:T(2,128)S(1)} collective-permute-done((f32[2,128]{1,0:T(2,128)S(1)}, f32[2,128]{1,0:T(2,128)S(1)}, u32[]{:S(2)}, u32[]{:S(2)}) %collective-permute-start.12) | collective-permute-done | bytes 1056 | tf_op jit(solution)/shard_map/ppermute | solution.py:383
  56.6 0.0 collective-permute-start.13
  56.6 3.6 %collective-permute-done.13 = f32[2,128]{1,0:T(2,128)S(1)} collective-permute-done((f32[2,128]{1,0:T(2,128)S(1)}, f32[2,128]{1,0:T(2,128)S(1)}, u32[]{:S(2)}, u32[]{:S(2)}) %collective-permute-start.13) | collective-permute-done | bytes 1056 | tf_op jit(solution)/shard_map/ppermute | solution.py:383
  60.2 0.3 collective-permute-start.14
  60.5 4.2 %collective-permute-done.14 = f32[2,128]{1,0:T(2,128)S(1)} collective-permute-done((f32[2,128]{1,0:T(2,128)S(1)}, f32[2,128]{1,0:T(2,128)S(1)}, u32[]{:S(2)}, u32[]{:S(2)}) %collective-permute-start.14) | collective-permute-done | bytes 1056 | tf_op jit(solution)/shard_map/ppermute | solution.py:383
  64.7 0.6 add.11
  (6 shorter events, 0.0 us)
Async XLA Ops:
  0.6 27.4 %collective-permute-start = (bf16[3,27,36864]{2,1,0:T(8,128)(2,1)}, bf16[3,27,36864]{2,1,0:T(8,128)(2,1)S(1)}, u32[]{:S(2)}, u32[]{:S(2)}) collective-permute-start(bf16[3,27,36864]{2,1,0:T(8,128)(2,1)} %tiles.1), channel_id=1, source_target_pairs={{0,1},{1,0},{2,3},{3,2},{4,5},{5,4},{6,7},{7,6},{8,9},{9,8},{10,11... | collective-permute-start | bytes 17915912 | tf_op jit(solution)/shard_map/ppermute | solution.py:406
  2.2 10.2 %collective-permute-start.1 = (bf16[6,192,128]{2,1,0:T(8,128)(2,1)S(1)}, bf16[6,192,128]{2,1,0:T(8,128)(2,1)S(1)}, u32[]{:S(2)}, u32[]{:S(2)}) collective-permute-start(bf16[6,192,128]{2,1,0:T(8,128)(2,1)S(1)} %get-tuple-element.17.refs_0_), channel_id=1, source_target_pairs={{0,2},{1,3},{2,0},{3,1},{4,6},{5,7},{6,4},{7,5},{8,10},{9,11},{10,... | collective-permute-start | bytes 884744 | tf_op jit(solution)/shard_map/ppermute | solution.py:407
  4.8 4.8 %copy-start.2 = (s32[12,27]{1,0:T(8,128)S(1)}, s32[12,27]{1,0:T(8,128)}, u32[]{:S(2)}) copy-start(s32[12,27]{1,0:T(8,128)} %neighbours.1) | copy-start | bytes 3892
  4.8 11.0 %collective-permute-start.6 = (bf16[6,192,128]{2,1,0:T(8,128)(2,1)S(1)}, bf16[6,192,128]{2,1,0:T(8,128)(2,1)S(1)}, u32[]{:S(2)}, u32[]{:S(2)}) collective-permute-start(bf16[6,192,128]{2,1,0:T(8,128)(2,1)S(1)} %get-tuple-element.16), channel_id=1, source_target_pairs={{0,4},{4,0},{8,12},{12,8},{16,20},{20,16},{24,28},{28,24},{1,5},{5... | collective-permute-start | bytes 884744 | tf_op jit(solution)/shard_map/ppermute | solution.py:408
  9.6 24.3 %copy-start = (bf16[3,27,96,384]{3,2,1,0:T(8,128)(2,1)}, bf16[3,27,96,384]{3,2,1,0:T(8,128)(2,1)S(1)}, u32[]{:S(2)}) copy-start(bf16[3,27,96,384]{3,2,1,0:T(8,128)(2,1)S(1)} %squares.2.refs_1_.first.first_held) | copy-start | bytes 17915908
  12.5 8.9 %collective-permute-start.3 = (bf16[6,192,128]{2,1,0:T(8,128)(2,1)S(1)}, bf16[6,192,128]{2,1,0:T(8,128)(2,1)S(1)}, u32[]{:S(2)}, u32[]{:S(2)}) collective-permute-start(bf16[6,192,128]{2,1,0:T(8,128)(2,1)S(1)} %gate.3), channel_id=1, source_target_pairs={{0,4},{4,0},{8,12},{12,8},{16,20},{20,16},{24,28},{28,24},{1,5},{5... | collective-permute-start | bytes 884744 | tf_op jit(solution)/shard_map/ppermute | solution.py:412
  14.3 8.7 %collective-permute-start.2 = (bf16[6,192,128]{2,1,0:T(8,128)(2,1)S(1)}, bf16[6,192,128]{2,1,0:T(8,128)(2,1)S(1)}, u32[]{:S(2)}, u32[]{:S(2)}) collective-permute-start(bf16[6,192,128]{2,1,0:T(8,128)(2,1)S(1)} %get-tuple-element.16), channel_id=1, source_target_pairs={{0,2},{1,3},{2,0},{3,1},{4,6},{5,7},{6,4},{7,5},{8,10},{9,11},{10,... | collective-permute-start | bytes 884744 | tf_op jit(solution)/shard_map/ppermute | solution.py:407
  15.8 10.8 %collective-permute-start.7 = (bf16[6,192,128]{2,1,0:T(8,128)(2,1)S(1)}, bf16[6,192,128]{2,1,0:T(8,128)(2,1)S(1)}, u32[]{:S(2)}, u32[]{:S(2)}) collective-permute-start(bf16[6,192,128]{2,1,0:T(8,128)(2,1)S(1)} %collective-permute-done.6.refs_2_), channel_id=1, source_target_pairs={{0,8},{4,28},{8,16},{12,4},{16,24},{20,12},{24,0},{28,20},{1,9},{5... | collective-permute-start | bytes 884744 | tf_op jit(solution)/shard_map/ppermute | solution.py:413
  21.4 10.7 %collective-permute-start.5 = (bf16[6,192,128]{2,1,0:T(8,128)(2,1)S(1)}, bf16[6,192,128]{2,1,0:T(8,128)(2,1)S(1)}, u32[]{:S(2)}, u32[]{:S(2)}) collective-permute-start(bf16[6,192,128]{2,1,0:T(8,128)(2,1)S(1)} %collective-permute-done.3.refs_2_), channel_id=1, source_target_pairs={{0,8},{4,28},{8,16},{12,4},{16,24},{20,12},{24,0},{28,20},{1,9},{5... | collective-permute-start | bytes 884744 | tf_op jit(solution)/shard_map/ppermute | solution.py:414
  23.0 10.3 %collective-permute-start.4 = (bf16[6,192,128]{2,1,0:T(8,128)(2,1)S(1)}, bf16[6,192,128]{2,1,0:T(8,128)(2,1)S(1)}, u32[]{:S(2)}, u32[]{:S(2)}) collective-permute-start(bf16[6,192,128]{2,1,0:T(8,128)(2,1)S(1)} %collective-permute-done.2.refs_1_), channel_id=1, source_target_pairs={{0,4},{4,0},{8,12},{12,8},{16,20},{20,16},{24,28},{28,24},{1,5},{5... | collective-permute-start | bytes 884744 | tf_op jit(solution)/shard_map/ppermute | solution.py:412
  26.6 7.3 %collective-permute-start.8 = (bf16[6,192,128]{2,1,0:T(8,128)(2,1)S(1)}, bf16[6,192,128]{2,1,0:T(8,128)(2,1)S(1)}, u32[]{:S(2)}, u32[]{:S(2)}) collective-permute-start(bf16[6,192,128]{2,1,0:T(8,128)(2,1)S(1)} %collective-permute-done.7.refs_4_), channel_id=1, source_target_pairs={{0,2},{1,3},{2,0},{3,1},{4,6},{5,7},{6,4},{7,5},{8,10},{9,11},{10,... | collective-permute-start | bytes 884744 | tf_op jit(solution)/shard_map/ppermute | solution.py:414
  29.7 10.9 %copy-start.1 = (bf16[3,27,96,384]{3,2,1,0:T(8,128)(2,1)}, bf16[3,27,96,384]{3,2,1,0:T(8,128)(2,1)S(1)}, u32[]{:S(2)}) copy-start(bf16[3,27,96,384]{3,2,1,0:T(8,128)(2,1)S(1)} %squares.3.second.refs_1_.second_held) | copy-start | bytes 17915908
  32.1 8.5 %collective-permute-start.10 = (bf16[6,192,128]{2,1,0:T(8,128)(2,1)S(1)}, bf16[6,192,128]{2,1,0:T(8,128)(2,1)S(1)}, u32[]{:S(2)}, u32[]{:S(2)}) collective-permute-start(bf16[6,192,128]{2,1,0:T(8,128)(2,1)S(1)} %collective-permute-done.5.refs_4_), channel_id=1, source_target_pairs={{0,2},{1,3},{2,0},{3,1},{4,6},{5,7},{6,4},{7,5},{8,10},{9,11},{10,... | collective-permute-start | bytes 884744 | tf_op jit(solution)/shard_map/ppermute | solution.py:416
  32.6 8.0 %collective-permute-start.9 = (bf16[6,192,128]{2,1,0:T(8,128)(2,1)S(1)}, bf16[6,192,128]{2,1,0:T(8,128)(2,1)S(1)}, u32[]{:S(2)}, u32[]{:S(2)}) collective-permute-start(bf16[6,192,128]{2,1,0:T(8,128)(2,1)S(1)} %gate.4), channel_id=1, source_target_pairs={{0,4},{4,0},{8,12},{12,8},{16,20},{20,16},{24,28},{28,24},{1,5},{5... | collective-permute-start | bytes 884744 | tf_op jit(solution)/shard_map/ppermute | solution.py:415
  40.6 11.4 %collective-permute-start.11 = (s16[1168,128]{1,0:T(8,128)(2,1)}, s16[1168,128]{1,0:T(8,128)(2,1)S(1)}, u32[]{:S(2)}, u32[]{:S(2)}) collective-permute-start(s16[1168,128]{1,0:T(8,128)(2,1)} %gate.5.refs_8_), channel_id=1, source_target_pairs={{0,2},{1,3},{2,0},{3,1},{4,6},{5,7},{6,4},{7,5},{8,10},{9,11},{10,... | collective-permute-start | bytes 897032 | tf_op jit(solution)/shard_map/ppermute | solution.py:420
  53.0 3.6 %collective-permute-start.12 = (f32[2,128]{1,0:T(2,128)S(1)}, f32[2,128]{1,0:T(2,128)S(1)}, u32[]{:S(2)}, u32[]{:S(2)}) collective-permute-start(f32[2,128]{1,0:T(2,128)S(1)} %get-tuple-element.15), channel_id=1, source_target_pairs={{0,4},{4,0},{8,12},{12,8},{16,20},{20,16},{24,28},{28,24},{1,5},{5... | collective-permute-start | bytes 3080 | tf_op jit(solution)/shard_map/ppermute | solution.py:383
  56.6 3.6 %collective-permute-start.13 = (f32[2,128]{1,0:T(2,128)S(1)}, f32[2,128]{1,0:T(2,128)S(1)}, u32[]{:S(2)}, u32[]{:S(2)}) collective-permute-start(f32[2,128]{1,0:T(2,128)S(1)} %add.9), channel_id=1, source_target_pairs={{0,8},{4,12},{8,0},{12,4},{16,24},{20,28},{24,16},{28,20},{1,9},{5... | collective-permute-start | bytes 3080 | tf_op jit(solution)/shard_map/ppermute | solution.py:383
  60.2 4.5 %collective-permute-start.14 = (f32[2,128]{1,0:T(2,128)S(1)}, f32[2,128]{1,0:T(2,128)S(1)}, u32[]{:S(2)}, u32[]{:S(2)}) collective-permute-start(f32[2,128]{1,0:T(2,128)S(1)} %add.10), channel_id=1, source_target_pairs={{0,16},{4,20},{8,24},{12,28},{16,0},{20,4},{24,8},{28,12},{1,17},{... | collective-permute-start | bytes 3080 | tf_op jit(solution)/shard_map/ppermute | solution.py:383

commit v4 on v3

--- a/solution.py
+++ b/solution.py
@@ -10,6 +10,7 @@
 
 GRANT = 20 * 1024 * 1024
 BLOCKS = 6
+TABLE = 8
 PAD = 64
 LEVELS = 32760.0
 LIGHT = pl.CostEstimate(flops=1, bytes_accessed=1, transcendentals=0)
@@ -44,7 +45,7 @@
     return made
 
 
-def meets_kernel(neighbours, out, table, sem):
+def order_kernel(neighbours, out, table, sem):
     blocks, neigh = neighbours.shape
     slab, lane = lax.axis_index("slab"), lax.axis_index("grp")
     per = BLOCKS // 2
@@ -52,23 +53,41 @@
     for side, first in enumerate((lane * per, (lane ^ 1) * per)):
         for n in range(per):
             table[pl.ds(side * per + n, 1), :neigh] = neighbours[pl.ds(first + n, 1), :]
-    mine = table[...]
+    mine = table[:TABLE, :]
     owner = mine // blocks
+    spot = lax.broadcasted_iota(jnp.int32, mine.shape, 1)
     kind = jnp.where(owner == slab, 0, jnp.where(owner == (slab ^ 1), 1, 2))
-    table[...] = kind * blocks + mine - owner * blocks
+    kind = jnp.where(spot < neigh, kind, 3)
+    near = kind * blocks + mine - owner * blocks
+    key = kind * 128 + spot
+    slot = jnp.zeros_like(mine)
+    for k in range(neigh):
+        slot += (key[:, k : k + 1] < key).astype(jnp.int32)
+    order = found = jnp.zeros_like(mine)
+    for k in range(neigh):
+        here = spot == k
+        hit = slot == k
+        order = jnp.where(here, jnp.sum(jnp.where(hit, spot, 0), axis=1, keepdims=True), order)
+        found = jnp.where(here, jnp.sum(jnp.where(hit, near, 0), axis=1, keepdims=True), found)
+    own = found < blocks
+    count = jnp.sum((kind == 0).astype(jnp.int32), axis=1, keepdims=True)
+    table[:TABLE, :] = order
+    table[TABLE : 2 * TABLE, :] = jnp.where(own, found, blocks)
+    table[2 * TABLE : 3 * TABLE, :] = jnp.where(own, 2 * blocks, found - blocks)
+    table[3 * TABLE :, :] = jnp.broadcast_to(count, mine.shape)
     copy(table, out, sem).wait()
 
 
-def meets(neighbours):
-    return pl.pallas_call(
-        meets_kernel,
+def ordered(neighbours):
+    return pl.pallas_call(
+        order_kernel,
         in_specs=[VMEM],
         out_specs=SMEM,
-        out_shape=pltpu.SMEM((8, 128), jnp.int32),
-        scratch_shapes=[pltpu.VMEM((8, 128), jnp.int32), DMA],
+        out_shape=pltpu.SMEM((4 * TABLE, 128), jnp.int32),
+        scratch_shapes=[pltpu.VMEM((4 * TABLE, 128), jnp.int32), DMA],
         compiler_params=params(),
         cost_estimate=LIGHT,
-        name="meets",
+        name="ordered",
     )(neighbours)
 
 
@@ -123,22 +142,27 @@
     )(*(in_vmem([tiles]) if resident else in_hbm([tiles])))
 
 
-def start_near(chunks, near, sems):
-    copies, at = [], 0
-    for n, chunk in enumerate(chunks):
-        copies.append(copy(chunk, near.at[pl.ds(at, chunk.shape[0])], sems.at[n]))
-        at += chunk.shape[0]
+def start_near(sides, near, sems):
+    copies = []
+    cols = near.shape[2] // len(sides)
+    for side, chunks in enumerate(sides):
+        at = 0
+        for chunk in chunks:
+            spot = near.at[pl.ds(at, chunk.shape[0]), :, pl.ds(side * cols, cols)]
+            copies.append(copy(chunk, spot, sems.at[len(copies)]))
+            at += chunk.shape[0]
+    near[near.shape[0] - 1] = jnp.zeros(near.shape[1:], near.dtype)
     return copies
 
 
-def multiply(tiles, table, row, near):
-    count, half, wide = tiles.shape
+def multiply(tiles, table, b, part, first, count, near):
+    half, wide = tiles.shape[1:]
     rows = wide // 2
     lane = lax.broadcasted_iota(jnp.int32, (half, 128), 1)
     even = odd = None
-    for k in range(count):
-        vec = near[table[row, k]]
-        tile = tiles[k]
+    for k in range(first, first + count):
+        vec = near[table[part * TABLE + b, k]]
+        tile = tiles[table[b, k]]
         mid = tile[:, 128:256]
         none = jnp.zeros_like(mid)
         left = jnp.concatenate([tile[:, :128], jnp.where(lane < PAD, mid, none)], axis=1)
@@ -164,36 +188,99 @@
         first += square.shape[0]
 
 
+def any_block(needed):
+    found = needed(0)
+    for b in range(1, BLOCKS):
+        found |= needed(b)
+    return found
+
+
 def place(b):
     per = BLOCKS // 2
     core = lax.axis_index("grp") % 2
     return jnp.where(b < per, core * per + b, (1 - core) * per + b - per)
 
 
-def near_scratch(chunks):
-    return pltpu.VMEM((sum(c.shape[0] for c in chunks),) + chunks[0].shape[1:], chunks[0].dtype)
+def near_scratch(chunks, sides):
+    rows, cols = chunks[0].shape[1:]
+    return pltpu.VMEM((sum(c.shape[0] for c in chunks) + 1, rows, sides * cols), chunks[0].dtype)
+
+
+def slab_kernel(n_other, table, first, second, own, *refs):
+    other = refs[:n_other]
+    acc, near, near_sems = refs[-3:]
+    held = (first, second)
+    for load in start_near(([own], other), near, near_sems):
+        load.wait()
+
+    def body(b, tiles):
+        acc[b, 0], acc[b, 1] = multiply(tiles, table, b, 1, 0, 9, near)
+
+    each_block(held, body)
+    for group in range(1, 3):
+        more = lambda b: table[3 * TABLE + b, 0] > 9 * group
+
+        @pl.when(any_block(more))
+        def _():
+            def spread(b, tiles):
+                @pl.when(more(b))
+                def _():
+                    even, odd = multiply(tiles, table, b, 1, 9 * group, 9, near)
+                    acc[b, 0] += even
+                    acc[b, 1] += odd
+
+            each_block(held, spread)
+
+
+def own_slab(table, held, own, other):
+    cols = own.shape[2]
+    return pl.pallas_call(
+        functools.partial(slab_kernel, len(other)),
+        in_specs=[SMEM] + [VMEM] * 2 + [ANY] * (1 + len(other)),
+        out_specs=VMEM,
+        out_shape=pltpu.VMEM((BLOCKS, 2, held[0].shape[2], 2 * cols), jnp.float32),
+        scratch_shapes=[near_scratch([own], 2), DMA((1 + len(other),))],
+        compiler_params=params(),
+        cost_estimate=LIGHT,
+        name="own_slab",
+    )(in_smem(table), *in_vmem(held), own, *other)
 
 
 def largest(power, size):
     return size * jnp.exp2(power - 14.0)
 
 
-def other_kernel(n_chunks, table, first, second, *refs):
+def few(table):
+    return lambda b: table[3 * TABLE + b, 0] < 9
+
+
+def other_kernel(n_chunks, table, acc, first, second, *refs):
     chunks = refs[:n_chunks]
-    out, near, image, coded, scales, near_sems, out_sems = refs[-7:]
-    half, rows = first.shape[2], image.shape[0]
+    out, near, total, image, scales, near_sems = refs[-6:]
+    half, rows, cols = first.shape[2], image.shape[0], image.shape[1]
     scales[...] = jnp.zeros_like(scales)
-    for load in start_near(chunks, near, near_sems):
+    loads = start_near((chunks,), near, near_sems)
+    for n in range(2):
+        for b in range(BLOCKS):
+            total[b, n] = acc[b, n, :, cols:]
+    for load in loads:
         load.wait()
 
-    def send(b):
-        rows_out = out.at[pl.ds(pl.multiple_of(place(b) * rows, rows), rows)]
-        return pltpu.make_async_copy(coded.at[b], rows_out, out_sems.at[b])
+    @pl.when(any_block(few(table)))
+    def _():
+        def spread(b, tiles):
+            @pl.when(few(table)(b))
+            def _():
+                even, odd = multiply(tiles, table, b, 2, 0, 9, near)
+                total[b, 0] += even
+                total[b, 1] += odd
+
+        each_block((first, second), spread)
 
     def body(b, tiles):
-        even, odd = multiply(tiles, table, b, near)
-        image[pl.ds(0, half, 2), :] = even
-        image[pl.ds(1, half, 2), :] = odd
+        even, odd = multiply(tiles, table, b, 2, 9, 18, near)
+        image[pl.ds(0, half, 2), :] = total[b, 0] + even
+        image[pl.ds(1, half, 2), :] = total[b, 1] + odd
         value = image[...]
         top = jnp.maximum(jnp.max(jnp.abs(value), axis=0, keepdims=True), 1e-30)
         power = jnp.ceil(jnp.log2(top))
@@ -201,36 +288,31 @@
         scales[pl.ds(place(b), 1), :] = power
         scales[pl.ds(8 + place(b), 1), :] = size
         value = jnp.round(value * (LEVELS / largest(power, size)))
-        coded[b] = value.astype(jnp.int32).astype(jnp.int16)
-        send(b).start()
+        rows_out = pl.ds(pl.multiple_of(place(b) * rows, rows), rows)
+        out[rows_out, :] = value.astype(jnp.int32).astype(jnp.int16)
 
     each_block((first, second), body)
-    coded[BLOCKS, :16, :] = scales[...].astype(jnp.int32).astype(jnp.int16)
-    last = copy(coded.at[BLOCKS, pl.ds(0, 16)], out.at[pl.ds(BLOCKS * rows, 16)], out_sems.at[BLOCKS])
-    for b in range(BLOCKS):
-        send(b).wait()
-    last.wait()
-
-
-def other_images(table, held, chunks, after):
+    out[pl.ds(BLOCKS * rows, 16), :] = scales[...].astype(jnp.int32).astype(jnp.int16)
+
+
+def other_images(table, acc, held, chunks, after):
     rows, cols = chunks[0].shape[1:]
     return pl.pallas_call(
         functools.partial(other_kernel, len(chunks)),
-        in_specs=[SMEM] + [VMEM] * 2 + [ANY] * (len(chunks) + len(after)),
-        out_specs=HBM,
-        out_shape=pltpu.HBM((BLOCKS * rows + 16, cols), jnp.int16),
+        in_specs=[SMEM] + [VMEM] * 3 + [ANY] * (len(chunks) + len(after)),
+        out_specs=VMEM,
+        out_shape=pltpu.VMEM((BLOCKS * rows + 16, cols), jnp.int16),
         scratch_shapes=[
-            near_scratch(chunks),
+            near_scratch(chunks, 1),
+            pltpu.VMEM((BLOCKS, 2, rows // 2, cols), jnp.float32),
             pltpu.VMEM((rows, cols), jnp.float32),
-            pltpu.VMEM((BLOCKS + 1, rows, cols), jnp.int16),
             pltpu.VMEM((16, cols), jnp.float32),
             DMA((len(chunks),)),
-            DMA((BLOCKS + 1,)),
         ],
         compiler_params=params(),
         cost_estimate=LONG,
         name="other_images",
-    )(in_smem(table), *in_vmem(held), *chunks, *after)
+    )(in_smem(table), *in_vmem([acc, *held]), *chunks, *after)
 
 
 def add_sums(factor, value, probes, cur, sums):
@@ -239,25 +321,13 @@
         sums[pl.ds(8 * n, 8), :] += part
 
 
-def own_kernel(n_chunks, factor, table, first_held, second_held, *refs):
+def own_kernel(n_chunks, factor, table, acc, first_held, second_held, *refs):
     chunks, rows_in = refs[:n_chunks], refs[n_chunks : n_chunks + 3]
     out, sums, *later = refs[n_chunks + 4 : n_chunks + 9]
-    near, held, image, prev, probes, cur, near_sems, held_sems, row_sems, later_sems, out_sems = refs[-11:]
+    near, image, prev, probes, cur, near_sems, row_sems, later_sems, out_sems = refs[-9:]
     half = first_held.shape[2]
-    loads = start_near(chunks, near, near_sems)
-    slots = held.shape[0]
-
-    def load(n, square):
-        return pltpu.make_async_copy(square, held.at[n % slots], held_sems.at[n % slots])
-
-    def load_next(n):
-        count = first_held.shape[0]
-        pl.when(n < count)(lambda: load(n, first_held.at[jnp.minimum(n, count - 1)]).start())
-        more = (n >= count) & (n < BLOCKS)
-        pl.when(more)(lambda: load(n, second_held.at[jnp.clip(n - count, 0, BLOCKS - count - 1)]).start())
-
-    for n in range(slots - 1):
-        load_next(n)
+    loads = start_near((chunks,), near, near_sems)
+    cols = image.shape[2]
     first = (lax.axis_index("grp") // 2) * BLOCKS
     mine = []
     for n, (src, dst) in enumerate(zip(rows_in, (prev, probes, cur))):
@@ -266,12 +336,17 @@
     for made in loads:
         made.wait()
 
-    @pl.loop(0, BLOCKS)
-    def _(b):
-        load_next(b + slots - 1)
-        load(b, first_held.at[0]).wait()
+    def body(b, tiles):
         at = place(b)
-        even, odd = multiply(held.at[b % slots], table, b, near)
+        even, odd = multiply(tiles, table, b, 2, 9, 18, near)
+        image[b, pl.ds(0, half, 2), :] = acc[b, 0, :, :cols] + even
+        image[b, pl.ds(1, half, 2), :] = acc[b, 1, :, :cols] + odd
+
+        @pl.when(few(table)(b))
+        def _():
+            even, odd = multiply(tiles, table, b, 2, 0, 9, near)
+            image[b, pl.ds(0, half, 2), :] += even
+            image[b, pl.ds(1, half, 2), :] += odd
 
         @pl.when(b == 0)
         def _():
@@ -280,25 +355,24 @@
             for n, (src, dst) in enumerate(zip(rows_in, later)):
                 copy(src.at[pl.ds(BLOCKS - first, BLOCKS)], dst, later_sems.at[n])
 
-        image[b, pl.ds(0, half, 2), :] = even
-        image[b, pl.ds(1, half, 2), :] = odd
         value = 2.0 * image[b] - prev[at]
         image[b] = value
         copy(image.at[b], out.at[first + at], out_sems.at[b])
         add_sums(factor, value, probes[at], cur[at], sums)
 
+    each_block((first_held, second_held), body)
     for n, (src, dst) in enumerate(zip(rows_in, later)):
         pltpu.make_async_copy(src.at[pl.ds(BLOCKS - first, BLOCKS)], dst, later_sems.at[n]).wait()
     for b in range(BLOCKS):
         pltpu.make_async_copy(image.at[b], out.at[first + place(b)], out_sems.at[b]).wait()
 
 
-def own_rows(table, held, chunks, factor, prev, probes, cur, after):
+def own_rows(table, acc, held, chunks, factor, prev, probes, cur, after):
     rows, cols = cur.shape[1:]
     part = (BLOCKS, rows, cols)
     return pl.pallas_call(
         functools.partial(own_kernel, len(chunks), factor),
-        in_specs=[SMEM] + [HBM] * 2 + [ANY] * (len(chunks) + 3 + len(after)),
+        in_specs=[SMEM] + [VMEM] * 3 + [ANY] * (len(chunks) + 3 + len(after)),
         out_specs=[HBM] + [VMEM] * 4,
         out_shape=[
             pltpu.HBM(prev.shape, jnp.float32),
@@ -308,8 +382,7 @@
             pltpu.VMEM(part, cur.dtype),
         ],
         scratch_shapes=[
-            near_scratch(chunks),
-            pltpu.VMEM((3,) + held[0].shape[1:], held[0].dtype),
+            near_scratch(chunks, 1),
             pltpu.VMEM(part, jnp.float32),
             pltpu.VMEM(part, jnp.float32),
             pltpu.VMEM(part, jnp.float32),
@@ -317,13 +390,12 @@
             DMA((len(chunks),)),
             DMA((3,)),
             DMA((3,)),
-            DMA((3,)),
             DMA((BLOCKS,)),
         ],
         compiler_params=params(),
         cost_estimate=LONG,
         name="own_rows",
-    )(in_smem(table), *in_hbm(held), *chunks, prev, probes, cur, *after)
+    )(in_smem(table), *in_vmem([acc, *held]), *chunks, prev, probes, cur, *after)
 
 
 def final_kernel(factor, coded, prev, probes, cur, sums_in, _, out, sums, value, acc, sem):
@@ -406,20 +478,21 @@
     sib_tiles = sibling(tiles)
     oth = [across(low), across(high)]
     near_high = pair(high)
-    table = meets(neighbours)
-    held = [squares(tiles, rows, False)]
-    held.append(squares(sib_tiles, rows, True))
-    near_oth = [pair(gate(oth[0], held[0], table)), pair(oth[1])]
+    table = ordered(neighbours)
+    held = [squares(tiles, rows, False), squares(sib_tiles, rows, True)]
+    oth[0] = gate(oth[0], held[0], table)
+    near_oth = [pair(c) for c in oth]
     far_high = along(near_high)
     far_oth = [along(near_oth[0]), across(far_high)]
-    near_low = pair(gate(low, held[1]))
+    acc = own_slab(table, held, fixed, oth)
+    near_low = pair(gate(low, acc))
     far_low = across(far_oth[0])
 
-    images = other_images(table, held, [*oth, *near_oth, *far_oth], ())
+    images = other_images(table, acc, held, [*near_oth, *far_oth], ())
     images = gate(images, near_low, far_low)
     back = across(images)
-    own = [fixed, near_low, near_high, far_low, far_high]
-    t_next, sums, *later = own_rows(table, held, own, factor, t_prev, probes, fixed, in_hbm([images]))
+    own = [near_low, near_high, far_low, far_high]
+    t_next, sums, *later = own_rows(table, acc, held, own, factor, t_prev, probes, fixed, [images])
     t_next, sums = other_rows(factor, back, *later, t_next, sums)
     return (t_next, sum_over(sums, "slab"))
 

time: 65.4 us -> 62.4 us (0.954)
  starting transfers between devices: 21.2 us -> 18.6 us
    pallas_call x1 -> x2, Pallas kernels: 0.64 us -> 5.39 us  [the longest x1 4.24 us: own_slab(): pl.pallas_call(functools.partial(slab_kernel, len(other)), in_specs=[SMEM...]
    pallas_call x1, Pallas kernels: 8.83 us -> 5.77 us  [own_rows(): pl.pallas_call(functools.partial(own_kernel, len(chunks), factor), in_spe...]
    pallas_call x1, Pallas kernels: 6.65 us -> 4.53 us  [other_images(): pl.pallas_call(functools.partial(other_kernel, len(chunks)), in_specs=[SM...]
    ppermute x2, waiting for transfers between devices: 2.97 us -> 1.52 us  [shards(): far_oth = [along(near_oth[0]), across(far_high)]]
    ppermute x1, waiting for transfers between devices: 0.01 us -> 1.06 us  [shards(): far_low = across(far_oth[0])]
    ppermute x1, starting transfers between devices: 2.55 us -> 1.5 us  [shards(): back = across(images)]
    ppermute x3, waiting for transfers between devices: 10.4 us -> 11.3 us  [sum_over(): lax.ppermute(value, axis, [(i, i ^ hop) for i in range(size)])]
    ppermute x3, starting transfers between devices: 1.26 us -> 0.35 us  [sum_over(): lax.ppermute(value, axis, [(i, i ^ hop) for i in range(size)])]
  transfers between devices with their start and end apart: 15 -> 15, of which waited for: 7 -> 7; matrix products, arithmetic and copies ran while one was open for 2% -> 2% of each run, Pallas kernels for 32% -> 33%
where the time goes in v4:
time: 62.4 us; the launch traced here: 62.2 us
  Pallas kernels  21.5 us (34%)
  waiting for transfers between devices  19.6 us (31%)
  starting transfers between devices  18.6 us (30%)
  local copies, waits for them, and re-layouts  1.09 us (2%)
  between operations  0.74 us (1%)
    ppermute x3, waiting for transfers between devices, sum_over(): lax.ppermute(value, axis, [(i, i ^ hop) for i in range(size)])  11.3 us
    pallas_call x1, Pallas kernels, own_rows(): pl.pallas_call(functools.partial(own_kernel, len(chunks), factor), in_spe...  5.77 us
    ppermute x2, starting transfers between devices, shards(): near_oth = [pair(c) for c in oth]  5.31 us
    pallas_call x2, Pallas kernels, squares(): pl.pallas_call(held_kernel if resident else functools.partial(square_kern...  4.88 us
    pallas_call x1, Pallas kernels, other_images(): pl.pallas_call(functools.partial(other_kernel, len(chunks)), in_specs=[SM...  4.53 us
    pallas_call x1, Pallas kernels, own_slab(): pl.pallas_call(functools.partial(slab_kernel, len(other)), in_specs=[SMEM...  4.24 us
    ppermute x2, starting transfers between devices, shards(): oth = [across(low), across(high)]  4.06 us
    ppermute x2, waiting for transfers between devices, shards(): near_oth = [pair(c) for c in oth]  3.99 us
  transfers between devices with their start and end apart: 15, of which 7 were waited for; matrix products, arithmetic and copies ran while one was open for 2% of the time, Pallas kernels for 33%

profile of v4, /device:TPU:0, one launch (start us, length us, event | category | flops | bytes accessed | tf_op | source)
XLA Modules:
  0.0 62.2 jit_solution(8645035591447379785)
XLA Ops:
  0.6 0.5 collective-permute-start
  1.1 1.1 %fusion = (bf16[6,192,128]{2,1,0:T(8,128)(2,1)S(1)}, bf16[6,192,128]{2,1,0:T(8,128)(2,1)S(1)}) fusion(bf16[12,192,128]{2,1,0:T(8,128)(2,1)} %refs_6_.1), kind=kLoop, calls=%fused_computation | loop fusion | bytes 1179648 | tf_op jit(solution)/shard_map/slice | solution.py:476
  2.2 2.6 %collective-permute-start.1 = (bf16[6,192,128]{2,1,0:T(8,128)(2,1)S(1)}, bf16[6,192,128]{2,1,0:T(8,128)(2,1)S(1)}, u32[]{:S(2)}, u32[]{:S(2)}) collective-permute-start(bf16[6,192,128]{2,1,0:T(8,128)(2,1)S(1)} %get-tuple-element.17.refs_0_), channel_id=1, source_target_pairs={{0,2},{1,3},{2,0},{3,1},{4,6},{5,7},{6,4},{7,5},{8,10},{9,11},{10,... | collective-permute-start | bytes 884744 | tf_op jit(solution)/shard_map/ppermute | solution.py:479
  4.8 0.0 copy-start
  4.8 1.5 %collective-permute-start.6 = (bf16[6,192,128]{2,1,0:T(8,128)(2,1)S(1)}, bf16[6,192,128]{2,1,0:T(8,128)(2,1)S(1)}, u32[]{:S(2)}, u32[]{:S(2)}) collective-permute-start(bf16[6,192,128]{2,1,0:T(8,128)(2,1)S(1)} %get-tuple-element.16), channel_id=1, source_target_pairs={{0,4},{4,0},{8,12},{12,8},{16,20},{20,16},{24,28},{28,24},{1,5},{5... | collective-permute-start | bytes 884744 | tf_op jit(solution)/shard_map/ppermute | solution.py:480
  6.3 3.2 %squares.2.refs_1_.first.first_held = bf16[3,27,96,384]{3,2,1,0:T(8,128)(2,1)S(1)} custom-call(bf16[3,27,36864]{2,1,0:T(8,128)(2,1)} %tiles.1), custom_call_target="tpu_custom_call" | custom-call | flops 1 | bytes 18000000 | tf_op jit(solution)/shard_map/squares/pallas_call | solution.py:133
  9.6 0.0 copy-done
  9.6 1.1 %ordered.1.refs_2_.table = s32[32,128]{1,0:T(8,128)S(4)} custom-call(s32[12,27]{1,0:T(8,128)S(1)} %copy-done), custom_call_target="tpu_custom_call" | custom-call | flops 1 | bytes 1 | tf_op jit(solution)/shard_map/ordered/pallas_call | solution.py:82
  10.8 1.7 %collective-permute-done.1.refs_0_ = bf16[6,192,128]{2,1,0:T(8,128)(2,1)S(1)} collective-permute-done((bf16[6,192,128]{2,1,0:T(8,128)(2,1)S(1)}, bf16[6,192,128]{2,1,0:T(8,128)(2,1)S(1)}, u32[]{:S(2)}, u32[]{:S(2)}) %collective-permute-start.1) | collective-permute-done | bytes 294944 | tf_op jit(solution)/shard_map/ppermute | solution.py:479
  12.5 1.8 %collective-permute-start.3 = (bf16[6,192,128]{2,1,0:T(8,128)(2,1)S(1)}, bf16[6,192,128]{2,1,0:T(8,128)(2,1)S(1)}, u32[]{:S(2)}, u32[]{:S(2)}) collective-permute-start(bf16[6,192,128]{2,1,0:T(8,128)(2,1)S(1)} %gate.3.refs_0_), channel_id=1, source_target_pairs={{0,4},{4,0},{8,12},{12,8},{16,20},{20,16},{24,28},{28,24},{1,5},{5... | collective-permute-start | bytes 884744 | tf_op jit(solution)/shard_map/ppermute | solution.py:484
  14.2 1.5 %collective-permute-start.2 = (bf16[6,192,128]{2,1,0:T(8,128)(2,1)S(1)}, bf16[6,192,128]{2,1,0:T(8,128)(2,1)S(1)}, u32[]{:S(2)}, u32[]{:S(2)}) collective-permute-start(bf16[6,192,128]{2,1,0:T(8,128)(2,1)S(1)} %get-tuple-element.16), channel_id=1, source_target_pairs={{0,2},{1,3},{2,0},{3,1},{4,6},{5,7},{6,4},{7,5},{8,10},{9,11},{10,... | collective-permute-start | bytes 884744 | tf_op jit(solution)/shard_map/ppermute | solution.py:479
  15.7 0.0 collective-permute-done.6.refs_1_
  15.7 1.6 %collective-permute-start.7 = (bf16[6,192,128]{2,1,0:T(8,128)(2,1)S(1)}, bf16[6,192,128]{2,1,0:T(8,128)(2,1)S(1)}, u32[]{:S(2)}, u32[]{:S(2)}) collective-permute-start(bf16[6,192,128]{2,1,0:T(8,128)(2,1)S(1)} %collective-permute-done.6.refs_1_), channel_id=1, source_target_pairs={{0,8},{4,28},{8,16},{12,4},{16,24},{20,12},{24,0},{28,20},{1,9},{5... | collective-permute-start | bytes 884744 | tf_op jit(solution)/shard_map/ppermute | solution.py:485
  17.3 4.0 %collective-permute-done.3.refs_0_ = bf16[6,192,128]{2,1,0:T(8,128)(2,1)S(1)} collective-permute-done((bf16[6,192,128]{2,1,0:T(8,128)(2,1)S(1)}, bf16[6,192,128]{2,1,0:T(8,128)(2,1)S(1)}, u32[]{:S(2)}, u32[]{:S(2)}) %collective-permute-start.3) | collective-permute-done | bytes 294944 | tf_op jit(solution)/shard_map/ppermute | solution.py:484
  21.3 1.6 %collective-permute-start.5 = (bf16[6,192,128]{2,1,0:T(8,128)(2,1)S(1)}, bf16[6,192,128]{2,1,0:T(8,128)(2,1)S(1)}, u32[]{:S(2)}, u32[]{:S(2)}) collective-permute-start(bf16[6,192,128]{2,1,0:T(8,128)(2,1)S(1)} %collective-permute-done.3.refs_0_), channel_id=1, source_target_pairs={{0,8},{4,28},{8,16},{12,4},{16,24},{20,12},{24,0},{28,20},{1,9},{5... | collective-permute-start | bytes 884744 | tf_op jit(solution)/shard_map/ppermute | solution.py:486
  22.9 0.0 collective-permute-done.2.refs_1_
  22.9 3.5 %collective-permute-start.4 = (bf16[6,192,128]{2,1,0:T(8,128)(2,1)S(1)}, bf16[6,192,128]{2,1,0:T(8,128)(2,1)S(1)}, u32[]{:S(2)}, u32[]{:S(2)}) collective-permute-start(bf16[6,192,128]{2,1,0:T(8,128)(2,1)S(1)} %collective-permute-done.2.refs_1_), channel_id=1, source_target_pairs={{0,4},{4,0},{8,12},{12,8},{16,20},{20,16},{24,28},{28,24},{1,5},{5... | collective-permute-start | bytes 884744 | tf_op jit(solution)/shard_map/ppermute | solution.py:484
  26.5 0.0 collective-permute-done.tiles
  26.5 1.6 %squares.3.second.second_held = bf16[3,27,96,384]{3,2,1,0:T(8,128)(2,1)S(1)} custom-call(bf16[3,27,36864]{2,1,0:T(8,128)(2,1)S(1)} %collective-permute-done.tiles), custom_call_target="tpu_custom_call" | custom-call | flops 1 | bytes 18000000 | tf_op jit(solution)/shard_map/squares/pallas_call | solution.py:133
  28.1 0.0 collective-permute-done.7.refs_3_
  28.1 1.6 %collective-permute-start.8 = (bf16[6,192,128]{2,1,0:T(8,128)(2,1)S(1)}, bf16[6,192,128]{2,1,0:T(8,128)(2,1)S(1)}, u32[]{:S(2)}, u32[]{:S(2)}) collective-permute-start(bf16[6,192,128]{2,1,0:T(8,128)(2,1)S(1)} %collective-permute-done.7.refs_3_), channel_id=1, source_target_pairs={{0,2},{1,3},{2,0},{3,1},{4,6},{5,7},{6,4},{7,5},{8,10},{9,11},{10,... | collective-permute-start | bytes 884744 | tf_op jit(solution)/shard_map/ppermute | solution.py:486
  29.7 4.2 %own_slab.1.acc.refs_1_ = f32[6,2,96,256]{3,2,1,0:T(8,128)S(1)} custom-call(s32[32,128]{1,0:T(8,128)S(4)} %ordered.1.refs_2_.table, bf16[3,27,96,384]{3,2,1,0:T(8,128)(2,1)S(1)} %squares.2.refs_1_.first.first_held, bf16[3,27,96,384]{3,2,1,0:T(8,128)(2,1)S(1)} %squares.3.second.second_held, bf16[12,192,128]{2,1,0:T(8,128)(2,1)} %refs_6_.1, ...), custom_call_target="tpu_custom_call" | custom-call | flops 1 | bytes 1 | tf_op jit(solution)/shard_map/own_slab/pallas_call | solution.py:237
  33.9 0.0 collective-permute-done.5.refs_2_
  33.9 0.6 collective-permute-start.10
  34.5 0.0 collective-permute-start.9
  34.6 0.0 collective-permute-done.4.refs_1_
  34.6 1.5 %collective-permute-done.8.refs_3_ = bf16[6,192,128]{2,1,0:T(8,128)(2,1)S(1)} collective-permute-done((bf16[6,192,128]{2,1,0:T(8,128)(2,1)S(1)}, bf16[6,192,128]{2,1,0:T(8,128)(2,1)S(1)}, u32[]{:S(2)}, u32[]{:S(2)}) %collective-permute-start.8) | collective-permute-done | bytes 294944 | tf_op jit(solution)/shard_map/ppermute | solution.py:486
  36.1 4.5 %other_images.1.refs_0_ = s16[1168,128]{1,0:T(8,128)(2,1)S(1)} custom-call(s32[32,128]{1,0:T(8,128)S(4)} %ordered.1.refs_2_.table, f32[6,2,96,256]{3,2,1,0:T(8,128)S(1)} %own_slab.1.acc.refs_1_, bf16[3,27,96,384]{3,2,1,0:T(8,128)(2,1)S(1)} %squares.2.refs_1_.first.first_held, bf16[3,27,96,384]{3,2,1,0:T(8,128)(2,1)S(1)} %squares.3.second.second_held, ...), custom_call_target="tpu_custom_call" | custom-call | flops 1 | bytes 1000000000 | tf_op jit(solution)/shard_map/other_images/pallas_call | solution.py:300
  40.6 1.1 %collective-permute-done.10.refs_2_ = bf16[6,192,128]{2,1,0:T(8,128)(2,1)S(1)} collective-permute-done((bf16[6,192,128]{2,1,0:T(8,128)(2,1)S(1)}, bf16[6,192,128]{2,1,0:T(8,128)(2,1)S(1)}, u32[]{:S(2)}, u32[]{:S(2)}) %collective-permute-start.10) | collective-permute-done | bytes 294944 | tf_op jit(solution)/shard_map/ppermute | solution.py:489
  41.7 0.0 collective-permute-done.9.refs_1_.refs_0_
  41.7 1.5 %collective-permute-start.11 = (s16[1168,128]{1,0:T(8,128)(2,1)S(1)}, s16[1168,128]{1,0:T(8,128)(2,1)S(1)}, u32[]{:S(2)}, u32[]{:S(2)}) collective-permute-start(s16[1168,128]{1,0:T(8,128)(2,1)S(1)} %gate.5.refs_7_), channel_id=1, source_target_pairs={{0,2},{1,3},{2,0},{3,1},{4,6},{5,7},{6,4},{7,5},{8,10},{9,11},{10,... | collective-permute-start | bytes 897032 | tf_op jit(solution)/shard_map/ppermute | solution.py:493
  43.2 5.8 %own_rows.1 = (f32[12,192,128]{2,1,0:T(8,128)}, f32[16,128]{1,0:T(8,128)S(1)}, f32[6,192,128]{2,1,0:T(8,128)S(1)}, f32[6,192,128]{2,1,0:T(8,128)S(1)}, bf16[6,192,128]{2,1,0:T(8,128)(2,1)S(1)}) custom-call(s32[32,128]{1,0:T(8,128)S(4)} %ordered.1.refs_2_.table, f32[6,2,96,256]{3,2,1,0:T(8,128)S(1)} %own_slab.1.acc.refs_1_, ...), custom_call_target="tpu_custom_call" | custom-call | flops 1 | bytes 1000000000 | tf_op jit(solution)/shard_map/own_rows/pallas_call | solution.py:373
  49.0 0.0 collective-permute-done.11.coded
  49.0 0.9 %other_rows.1 = (f32[12,192,128]{2,1,0:T(8,128)}, f32[2,128]{1,0:T(2,128)S(1)}) custom-call(s16[1168,128]{1,0:T(8,128)(2,1)S(1)} %collective-permute-done.11.coded, f32[6,192,128]{2,1,0:T(8,128)S(1)} %get-tuple-element.9.prev, f32[6,192,128]{2,1,0:T(8,128)S(1)} %get-tuple-element.10.probes, ...), custom_call_target="tpu_custom_call", output_to_operand_aliasing={{0}: (5, {})} | custom-call | flops 1 | bytes 1 | tf_op jit(solution)/shard_map/other_rows/pallas_call | solution.py:420
  49.9 0.3 collective-permute-start.12
  50.3 3.3 %collective-permute-done.12 = f32[2,128]{1,0:T(2,128)S(1)} collective-permute-done((f32[2,128]{1,0:T(2,128)S(1)}, f32[2,128]{1,0:T(2,128)S(1)}, u32[]{:S(2)}, u32[]{:S(2)}) %collective-permute-start.12) | collective-permute-done | bytes 1056 | tf_op jit(solution)/shard_map/ppermute | solution.py:455
  53.6 0.0 collective-permute-start.13
  53.6 3.6 %collective-permute-done.13 = f32[2,128]{1,0:T(2,128)S(1)} collective-permute-done((f32[2,128]{1,0:T(2,128)S(1)}, f32[2,128]{1,0:T(2,128)S(1)}, u32[]{:S(2)}, u32[]{:S(2)}) %collective-permute-start.13) | collective-permute-done | bytes 1056 | tf_op jit(solution)/shard_map/ppermute | solution.py:455
  57.1 0.0 collective-permute-start.14
  57.1 4.5 %collective-permute-done.14 = f32[2,128]{1,0:T(2,128)S(1)} collective-permute-done((f32[2,128]{1,0:T(2,128)S(1)}, f32[2,128]{1,0:T(2,128)S(1)}, u32[]{:S(2)}, u32[]{:S(2)}) %collective-permute-start.14) | collective-permute-done | bytes 1056 | tf_op jit(solution)/shard_map/ppermute | solution.py:455
  61.6 0.6 add.11
  (5 shorter events, 0.0 us)
Async XLA Ops:
  0.6 25.8 %collective-permute-start = (bf16[3,27,36864]{2,1,0:T(8,128)(2,1)}, bf16[3,27,36864]{2,1,0:T(8,128)(2,1)S(1)}, u32[]{:S(2)}, u32[]{:S(2)}) collective-permute-start(bf16[3,27,36864]{2,1,0:T(8,128)(2,1)} %tiles.1), channel_id=1, source_target_pairs={{0,1},{1,0},{2,3},{3,2},{4,5},{5,4},{6,7},{7,6},{8,9},{9,8},{10,11... | collective-permute-start | bytes 17915912 | tf_op jit(solution)/shard_map/ppermute | solution.py:478
  2.2 10.2 %collective-permute-start.1 = (bf16[6,192,128]{2,1,0:T(8,128)(2,1)S(1)}, bf16[6,192,128]{2,1,0:T(8,128)(2,1)S(1)}, u32[]{:S(2)}, u32[]{:S(2)}) collective-permute-start(bf16[6,192,128]{2,1,0:T(8,128)(2,1)S(1)} %get-tuple-element.17.refs_0_), channel_id=1, source_target_pairs={{0,2},{1,3},{2,0},{3,1},{4,6},{5,7},{6,4},{7,5},{8,10},{9,11},{10,... | collective-permute-start | bytes 884744 | tf_op jit(solution)/shard_map/ppermute | solution.py:479
  4.8 4.8 %copy-start = (s32[12,27]{1,0:T(8,128)S(1)}, s32[12,27]{1,0:T(8,128)}, u32[]{:S(2)}) copy-start(s32[12,27]{1,0:T(8,128)} %neighbours.1) | copy-start | bytes 3892
  4.8 10.9 %collective-permute-start.6 = (bf16[6,192,128]{2,1,0:T(8,128)(2,1)S(1)}, bf16[6,192,128]{2,1,0:T(8,128)(2,1)S(1)}, u32[]{:S(2)}, u32[]{:S(2)}) collective-permute-start(bf16[6,192,128]{2,1,0:T(8,128)(2,1)S(1)} %get-tuple-element.16), channel_id=1, source_target_pairs={{0,4},{4,0},{8,12},{12,8},{16,20},{20,16},{24,28},{28,24},{1,5},{5... | collective-permute-start | bytes 884744 | tf_op jit(solution)/shard_map/ppermute | solution.py:480
  12.5 8.8 %collective-permute-start.3 = (bf16[6,192,128]{2,1,0:T(8,128)(2,1)S(1)}, bf16[6,192,128]{2,1,0:T(8,128)(2,1)S(1)}, u32[]{:S(2)}, u32[]{:S(2)}) collective-permute-start(bf16[6,192,128]{2,1,0:T(8,128)(2,1)S(1)} %gate.3.refs_0_), channel_id=1, source_target_pairs={{0,4},{4,0},{8,12},{12,8},{16,20},{20,16},{24,28},{28,24},{1,5},{5... | collective-permute-start | bytes 884744 | tf_op jit(solution)/shard_map/ppermute | solution.py:484
  14.2 8.7 %collective-permute-start.2 = (bf16[6,192,128]{2,1,0:T(8,128)(2,1)S(1)}, bf16[6,192,128]{2,1,0:T(8,128)(2,1)S(1)}, u32[]{:S(2)}, u32[]{:S(2)}) collective-permute-start(bf16[6,192,128]{2,1,0:T(8,128)(2,1)S(1)} %get-tuple-element.16), channel_id=1, source_target_pairs={{0,2},{1,3},{2,0},{3,1},{4,6},{5,7},{6,4},{7,5},{8,10},{9,11},{10,... | collective-permute-start | bytes 884744 | tf_op jit(solution)/shard_map/ppermute | solution.py:479
  15.7 12.4 %collective-permute-start.7 = (bf16[6,192,128]{2,1,0:T(8,128)(2,1)S(1)}, bf16[6,192,128]{2,1,0:T(8,128)(2,1)S(1)}, u32[]{:S(2)}, u32[]{:S(2)}) collective-permute-start(bf16[6,192,128]{2,1,0:T(8,128)(2,1)S(1)} %collective-permute-done.6.refs_1_), channel_id=1, source_target_pairs={{0,8},{4,28},{8,16},{12,4},{16,24},{20,12},{24,0},{28,20},{1,9},{5... | collective-permute-start | bytes 884744 | tf_op jit(solution)/shard_map/ppermute | solution.py:485
  21.3 12.6 %collective-permute-start.5 = (bf16[6,192,128]{2,1,0:T(8,128)(2,1)S(1)}, bf16[6,192,128]{2,1,0:T(8,128)(2,1)S(1)}, u32[]{:S(2)}, u32[]{:S(2)}) collective-permute-start(bf16[6,192,128]{2,1,0:T(8,128)(2,1)S(1)} %collective-permute-done.3.refs_0_), channel_id=1, source_target_pairs={{0,8},{4,28},{8,16},{12,4},{16,24},{20,12},{24,0},{28,20},{1,9},{5... | collective-permute-start | bytes 884744 | tf_op jit(solution)/shard_map/ppermute | solution.py:486
  22.9 11.6 %collective-permute-start.4 = (bf16[6,192,128]{2,1,0:T(8,128)(2,1)S(1)}, bf16[6,192,128]{2,1,0:T(8,128)(2,1)S(1)}, u32[]{:S(2)}, u32[]{:S(2)}) collective-permute-start(bf16[6,192,128]{2,1,0:T(8,128)(2,1)S(1)} %collective-permute-done.2.refs_1_), channel_id=1, source_target_pairs={{0,4},{4,0},{8,12},{12,8},{16,20},{20,16},{24,28},{28,24},{1,5},{5... | collective-permute-start | bytes 884744 | tf_op jit(solution)/shard_map/ppermute | solution.py:484
  28.1 8.0 %collective-permute-start.8 = (bf16[6,192,128]{2,1,0:T(8,128)(2,1)S(1)}, bf16[6,192,128]{2,1,0:T(8,128)(2,1)S(1)}, u32[]{:S(2)}, u32[]{:S(2)}) collective-permute-start(bf16[6,192,128]{2,1,0:T(8,128)(2,1)S(1)} %collective-permute-done.7.refs_3_), channel_id=1, source_target_pairs={{0,2},{1,3},{2,0},{3,1},{4,6},{5,7},{6,4},{7,5},{8,10},{9,11},{10,... | collective-permute-start | bytes 884744 | tf_op jit(solution)/shard_map/ppermute | solution.py:486
  33.9 7.7 %collective-permute-start.10 = (bf16[6,192,128]{2,1,0:T(8,128)(2,1)S(1)}, bf16[6,192,128]{2,1,0:T(8,128)(2,1)S(1)}, u32[]{:S(2)}, u32[]{:S(2)}) collective-permute-start(bf16[6,192,128]{2,1,0:T(8,128)(2,1)S(1)} %collective-permute-done.5.refs_2_), channel_id=1, source_target_pairs={{0,2},{1,3},{2,0},{3,1},{4,6},{5,7},{6,4},{7,5},{8,10},{9,11},{10,... | collective-permute-start | bytes 884744 | tf_op jit(solution)/shard_map/ppermute | solution.py:489
  34.5 7.1 %collective-permute-start.9 = (bf16[6,192,128]{2,1,0:T(8,128)(2,1)S(1)}, bf16[6,192,128]{2,1,0:T(8,128)(2,1)S(1)}, u32[]{:S(2)}, u32[]{:S(2)}) collective-permute-start(bf16[6,192,128]{2,1,0:T(8,128)(2,1)S(1)} %gate.4), channel_id=1, source_target_pairs={{0,4},{4,0},{8,12},{12,8},{16,20},{20,16},{24,28},{28,24},{1,5},{5... | collective-permute-start | bytes 884744 | tf_op jit(solution)/shard_map/ppermute | solution.py:488
  41.7 7.3 %collective-permute-start.11 = (s16[1168,128]{1,0:T(8,128)(2,1)S(1)}, s16[1168,128]{1,0:T(8,128)(2,1)S(1)}, u32[]{:S(2)}, u32[]{:S(2)}) collective-permute-start(s16[1168,128]{1,0:T(8,128)(2,1)S(1)} %gate.5.refs_7_), channel_id=1, source_target_pairs={{0,2},{1,3},{2,0},{3,1},{4,6},{5,7},{6,4},{7,5},{8,10},{9,11},{10,... | collective-permute-start | bytes 897032 | tf_op jit(solution)/shard_map/ppermute | solution.py:493
  49.9 3.6 %collective-permute-start.12 = (f32[2,128]{1,0:T(2,128)S(1)}, f32[2,128]{1,0:T(2,128)S(1)}, u32[]{:S(2)}, u32[]{:S(2)}) collective-permute-start(f32[2,128]{1,0:T(2,128)S(1)} %get-tuple-element.15), channel_id=1, source_target_pairs={{0,4},{4,0},{8,12},{12,8},{16,20},{20,16},{24,28},{28,24},{1,5},{5... | collective-permute-start | bytes 3080 | tf_op jit(solution)/shard_map/ppermute | solution.py:455
  53.6 3.6 %collective-permute-start.13 = (f32[2,128]{1,0:T(2,128)S(1)}, f32[2,128]{1,0:T(2,128)S(1)}, u32[]{:S(2)}, u32[]{:S(2)}) collective-permute-start(f32[2,128]{1,0:T(2,128)S(1)} %add.9), channel_id=1, source_target_pairs={{0,8},{4,12},{8,0},{12,4},{16,24},{20,28},{24,16},{28,20},{1,9},{5... | collective-permute-start | bytes 3080 | tf_op jit(solution)/shard_map/ppermute | solution.py:455
  57.1 4.5 %collective-permute-start.14 = (f32[2,128]{1,0:T(2,128)S(1)}, f32[2,128]{1,0:T(2,128)S(1)}, u32[]{:S(2)}, u32[]{:S(2)}) collective-permute-start(f32[2,128]{1,0:T(2,128)S(1)} %add.10), channel_id=1, source_target_pairs={{0,16},{4,20},{8,24},{12,28},{16,0},{20,4},{24,8},{28,12},{1,17},{... | collective-permute-start | bytes 3080 | tf_op jit(solution)/shard_map/ppermute | solution.py:455

commit v5 on v4

--- a/solution.py
+++ b/solution.py
@@ -450,10 +450,14 @@
     size = lax.axis_size(axis)
     if size & (size - 1):
         return lax.psum(value, axis)
-    hop = 1
+    value, hop = value + lax.ppermute(value, axis, [(i, i ^ 1) for i in range(size)]), 2
     while hop < size:
-        value = value + lax.ppermute(value, axis, [(i, i ^ hop) for i in range(size)])
-        hop *= 2
+        jumps = (hop, 2 * hop, 3 * hop) if 2 * hop < size else (hop,)
+        far = [lax.ppermute(value, axis, [(i, i ^ j) for i in range(size)]) for j in jumps]
+        value = value + far[0]
+        if len(far) > 1:
+            value = value + (far[1] + far[2])
+        hop *= len(jumps) + 1
     return value
 
 
@@ -481,7 +485,7 @@
     table = ordered(neighbours)
     held = [squares(tiles, rows, False), squares(sib_tiles, rows, True)]
     oth[0] = gate(oth[0], held[0], table)
-    near_oth = [pair(c) for c in oth]
+    near_oth = [pair(oth[0]), pair(oth[1])]
     far_high = along(near_high)
     far_oth = [along(near_oth[0]), across(far_high)]
     acc = own_slab(table, held, fixed, oth)

time: 62.4 us -> 59.7 us (0.957)
  waiting for transfers between devices: 19.6 us -> 13.4 us
  starting transfers between devices: 18.6 us -> 22.1 us
    ppermute x5 -> x6, waiting for transfers between devices: 15.3 us -> 9.16 us  [the longest x2 3.99 us: shards(): near_oth = [pair(oth[0]), pair(oth[1])]]
    ppermute x5 -> x6, starting transfers between devices: 5.66 us -> 9.14 us  [the longest x2 5.31 us: shards(): near_oth = [pair(oth[0]), pair(oth[1])]]
  transfers between devices with their start and end apart: 15 -> 16, of which waited for: 7 -> 7; matrix products, arithmetic and copies ran while one was open for 2% -> 2% of each run, Pallas kernels for 33% -> 35%
where the time goes in v5:
time: 59.7 us; the launch traced here: 59.5 us
  starting transfers between devices  22.1 us (37%)
  Pallas kernels  21.6 us (36%)
  waiting for transfers between devices  13.4 us (22%)
  local copies, waits for them, and re-layouts  1.09 us (2%)
  between operations  0.74 us (1%)
    pallas_call x1, Pallas kernels, own_rows(): pl.pallas_call(functools.partial(own_kernel, len(chunks), factor), in_spe...  5.77 us
    ppermute x2, starting transfers between devices, shards(): near_oth = [pair(oth[0]), pair(oth[1])]  5.31 us
    pallas_call x2, Pallas kernels, squares(): pl.pallas_call(held_kernel if resident else functools.partial(square_kern...  4.88 us
    pallas_call x1, Pallas kernels, other_images(): pl.pallas_call(functools.partial(other_kernel, len(chunks)), in_specs=[SM...  4.56 us
    pallas_call x1, Pallas kernels, own_slab(): pl.pallas_call(functools.partial(slab_kernel, len(other)), in_specs=[SMEM...  4.24 us
    ppermute x2, starting transfers between devices, shards(): oth = [across(low), across(high)]  4.06 us
    ppermute x2, waiting for transfers between devices, shards(): near_oth = [pair(oth[0]), pair(oth[1])]  3.99 us
    ppermute x3, starting transfers between devices, sum_over(): lax.ppermute(value, axis, [(i, i ^ j) for i in range(size)])  3.49 us
  transfers between devices with their start and end apart: 16, of which 7 were waited for; matrix products, arithmetic and copies ran while one was open for 2% of the time, Pallas kernels for 35%

profile of v5, /device:TPU:0, one launch (start us, length us, event | category | flops | bytes accessed | tf_op | source)
XLA Modules:
  0.0 59.5 jit_solution(5427017342536609621)
XLA Ops:
  0.6 0.5 collective-permute-start
  1.1 1.1 %fusion = (bf16[6,192,128]{2,1,0:T(8,128)(2,1)S(1)}, bf16[6,192,128]{2,1,0:T(8,128)(2,1)S(1)}) fusion(bf16[12,192,128]{2,1,0:T(8,128)(2,1)} %refs_6_.1), kind=kLoop, calls=%fused_computation.1 | loop fusion | bytes 1179648 | tf_op jit(solution)/shard_map/slice | solution.py:480
  2.2 2.6 %collective-permute-start.1 = (bf16[6,192,128]{2,1,0:T(8,128)(2,1)S(1)}, bf16[6,192,128]{2,1,0:T(8,128)(2,1)S(1)}, u32[]{:S(2)}, u32[]{:S(2)}) collective-permute-start(bf16[6,192,128]{2,1,0:T(8,128)(2,1)S(1)} %get-tuple-element.17.refs_0_), channel_id=1, source_target_pairs={{0,2},{1,3},{2,0},{3,1},{4,6},{5,7},{6,4},{7,5},{8,10},{9,11},{10,... | collective-permute-start | bytes 884744 | tf_op jit(solution)/shard_map/ppermute | solution.py:483
  4.8 0.0 copy-start
  4.8 1.5 %collective-permute-start.6 = (bf16[6,192,128]{2,1,0:T(8,128)(2,1)S(1)}, bf16[6,192,128]{2,1,0:T(8,128)(2,1)S(1)}, u32[]{:S(2)}, u32[]{:S(2)}) collective-permute-start(bf16[6,192,128]{2,1,0:T(8,128)(2,1)S(1)} %get-tuple-element.16), channel_id=1, source_target_pairs={{0,4},{4,0},{8,12},{12,8},{16,20},{20,16},{24,28},{28,24},{1,5},{5... | collective-permute-start | bytes 884744 | tf_op jit(solution)/shard_map/ppermute | solution.py:484
  6.3 3.2 %squares.2.refs_1_.first.first_held = bf16[3,27,96,384]{3,2,1,0:T(8,128)(2,1)S(1)} custom-call(bf16[3,27,36864]{2,1,0:T(8,128)(2,1)} %tiles.1), custom_call_target="tpu_custom_call" | custom-call | flops 1 | bytes 18000000 | tf_op jit(solution)/shard_map/squares/pallas_call | solution.py:133
  9.6 0.0 copy-done
  9.6 1.1 %ordered.1.refs_2_.table = s32[32,128]{1,0:T(8,128)S(4)} custom-call(s32[12,27]{1,0:T(8,128)S(1)} %copy-done), custom_call_target="tpu_custom_call" | custom-call | flops 1 | bytes 1 | tf_op jit(solution)/shard_map/ordered/pallas_call | solution.py:82
  10.8 1.7 %collective-permute-done.1.refs_0_ = bf16[6,192,128]{2,1,0:T(8,128)(2,1)S(1)} collective-permute-done((bf16[6,192,128]{2,1,0:T(8,128)(2,1)S(1)}, bf16[6,192,128]{2,1,0:T(8,128)(2,1)S(1)}, u32[]{:S(2)}, u32[]{:S(2)}) %collective-permute-start.1) | collective-permute-done | bytes 294944 | tf_op jit(solution)/shard_map/ppermute | solution.py:483
  12.5 1.8 %collective-permute-start.3 = (bf16[6,192,128]{2,1,0:T(8,128)(2,1)S(1)}, bf16[6,192,128]{2,1,0:T(8,128)(2,1)S(1)}, u32[]{:S(2)}, u32[]{:S(2)}) collective-permute-start(bf16[6,192,128]{2,1,0:T(8,128)(2,1)S(1)} %gate.3.refs_0_), channel_id=1, source_target_pairs={{0,4},{4,0},{8,12},{12,8},{16,20},{20,16},{24,28},{28,24},{1,5},{5... | collective-permute-start | bytes 884744 | tf_op jit(solution)/shard_map/ppermute | solution.py:488
  14.2 1.5 %collective-permute-start.2 = (bf16[6,192,128]{2,1,0:T(8,128)(2,1)S(1)}, bf16[6,192,128]{2,1,0:T(8,128)(2,1)S(1)}, u32[]{:S(2)}, u32[]{:S(2)}) collective-permute-start(bf16[6,192,128]{2,1,0:T(8,128)(2,1)S(1)} %get-tuple-element.16), channel_id=1, source_target_pairs={{0,2},{1,3},{2,0},{3,1},{4,6},{5,7},{6,4},{7,5},{8,10},{9,11},{10,... | collective-permute-start | bytes 884744 | tf_op jit(solution)/shard_map/ppermute | solution.py:483
  15.7 0.0 collective-permute-done.6.refs_1_
  15.7 1.6 %collective-permute-start.7 = (bf16[6,192,128]{2,1,0:T(8,128)(2,1)S(1)}, bf16[6,192,128]{2,1,0:T(8,128)(2,1)S(1)}, u32[]{:S(2)}, u32[]{:S(2)}) collective-permute-start(bf16[6,192,128]{2,1,0:T(8,128)(2,1)S(1)} %collective-permute-done.6.refs_1_), channel_id=1, source_target_pairs={{0,8},{4,28},{8,16},{12,4},{16,24},{20,12},{24,0},{28,20},{1,9},{5... | collective-permute-start | bytes 884744 | tf_op jit(solution)/shard_map/ppermute | solution.py:489
  17.3 4.0 %collective-permute-done.3.refs_0_ = bf16[6,192,128]{2,1,0:T(8,128)(2,1)S(1)} collective-permute-done((bf16[6,192,128]{2,1,0:T(8,128)(2,1)S(1)}, bf16[6,192,128]{2,1,0:T(8,128)(2,1)S(1)}, u32[]{:S(2)}, u32[]{:S(2)}) %collective-permute-start.3) | collective-permute-done | bytes 294944 | tf_op jit(solution)/shard_map/ppermute | solution.py:488
  21.3 1.6 %collective-permute-start.5 = (bf16[6,192,128]{2,1,0:T(8,128)(2,1)S(1)}, bf16[6,192,128]{2,1,0:T(8,128)(2,1)S(1)}, u32[]{:S(2)}, u32[]{:S(2)}) collective-permute-start(bf16[6,192,128]{2,1,0:T(8,128)(2,1)S(1)} %collective-permute-done.3.refs_0_), channel_id=1, source_target_pairs={{0,8},{4,28},{8,16},{12,4},{16,24},{20,12},{24,0},{28,20},{1,9},{5... | collective-permute-start | bytes 884744 | tf_op jit(solution)/shard_map/ppermute | solution.py:490
  22.9 0.0 collective-permute-done.2.refs_1_
  22.9 3.5 %collective-permute-start.4 = (bf16[6,192,128]{2,1,0:T(8,128)(2,1)S(1)}, bf16[6,192,128]{2,1,0:T(8,128)(2,1)S(1)}, u32[]{:S(2)}, u32[]{:S(2)}) collective-permute-start(bf16[6,192,128]{2,1,0:T(8,128)(2,1)S(1)} %collective-permute-done.2.refs_1_), channel_id=1, source_target_pairs={{0,4},{4,0},{8,12},{12,8},{16,20},{20,16},{24,28},{28,24},{1,5},{5... | collective-permute-start | bytes 884744 | tf_op jit(solution)/shard_map/ppermute | solution.py:488
  26.5 0.0 collective-permute-done.tiles
  26.5 1.6 %squares.3.second.second_held = bf16[3,27,96,384]{3,2,1,0:T(8,128)(2,1)S(1)} custom-call(bf16[3,27,36864]{2,1,0:T(8,128)(2,1)S(1)} %collective-permute-done.tiles), custom_call_target="tpu_custom_call" | custom-call | flops 1 | bytes 18000000 | tf_op jit(solution)/shard_map/squares/pallas_call | solution.py:133
  28.1 0.0 collective-permute-done.7.refs_3_
  28.1 1.6 %collective-permute-start.8 = (bf16[6,192,128]{2,1,0:T(8,128)(2,1)S(1)}, bf16[6,192,128]{2,1,0:T(8,128)(2,1)S(1)}, u32[]{:S(2)}, u32[]{:S(2)}) collective-permute-start(bf16[6,192,128]{2,1,0:T(8,128)(2,1)S(1)} %collective-permute-done.7.refs_3_), channel_id=1, source_target_pairs={{0,2},{1,3},{2,0},{3,1},{4,6},{5,7},{6,4},{7,5},{8,10},{9,11},{10,... | collective-permute-start | bytes 884744 | tf_op jit(solution)/shard_map/ppermute | solution.py:490
  29.7 4.2 %own_slab.1.acc.refs_1_ = f32[6,2,96,256]{3,2,1,0:T(8,128)S(1)} custom-call(s32[32,128]{1,0:T(8,128)S(4)} %ordered.1.refs_2_.table, bf16[3,27,96,384]{3,2,1,0:T(8,128)(2,1)S(1)} %squares.2.refs_1_.first.first_held, bf16[3,27,96,384]{3,2,1,0:T(8,128)(2,1)S(1)} %squares.3.second.second_held, bf16[12,192,128]{2,1,0:T(8,128)(2,1)} %refs_6_.1, ...), custom_call_target="tpu_custom_call" | custom-call | flops 1 | bytes 1 | tf_op jit(solution)/shard_map/own_slab/pallas_call | solution.py:237
  33.9 0.0 collective-permute-done.5.refs_2_
  34.0 0.6 %collective-permute-start.10 = (bf16[6,192,128]{2,1,0:T(8,128)(2,1)S(1)}, bf16[6,192,128]{2,1,0:T(8,128)(2,1)S(1)}, u32[]{:S(2)}, u32[]{:S(2)}) collective-permute-start(bf16[6,192,128]{2,1,0:T(8,128)(2,1)S(1)} %collective-permute-done.5.refs_2_), channel_id=1, source_target_pairs={{0,2},{1,3},{2,0},{3,1},{4,6},{5,7},{6,4},{7,5},{8,10},{9,11},{10,... | collective-permute-start | bytes 884744 | tf_op jit(solution)/shard_map/ppermute | solution.py:493
  34.5 0.0 collective-permute-start.9
  34.6 0.0 collective-permute-done.4.refs_1_
  34.6 1.5 %collective-permute-done.8.refs_3_ = bf16[6,192,128]{2,1,0:T(8,128)(2,1)S(1)} collective-permute-done((bf16[6,192,128]{2,1,0:T(8,128)(2,1)S(1)}, bf16[6,192,128]{2,1,0:T(8,128)(2,1)S(1)}, u32[]{:S(2)}, u32[]{:S(2)}) %collective-permute-start.8) | collective-permute-done | bytes 294944 | tf_op jit(solution)/shard_map/ppermute | solution.py:490
  36.1 4.6 %other_images.1.refs_0_ = s16[1168,128]{1,0:T(8,128)(2,1)S(1)} custom-call(s32[32,128]{1,0:T(8,128)S(4)} %ordered.1.refs_2_.table, f32[6,2,96,256]{3,2,1,0:T(8,128)S(1)} %own_slab.1.acc.refs_1_, bf16[3,27,96,384]{3,2,1,0:T(8,128)(2,1)S(1)} %squares.2.refs_1_.first.first_held, bf16[3,27,96,384]{3,2,1,0:T(8,128)(2,1)S(1)} %squares.3.second.second_held, ...), custom_call_target="tpu_custom_call" | custom-call | flops 1 | bytes 1000000000 | tf_op jit(solution)/shard_map/other_images/pallas_call | solution.py:300
  40.7 1.0 %collective-permute-done.10.refs_2_ = bf16[6,192,128]{2,1,0:T(8,128)(2,1)S(1)} collective-permute-done((bf16[6,192,128]{2,1,0:T(8,128)(2,1)S(1)}, bf16[6,192,128]{2,1,0:T(8,128)(2,1)S(1)}, u32[]{:S(2)}, u32[]{:S(2)}) %collective-permute-start.10) | collective-permute-done | bytes 294944 | tf_op jit(solution)/shard_map/ppermute | solution.py:493
  41.7 0.0 collective-permute-done.9.refs_1_.refs_0_
  41.7 1.5 %collective-permute-start.11 = (s16[1168,128]{1,0:T(8,128)(2,1)S(1)}, s16[1168,128]{1,0:T(8,128)(2,1)S(1)}, u32[]{:S(2)}, u32[]{:S(2)}) collective-permute-start(s16[1168,128]{1,0:T(8,128)(2,1)S(1)} %gate.5.refs_7_), channel_id=1, source_target_pairs={{0,2},{1,3},{2,0},{3,1},{4,6},{5,7},{6,4},{7,5},{8,10},{9,11},{10,... | collective-permute-start | bytes 897032 | tf_op jit(solution)/shard_map/ppermute | solution.py:497
  43.2 5.8 %own_rows.1 = (f32[12,192,128]{2,1,0:T(8,128)}, f32[16,128]{1,0:T(8,128)S(1)}, f32[6,192,128]{2,1,0:T(8,128)S(1)}, f32[6,192,128]{2,1,0:T(8,128)S(1)}, bf16[6,192,128]{2,1,0:T(8,128)(2,1)S(1)}) custom-call(s32[32,128]{1,0:T(8,128)S(4)} %ordered.1.refs_2_.table, f32[6,2,96,256]{3,2,1,0:T(8,128)S(1)} %own_slab.1.acc.refs_1_, ...), custom_call_target="tpu_custom_call" | custom-call | flops 1 | bytes 1000000000 | tf_op jit(solution)/shard_map/own_rows/pallas_call | solution.py:373
  49.0 0.0 collective-permute-done.11.coded
  49.0 0.9 %other_rows.1 = (f32[12,192,128]{2,1,0:T(8,128)}, f32[2,128]{1,0:T(2,128)S(1)}) custom-call(s16[1168,128]{1,0:T(8,128)(2,1)S(1)} %collective-permute-done.11.coded, f32[6,192,128]{2,1,0:T(8,128)S(1)} %get-tuple-element.9.prev, f32[6,192,128]{2,1,0:T(8,128)S(1)} %get-tuple-element.10.probes, ...), custom_call_target="tpu_custom_call", output_to_operand_aliasing={{0}: (5, {})} | custom-call | flops 1 | bytes 1 | tf_op jit(solution)/shard_map/other_rows/pallas_call | solution.py:420
  50.0 0.3 collective-permute-start.12
  50.3 3.3 %collective-permute-done.12 = f32[2,128]{1,0:T(2,128)S(1)} collective-permute-done((f32[2,128]{1,0:T(2,128)S(1)}, f32[2,128]{1,0:T(2,128)S(1)}, u32[]{:S(2)}, u32[]{:S(2)}) %collective-permute-start.12) | collective-permute-done | bytes 1056 | tf_op jit(solution)/shard_map/ppermute | solution.py:453
  53.6 0.0 collective-permute-start.14
  53.6 0.7 %collective-permute-start.15 = (f32[2,128]{1,0:T(2,128)S(1)}, f32[2,128]{1,0:T(2,128)S(1)}, u32[]{:S(2)}, u32[]{:S(2)}) collective-permute-start(f32[2,128]{1,0:T(2,128)S(1)} %add.12), channel_id=1, source_target_pairs={{0,24},{4,28},{8,16},{12,20},{16,8},{20,12},{24,0},{28,4},{1,25},{... | collective-permute-start | bytes 3080 | tf_op jit(solution)/shard_map/ppermute | solution.py:456
  54.3 2.7 %collective-permute-start.13 = (f32[2,128]{1,0:T(2,128)S(1)}, f32[2,128]{1,0:T(2,128)S(1)}, u32[]{:S(2)}, u32[]{:S(2)}) collective-permute-start(f32[2,128]{1,0:T(2,128)S(1)} %add.12), channel_id=1, source_target_pairs={{0,8},{4,12},{8,0},{12,4},{16,24},{20,28},{24,16},{28,20},{1,9},{5... | collective-permute-start | bytes 3080 | tf_op jit(solution)/shard_map/ppermute | solution.py:456
  57.1 1.0 %collective-permute-done.14 = f32[2,128]{1,0:T(2,128)S(1)} collective-permute-done((f32[2,128]{1,0:T(2,128)S(1)}, f32[2,128]{1,0:T(2,128)S(1)}, u32[]{:S(2)}, u32[]{:S(2)}) %collective-permute-start.14) | collective-permute-done | bytes 1056 | tf_op jit(solution)/shard_map/ppermute | solution.py:456
  58.1 0.9 %collective-permute-done.15 = f32[2,128]{1,0:T(2,128)S(1)} collective-permute-done((f32[2,128]{1,0:T(2,128)S(1)}, f32[2,128]{1,0:T(2,128)S(1)}, u32[]{:S(2)}, u32[]{:S(2)}) %collective-permute-start.15) | collective-permute-done | bytes 1056 | tf_op jit(solution)/shard_map/ppermute | solution.py:456
  59.0 0.0 collective-permute-done.13
  59.0 0.6 add_add_fusion
  (4 shorter events, 0.0 us)
Async XLA Ops:
  0.6 25.8 %collective-permute-start = (bf16[3,27,36864]{2,1,0:T(8,128)(2,1)}, bf16[3,27,36864]{2,1,0:T(8,128)(2,1)S(1)}, u32[]{:S(2)}, u32[]{:S(2)}) collective-permute-start(bf16[3,27,36864]{2,1,0:T(8,128)(2,1)} %tiles.1), channel_id=1, source_target_pairs={{0,1},{1,0},{2,3},{3,2},{4,5},{5,4},{6,7},{7,6},{8,9},{9,8},{10,11... | collective-permute-start | bytes 17915912 | tf_op jit(solution)/shard_map/ppermute | solution.py:482
  2.2 10.2 %collective-permute-start.1 = (bf16[6,192,128]{2,1,0:T(8,128)(2,1)S(1)}, bf16[6,192,128]{2,1,0:T(8,128)(2,1)S(1)}, u32[]{:S(2)}, u32[]{:S(2)}) collective-permute-start(bf16[6,192,128]{2,1,0:T(8,128)(2,1)S(1)} %get-tuple-element.17.refs_0_), channel_id=1, source_target_pairs={{0,2},{1,3},{2,0},{3,1},{4,6},{5,7},{6,4},{7,5},{8,10},{9,11},{10,... | collective-permute-start | bytes 884744 | tf_op jit(solution)/shard_map/ppermute | solution.py:483
  4.8 4.8 %copy-start = (s32[12,27]{1,0:T(8,128)S(1)}, s32[12,27]{1,0:T(8,128)}, u32[]{:S(2)}) copy-start(s32[12,27]{1,0:T(8,128)} %neighbours.1) | copy-start | bytes 3892
  4.8 10.9 %collective-permute-start.6 = (bf16[6,192,128]{2,1,0:T(8,128)(2,1)S(1)}, bf16[6,192,128]{2,1,0:T(8,128)(2,1)S(1)}, u32[]{:S(2)}, u32[]{:S(2)}) collective-permute-start(bf16[6,192,128]{2,1,0:T(8,128)(2,1)S(1)} %get-tuple-element.16), channel_id=1, source_target_pairs={{0,4},{4,0},{8,12},{12,8},{16,20},{20,16},{24,28},{28,24},{1,5},{5... | collective-permute-start | bytes 884744 | tf_op jit(solution)/shard_map/ppermute | solution.py:484
  12.5 8.8 %collective-permute-start.3 = (bf16[6,192,128]{2,1,0:T(8,128)(2,1)S(1)}, bf16[6,192,128]{2,1,0:T(8,128)(2,1)S(1)}, u32[]{:S(2)}, u32[]{:S(2)}) collective-permute-start(bf16[6,192,128]{2,1,0:T(8,128)(2,1)S(1)} %gate.3.refs_0_), channel_id=1, source_target_pairs={{0,4},{4,0},{8,12},{12,8},{16,20},{20,16},{24,28},{28,24},{1,5},{5... | collective-permute-start | bytes 884744 | tf_op jit(solution)/shard_map/ppermute | solution.py:488
  14.2 8.7 %collective-permute-start.2 = (bf16[6,192,128]{2,1,0:T(8,128)(2,1)S(1)}, bf16[6,192,128]{2,1,0:T(8,128)(2,1)S(1)}, u32[]{:S(2)}, u32[]{:S(2)}) collective-permute-start(bf16[6,192,128]{2,1,0:T(8,128)(2,1)S(1)} %get-tuple-element.16), channel_id=1, source_target_pairs={{0,2},{1,3},{2,0},{3,1},{4,6},{5,7},{6,4},{7,5},{8,10},{9,11},{10,... | collective-permute-start | bytes 884744 | tf_op jit(solution)/shard_map/ppermute | solution.py:483
  15.7 12.4 %collective-permute-start.7 = (bf16[6,192,128]{2,1,0:T(8,128)(2,1)S(1)}, bf16[6,192,128]{2,1,0:T(8,128)(2,1)S(1)}, u32[]{:S(2)}, u32[]{:S(2)}) collective-permute-start(bf16[6,192,128]{2,1,0:T(8,128)(2,1)S(1)} %collective-permute-done.6.refs_1_), channel_id=1, source_target_pairs={{0,8},{4,28},{8,16},{12,4},{16,24},{20,12},{24,0},{28,20},{1,9},{5... | collective-permute-start | bytes 884744 | tf_op jit(solution)/shard_map/ppermute | solution.py:489
  21.3 12.6 %collective-permute-start.5 = (bf16[6,192,128]{2,1,0:T(8,128)(2,1)S(1)}, bf16[6,192,128]{2,1,0:T(8,128)(2,1)S(1)}, u32[]{:S(2)}, u32[]{:S(2)}) collective-permute-start(bf16[6,192,128]{2,1,0:T(8,128)(2,1)S(1)} %collective-permute-done.3.refs_0_), channel_id=1, source_target_pairs={{0,8},{4,28},{8,16},{12,4},{16,24},{20,12},{24,0},{28,20},{1,9},{5... | collective-permute-start | bytes 884744 | tf_op jit(solution)/shard_map/ppermute | solution.py:490
  22.9 11.6 %collective-permute-start.4 = (bf16[6,192,128]{2,1,0:T(8,128)(2,1)S(1)}, bf16[6,192,128]{2,1,0:T(8,128)(2,1)S(1)}, u32[]{:S(2)}, u32[]{:S(2)}) collective-permute-start(bf16[6,192,128]{2,1,0:T(8,128)(2,1)S(1)} %collective-permute-done.2.refs_1_), channel_id=1, source_target_pairs={{0,4},{4,0},{8,12},{12,8},{16,20},{20,16},{24,28},{28,24},{1,5},{5... | collective-permute-start | bytes 884744 | tf_op jit(solution)/shard_map/ppermute | solution.py:488
  28.1 8.0 %collective-permute-start.8 = (bf16[6,192,128]{2,1,0:T(8,128)(2,1)S(1)}, bf16[6,192,128]{2,1,0:T(8,128)(2,1)S(1)}, u32[]{:S(2)}, u32[]{:S(2)}) collective-permute-start(bf16[6,192,128]{2,1,0:T(8,128)(2,1)S(1)} %collective-permute-done.7.refs_3_), channel_id=1, source_target_pairs={{0,2},{1,3},{2,0},{3,1},{4,6},{5,7},{6,4},{7,5},{8,10},{9,11},{10,... | collective-permute-start | bytes 884744 | tf_op jit(solution)/shard_map/ppermute | solution.py:490
  34.0 7.7 %collective-permute-start.10 = (bf16[6,192,128]{2,1,0:T(8,128)(2,1)S(1)}, bf16[6,192,128]{2,1,0:T(8,128)(2,1)S(1)}, u32[]{:S(2)}, u32[]{:S(2)}) collective-permute-start(bf16[6,192,128]{2,1,0:T(8,128)(2,1)S(1)} %collective-permute-done.5.refs_2_), channel_id=1, source_target_pairs={{0,2},{1,3},{2,0},{3,1},{4,6},{5,7},{6,4},{7,5},{8,10},{9,11},{10,... | collective-permute-start | bytes 884744 | tf_op jit(solution)/shard_map/ppermute | solution.py:493
  34.5 7.1 %collective-permute-start.9 = (bf16[6,192,128]{2,1,0:T(8,128)(2,1)S(1)}, bf16[6,192,128]{2,1,0:T(8,128)(2,1)S(1)}, u32[]{:S(2)}, u32[]{:S(2)}) collective-permute-start(bf16[6,192,128]{2,1,0:T(8,128)(2,1)S(1)} %gate.4), channel_id=1, source_target_pairs={{0,4},{4,0},{8,12},{12,8},{16,20},{20,16},{24,28},{28,24},{1,5},{5... | collective-permute-start | bytes 884744 | tf_op jit(solution)/shard_map/ppermute | solution.py:492
  41.7 7.3 %collective-permute-start.11 = (s16[1168,128]{1,0:T(8,128)(2,1)S(1)}, s16[1168,128]{1,0:T(8,128)(2,1)S(1)}, u32[]{:S(2)}, u32[]{:S(2)}) collective-permute-start(s16[1168,128]{1,0:T(8,128)(2,1)S(1)} %gate.5.refs_7_), channel_id=1, source_target_pairs={{0,2},{1,3},{2,0},{3,1},{4,6},{5,7},{6,4},{7,5},{8,10},{9,11},{10,... | collective-permute-start | bytes 897032 | tf_op jit(solution)/shard_map/ppermute | solution.py:497
  50.0 3.6 %collective-permute-start.12 = (f32[2,128]{1,0:T(2,128)S(1)}, f32[2,128]{1,0:T(2,128)S(1)}, u32[]{:S(2)}, u32[]{:S(2)}) collective-permute-start(f32[2,128]{1,0:T(2,128)S(1)} %get-tuple-element.15), channel_id=1, source_target_pairs={{0,4},{4,0},{8,12},{12,8},{16,20},{20,16},{24,28},{28,24},{1,5},{5... | collective-permute-start | bytes 3080 | tf_op jit(solution)/shard_map/ppermute | solution.py:453
  53.6 4.5 %collective-permute-start.14 = (f32[2,128]{1,0:T(2,128)S(1)}, f32[2,128]{1,0:T(2,128)S(1)}, u32[]{:S(2)}, u32[]{:S(2)}) collective-permute-start(f32[2,128]{1,0:T(2,128)S(1)} %add.12), channel_id=1, source_target_pairs={{0,16},{4,20},{8,24},{12,28},{16,0},{20,4},{24,8},{28,12},{1,17},{... | collective-permute-start | bytes 3080 | tf_op jit(solution)/shard_map/ppermute | solution.py:456
  53.6 5.4 %collective-permute-start.15 = (f32[2,128]{1,0:T(2,128)S(1)}, f32[2,128]{1,0:T(2,128)S(1)}, u32[]{:S(2)}, u32[]{:S(2)}) collective-permute-start(f32[2,128]{1,0:T(2,128)S(1)} %add.12), channel_id=1, source_target_pairs={{0,24},{4,28},{8,16},{12,20},{16,8},{20,12},{24,0},{28,4},{1,25},{... | collective-permute-start | bytes 3080 | tf_op jit(solution)/shard_map/ppermute | solution.py:456
  54.3 4.6 %collective-permute-start.13 = (f32[2,128]{1,0:T(2,128)S(1)}, f32[2,128]{1,0:T(2,128)S(1)}, u32[]{:S(2)}, u32[]{:S(2)}) collective-permute-start(f32[2,128]{1,0:T(2,128)S(1)} %add.12), channel_id=1, source_target_pairs={{0,8},{4,12},{8,0},{12,4},{16,24},{20,28},{24,16},{28,20},{1,9},{5... | collective-permute-start | bytes 3080 | tf_op jit(solution)/shard_map/ppermute | solution.py:456

commit v6 on v5

--- a/solution.py
+++ b/solution.py
@@ -125,21 +125,21 @@
         square_part(src, held.at[b], pl.multiple_of(part * 16, 16))
 
 
-def squares(tiles, rows, resident):
+def squares(tiles, rows):
     count, neigh = tiles.shape[:2]
     half, wide = rows // 2, 2 * rows
     parts = 3 * count
     raw = [pltpu.VMEM((parts, neigh, rows * rows // 3), tiles.dtype), DMA((parts,))]
     return pl.pallas_call(
-        held_kernel if resident else functools.partial(square_kernel, parts),
-        in_specs=[VMEM if resident else HBM],
+        functools.partial(square_kernel, parts),
+        in_specs=[HBM],
         out_specs=VMEM,
         out_shape=pltpu.VMEM((count, neigh, half, wide), tiles.dtype),
-        scratch_shapes=[] if resident else raw,
+        scratch_shapes=raw,
         compiler_params=params(),
         cost_estimate=HEAVY,
         name="squares",
-    )(*(in_vmem([tiles]) if resident else in_hbm([tiles])))
+    )(*in_hbm([tiles]))
 
 
 def start_near(sides, near, sems):
@@ -206,11 +206,13 @@
     return pltpu.VMEM((sum(c.shape[0] for c in chunks) + 1, rows, sides * cols), chunks[0].dtype)
 
 
-def slab_kernel(n_other, table, first, second, own, *refs):
+def slab_kernel(n_other, table, first, tiles, own, *refs):
     other = refs[:n_other]
-    acc, near, near_sems = refs[-3:]
+    acc, second, near, near_sems = refs[-4:]
     held = (first, second)
-    for load in start_near(([own], other), near, near_sems):
+    loads = start_near(([own], other), near, near_sems)
+    held_kernel(tiles, second)
+    for load in loads:
         load.wait()
 
     def body(b, tiles):
@@ -232,18 +234,21 @@
             each_block(held, spread)
 
 
-def own_slab(table, held, own, other):
+def own_slab(table, held, tiles, own, other):
     cols = own.shape[2]
     return pl.pallas_call(
         functools.partial(slab_kernel, len(other)),
         in_specs=[SMEM] + [VMEM] * 2 + [ANY] * (1 + len(other)),
-        out_specs=VMEM,
-        out_shape=pltpu.VMEM((BLOCKS, 2, held[0].shape[2], 2 * cols), jnp.float32),
+        out_specs=[VMEM, VMEM],
+        out_shape=[
+            pltpu.VMEM((BLOCKS, 2, held.shape[2], 2 * cols), jnp.float32),
+            pltpu.VMEM(held.shape, held.dtype),
+        ],
         scratch_shapes=[near_scratch([own], 2), DMA((1 + len(other),))],
         compiler_params=params(),
         cost_estimate=LIGHT,
         name="own_slab",
-    )(in_smem(table), *in_vmem(held), own, *other)
+    )(in_smem(table), *in_vmem([held, tiles]), own, *other)
 
 
 def largest(power, size):
@@ -452,7 +457,7 @@
         return lax.psum(value, axis)
     value, hop = value + lax.ppermute(value, axis, [(i, i ^ 1) for i in range(size)]), 2
     while hop < size:
-        jumps = (hop, 2 * hop, 3 * hop) if 2 * hop < size else (hop,)
+        jumps = (3 * hop, hop, 2 * hop) if 2 * hop < size else (hop,)
         far = [lax.ppermute(value, axis, [(i, i ^ j) for i in range(size)]) for j in jumps]
         value = value + far[0]
         if len(far) > 1:
@@ -483,12 +488,14 @@
     oth = [across(low), across(high)]
     near_high = pair(high)
     table = ordered(neighbours)
-    held = [squares(tiles, rows, False), squares(sib_tiles, rows, True)]
-    oth[0] = gate(oth[0], held[0], table)
+    held = squares(tiles, rows)
+    oth[0] = gate(oth[0], held, table)
     near_oth = [pair(oth[0]), pair(oth[1])]
     far_high = along(near_high)
     far_oth = [along(near_oth[0]), across(far_high)]
-    acc = own_slab(table, held, fixed, oth)
+    acc, sib_held = own_slab(table, held, sib_tiles, fixed, oth)
+    held = [held, sib_held]
+    far_oth[0] = gate(far_oth[0], acc)
     near_low = pair(gate(low, acc))
     far_low = across(far_oth[0])
 

time: 59.7 us -> 58.9 us (0.987)
  Pallas kernels: 21.6 us -> 20.5 us
  starting transfers between devices: 22.1 us -> 22.9 us
    pallas_call x2 -> x1, Pallas kernels: 4.88 us -> 3.25 us  [squares(): pl.pallas_call(functools.partial(square_kernel, parts), in_specs=[HBM], o...]
    ppermute x2, waiting for transfers between devices: 1.52 us -> 0.05 us  [shards(): far_oth = [along(near_oth[0]), across(far_high)]]
    ppermute x3, starting transfers between devices: 3.49 us -> 4.39 us  [sum_over(): lax.ppermute(value, axis, [(i, i ^ j) for i in range(size)])]
    ppermute x1, waiting for transfers between devices: 1.03 us -> 1.78 us  [shards(): far_low = across(far_oth[0])]
    pallas_call x1, Pallas kernels: 4.24 us -> 4.94 us  [own_slab(): pl.pallas_call(functools.partial(slab_kernel, len(other)), in_specs=[SMEM...]
  transfers between devices with their start and end apart: 16 -> 16, of which waited for: 7 -> 7; matrix products, arithmetic and copies ran while one was open for 2% -> 2% of each run, Pallas kernels for 35% -> 33%
where the time goes in v6:
time: 58.9 us; the launch traced here: 58.7 us
  starting transfers between devices  22.9 us (39%)
  Pallas kernels  20.5 us (35%)
  waiting for transfers between devices  12.9 us (22%)
  local copies, waits for them, and re-layouts  1.09 us (2%)
  between operations  0.73 us (1%)
    pallas_call x1, Pallas kernels, own_rows(): pl.pallas_call(functools.partial(own_kernel, len(chunks), factor), in_spe...  5.72 us
    ppermute x2, starting transfers between devices, shards(): near_oth = [pair(oth[0]), pair(oth[1])]  5.31 us
    pallas_call x1, Pallas kernels, own_slab(): pl.pallas_call(functools.partial(slab_kernel, len(other)), in_specs=[SMEM...  4.94 us
    pallas_call x1, Pallas kernels, other_images(): pl.pallas_call(functools.partial(other_kernel, len(chunks)), in_specs=[SM...  4.53 us
    ppermute x3, starting transfers between devices, sum_over(): lax.ppermute(value, axis, [(i, i ^ j) for i in range(size)])  4.39 us
    ppermute x2, starting transfers between devices, shards(): oth = [across(low), across(high)]  4.06 us
    ppermute x2, waiting for transfers between devices, shards(): near_oth = [pair(oth[0]), pair(oth[1])]  3.99 us
    ppermute x1, waiting for transfers between devices, sum_over(): lax.ppermute(value, axis, [(i, i ^ 1) for i in range(size)])  3.35 us
  transfers between devices with their start and end apart: 16, of which 7 were waited for; matrix products, arithmetic and copies ran while one was open for 2% of the time, Pallas kernels for 33%

profile of v6, /device:TPU:0, one launch (start us, length us, event | category | flops | bytes accessed | tf_op | source)
XLA Modules:
  0.0 58.7 jit_solution(14557128204710403892)
XLA Ops:
  0.6 0.5 collective-permute-start
  1.1 1.1 %fusion = (bf16[6,192,128]{2,1,0:T(8,128)(2,1)S(1)}, bf16[6,192,128]{2,1,0:T(8,128)(2,1)S(1)}) fusion(bf16[12,192,128]{2,1,0:T(8,128)(2,1)} %refs_6_.1), kind=kLoop, calls=%fused_computation.1 | loop fusion | bytes 1179648 | tf_op jit(solution)/shard_map/slice | solution.py:485
  2.2 2.6 %collective-permute-start.1 = (bf16[6,192,128]{2,1,0:T(8,128)(2,1)S(1)}, bf16[6,192,128]{2,1,0:T(8,128)(2,1)S(1)}, u32[]{:S(2)}, u32[]{:S(2)}) collective-permute-start(bf16[6,192,128]{2,1,0:T(8,128)(2,1)S(1)} %get-tuple-element.21.refs_0_), channel_id=1, source_target_pairs={{0,2},{1,3},{2,0},{3,1},{4,6},{5,7},{6,4},{7,5},{8,10},{9,11},{10,... | collective-permute-start | bytes 884744 | tf_op jit(solution)/shard_map/ppermute | solution.py:488
  4.8 0.0 copy-start
  4.8 1.5 %collective-permute-start.6 = (bf16[6,192,128]{2,1,0:T(8,128)(2,1)S(1)}, bf16[6,192,128]{2,1,0:T(8,128)(2,1)S(1)}, u32[]{:S(2)}, u32[]{:S(2)}) collective-permute-start(bf16[6,192,128]{2,1,0:T(8,128)(2,1)S(1)} %get-tuple-element.20), channel_id=1, source_target_pairs={{0,4},{4,0},{8,12},{12,8},{16,20},{20,16},{24,28},{28,24},{1,5},{5... | collective-permute-start | bytes 884744 | tf_op jit(solution)/shard_map/ppermute | solution.py:489
  6.3 3.2 %squares.1.refs_1_.first.first_held = bf16[3,27,96,384]{3,2,1,0:T(8,128)(2,1)S(1)} custom-call(bf16[3,27,36864]{2,1,0:T(8,128)(2,1)} %tiles.1), custom_call_target="tpu_custom_call" | custom-call | flops 1 | bytes 18000000 | tf_op jit(solution)/shard_map/squares/pallas_call | solution.py:133
  9.6 0.0 copy-done
  9.6 1.1 %ordered.1.refs_2_.table = s32[32,128]{1,0:T(8,128)S(4)} custom-call(s32[12,27]{1,0:T(8,128)S(1)} %copy-done), custom_call_target="tpu_custom_call" | custom-call | flops 1 | bytes 1 | tf_op jit(solution)/shard_map/ordered/pallas_call | solution.py:82
  10.8 1.7 %collective-permute-done.1.refs_0_ = bf16[6,192,128]{2,1,0:T(8,128)(2,1)S(1)} collective-permute-done((bf16[6,192,128]{2,1,0:T(8,128)(2,1)S(1)}, bf16[6,192,128]{2,1,0:T(8,128)(2,1)S(1)}, u32[]{:S(2)}, u32[]{:S(2)}) %collective-permute-start.1) | collective-permute-done | bytes 294944 | tf_op jit(solution)/shard_map/ppermute | solution.py:488
  12.5 1.8 %collective-permute-start.3 = (bf16[6,192,128]{2,1,0:T(8,128)(2,1)S(1)}, bf16[6,192,128]{2,1,0:T(8,128)(2,1)S(1)}, u32[]{:S(2)}, u32[]{:S(2)}) collective-permute-start(bf16[6,192,128]{2,1,0:T(8,128)(2,1)S(1)} %gate.4.refs_0_), channel_id=1, source_target_pairs={{0,4},{4,0},{8,12},{12,8},{16,20},{20,16},{24,28},{28,24},{1,5},{5... | collective-permute-start | bytes 884744 | tf_op jit(solution)/shard_map/ppermute | solution.py:493
  14.2 1.5 %collective-permute-start.2 = (bf16[6,192,128]{2,1,0:T(8,128)(2,1)S(1)}, bf16[6,192,128]{2,1,0:T(8,128)(2,1)S(1)}, u32[]{:S(2)}, u32[]{:S(2)}) collective-permute-start(bf16[6,192,128]{2,1,0:T(8,128)(2,1)S(1)} %get-tuple-element.20), channel_id=1, source_target_pairs={{0,2},{1,3},{2,0},{3,1},{4,6},{5,7},{6,4},{7,5},{8,10},{9,11},{10,... | collective-permute-start | bytes 884744 | tf_op jit(solution)/shard_map/ppermute | solution.py:488
  15.7 0.0 collective-permute-done.6.refs_1_
  15.7 1.6 %collective-permute-start.7 = (bf16[6,192,128]{2,1,0:T(8,128)(2,1)S(1)}, bf16[6,192,128]{2,1,0:T(8,128)(2,1)S(1)}, u32[]{:S(2)}, u32[]{:S(2)}) collective-permute-start(bf16[6,192,128]{2,1,0:T(8,128)(2,1)S(1)} %collective-permute-done.6.refs_1_), channel_id=1, source_target_pairs={{0,8},{4,28},{8,16},{12,4},{16,24},{20,12},{24,0},{28,20},{1,9},{5... | collective-permute-start | bytes 884744 | tf_op jit(solution)/shard_map/ppermute | solution.py:494
  17.3 4.0 %collective-permute-done.3.refs_0_ = bf16[6,192,128]{2,1,0:T(8,128)(2,1)S(1)} collective-permute-done((bf16[6,192,128]{2,1,0:T(8,128)(2,1)S(1)}, bf16[6,192,128]{2,1,0:T(8,128)(2,1)S(1)}, u32[]{:S(2)}, u32[]{:S(2)}) %collective-permute-start.3) | collective-permute-done | bytes 294944 | tf_op jit(solution)/shard_map/ppermute | solution.py:493
  21.3 1.6 %collective-permute-start.5 = (bf16[6,192,128]{2,1,0:T(8,128)(2,1)S(1)}, bf16[6,192,128]{2,1,0:T(8,128)(2,1)S(1)}, u32[]{:S(2)}, u32[]{:S(2)}) collective-permute-start(bf16[6,192,128]{2,1,0:T(8,128)(2,1)S(1)} %collective-permute-done.3.refs_0_), channel_id=1, source_target_pairs={{0,8},{4,28},{8,16},{12,4},{16,24},{20,12},{24,0},{28,20},{1,9},{5... | collective-permute-start | bytes 884744 | tf_op jit(solution)/shard_map/ppermute | solution.py:495
  22.9 0.0 collective-permute-done.2.refs_1_
  22.9 3.5 %collective-permute-start.4 = (bf16[6,192,128]{2,1,0:T(8,128)(2,1)S(1)}, bf16[6,192,128]{2,1,0:T(8,128)(2,1)S(1)}, u32[]{:S(2)}, u32[]{:S(2)}) collective-permute-start(bf16[6,192,128]{2,1,0:T(8,128)(2,1)S(1)} %collective-permute-done.2.refs_1_), channel_id=1, source_target_pairs={{0,4},{4,0},{8,12},{12,8},{16,20},{20,16},{24,28},{28,24},{1,5},{5... | collective-permute-start | bytes 884744 | tf_op jit(solution)/shard_map/ppermute | solution.py:493
  26.5 0.0 collective-permute-done.7.refs_3_
  26.5 1.5 %collective-permute-start.8 = (bf16[6,192,128]{2,1,0:T(8,128)(2,1)S(1)}, bf16[6,192,128]{2,1,0:T(8,128)(2,1)S(1)}, u32[]{:S(2)}, u32[]{:S(2)}) collective-permute-start(bf16[6,192,128]{2,1,0:T(8,128)(2,1)S(1)} %collective-permute-done.7.refs_3_), channel_id=1, source_target_pairs={{0,2},{1,3},{2,0},{3,1},{4,6},{5,7},{6,4},{7,5},{8,10},{9,11},{10,... | collective-permute-start | bytes 884744 | tf_op jit(solution)/shard_map/ppermute | solution.py:495
  28.0 0.0 collective-permute-done.tiles
  28.0 4.9 %own_slab.1 = (f32[6,2,96,256]{3,2,1,0:T(8,128)S(1)}, bf16[3,27,96,384]{3,2,1,0:T(8,128)(2,1)S(1)}) custom-call(s32[32,128]{1,0:T(8,128)S(4)} %ordered.1.refs_2_.table, bf16[3,27,96,384]{3,2,1,0:T(8,128)(2,1)S(1)} %squares.1.refs_1_.first.first_held, bf16[3,27,36864]{2,1,0:T(8,128)(2,1)S(1)} %collective-permute-done.tiles, bf16[12,192,128]{2,1,0:T(8,128)(2,1)} %refs_6_.1, ...), custom_call_target="tpu_custom_call" | custom-call | flops 1 | bytes 1 | tf_op jit(solution)/shard_map/own_slab/pallas_call | solution.py:239
  32.9 0.0 collective-permute-done.5.refs_0_
  32.9 0.6 %collective-permute-start.10 = (bf16[6,192,128]{2,1,0:T(8,128)(2,1)S(1)}, bf16[6,192,128]{2,1,0:T(8,128)(2,1)S(1)}, u32[]{:S(2)}, u32[]{:S(2)}) collective-permute-start(bf16[6,192,128]{2,1,0:T(8,128)(2,1)S(1)} %gate.5.refs_2_), channel_id=1, source_target_pairs={{0,2},{1,3},{2,0},{3,1},{4,6},{5,7},{6,4},{7,5},{8,10},{9,11},{10,... | collective-permute-start | bytes 884744 | tf_op jit(solution)/shard_map/ppermute | solution.py:500
  33.6 0.0 collective-permute-start.9
  33.6 0.0 collective-permute-done.4.refs_1_
  33.6 0.0 collective-permute-done.8.refs_3_
  33.7 4.5 %other_images.1.refs_0_ = s16[1168,128]{1,0:T(8,128)(2,1)S(1)} custom-call(s32[32,128]{1,0:T(8,128)S(4)} %ordered.1.refs_2_.table, f32[6,2,96,256]{3,2,1,0:T(8,128)S(1)} %get-tuple-element.11.refs_1_.acc, bf16[3,27,96,384]{3,2,1,0:T(8,128)(2,1)S(1)} %squares.1.refs_1_.first.first_held, bf16[3,27,96,384]{3,2,1,0:T(8,128)(2,1)S(1)} %get-tuple-element.12.second.second_held, ...), custom_call_target="tpu_custom_call" | custom-call | flops 1 | bytes 1000000000 | tf_op jit(solution)/shard_map/other_images/pallas_call | solution.py:305
  38.2 1.8 %collective-permute-done.10.refs_2_ = bf16[6,192,128]{2,1,0:T(8,128)(2,1)S(1)} collective-permute-done((bf16[6,192,128]{2,1,0:T(8,128)(2,1)S(1)}, bf16[6,192,128]{2,1,0:T(8,128)(2,1)S(1)}, u32[]{:S(2)}, u32[]{:S(2)}) %collective-permute-start.10) | collective-permute-done | bytes 294944 | tf_op jit(solution)/shard_map/ppermute | solution.py:500
  40.0 0.3 collective-permute-done.9.refs_1_.refs_0_
  40.3 1.5 %collective-permute-start.11 = (s16[1168,128]{1,0:T(8,128)(2,1)S(1)}, s16[1168,128]{1,0:T(8,128)(2,1)S(1)}, u32[]{:S(2)}, u32[]{:S(2)}) collective-permute-start(s16[1168,128]{1,0:T(8,128)(2,1)S(1)} %gate.7.refs_7_), channel_id=1, source_target_pairs={{0,2},{1,3},{2,0},{3,1},{4,6},{5,7},{6,4},{7,5},{8,10},{9,11},{10,... | collective-permute-start | bytes 897032 | tf_op jit(solution)/shard_map/ppermute | solution.py:504
  41.8 5.7 %own_rows.1 = (f32[12,192,128]{2,1,0:T(8,128)}, f32[16,128]{1,0:T(8,128)S(1)}, f32[6,192,128]{2,1,0:T(8,128)S(1)}, f32[6,192,128]{2,1,0:T(8,128)S(1)}, bf16[6,192,128]{2,1,0:T(8,128)(2,1)S(1)}) custom-call(s32[32,128]{1,0:T(8,128)S(4)} %ordered.1.refs_2_.table, f32[6,2,96,256]{3,2,1,0:T(8,128)S(1)} %get-tuple-element.11.refs_1_.acc, ...), custom_call_target="tpu_custom_call" | custom-call | flops 1 | bytes 1000000000 | tf_op jit(solution)/shard_map/own_rows/pallas_call | solution.py:378
  47.5 0.0 collective-permute-done.11.coded
  47.5 0.9 %other_rows.1 = (f32[12,192,128]{2,1,0:T(8,128)}, f32[2,128]{1,0:T(2,128)S(1)}) custom-call(s16[1168,128]{1,0:T(8,128)(2,1)S(1)} %collective-permute-done.11.coded, f32[6,192,128]{2,1,0:T(8,128)S(1)} %get-tuple-element.13.prev, f32[6,192,128]{2,1,0:T(8,128)S(1)} %get-tuple-element.14.probes, ...), custom_call_target="tpu_custom_call", output_to_operand_aliasing={{0}: (5, {})} | custom-call | flops 1 | bytes 1 | tf_op jit(solution)/shard_map/other_rows/pallas_call | solution.py:425
  48.4 0.3 collective-permute-start.12
  48.7 3.3 %collective-permute-done.12 = f32[2,128]{1,0:T(2,128)S(1)} collective-permute-done((f32[2,128]{1,0:T(2,128)S(1)}, f32[2,128]{1,0:T(2,128)S(1)}, u32[]{:S(2)}, u32[]{:S(2)}) %collective-permute-start.12) | collective-permute-done | bytes 1056 | tf_op jit(solution)/shard_map/ppermute | solution.py:458
  52.1 1.6 %collective-permute-start.13 = (f32[2,128]{1,0:T(2,128)S(1)}, f32[2,128]{1,0:T(2,128)S(1)}, u32[]{:S(2)}, u32[]{:S(2)}) collective-permute-start(f32[2,128]{1,0:T(2,128)S(1)} %add.12), channel_id=1, source_target_pairs={{0,24},{4,28},{8,16},{12,20},{16,8},{20,12},{24,0},{28,4},{1,25},{... | collective-permute-start | bytes 3080 | tf_op jit(solution)/shard_map/ppermute | solution.py:461
  53.6 0.0 collective-permute-start.14
  53.6 2.8 %collective-permute-start.15 = (f32[2,128]{1,0:T(2,128)S(1)}, f32[2,128]{1,0:T(2,128)S(1)}, u32[]{:S(2)}, u32[]{:S(2)}) collective-permute-start(f32[2,128]{1,0:T(2,128)S(1)} %add.12), channel_id=1, source_target_pairs={{0,16},{4,20},{8,24},{12,28},{16,0},{20,4},{24,8},{28,12},{1,17},{... | collective-permute-start | bytes 3080 | tf_op jit(solution)/shard_map/ppermute | solution.py:461
  56.5 1.0 %collective-permute-done.13 = f32[2,128]{1,0:T(2,128)S(1)} collective-permute-done((f32[2,128]{1,0:T(2,128)S(1)}, f32[2,128]{1,0:T(2,128)S(1)}, u32[]{:S(2)}, u32[]{:S(2)}) %collective-permute-start.13) | collective-permute-done | bytes 1056 | tf_op jit(solution)/shard_map/ppermute | solution.py:461
  57.4 0.0 collective-permute-done.14
  57.4 0.7 %collective-permute-done.15 = f32[2,128]{1,0:T(2,128)S(1)} collective-permute-done((f32[2,128]{1,0:T(2,128)S(1)}, f32[2,128]{1,0:T(2,128)S(1)}, u32[]{:S(2)}, u32[]{:S(2)}) %collective-permute-start.15) | collective-permute-done | bytes 1056 | tf_op jit(solution)/shard_map/ppermute | solution.py:461
  58.1 0.6 add_add_fusion
  (5 shorter events, 0.0 us)
Async XLA Ops:
  0.6 27.3 %collective-permute-start = (bf16[3,27,36864]{2,1,0:T(8,128)(2,1)}, bf16[3,27,36864]{2,1,0:T(8,128)(2,1)S(1)}, u32[]{:S(2)}, u32[]{:S(2)}) collective-permute-start(bf16[3,27,36864]{2,1,0:T(8,128)(2,1)} %tiles.1), channel_id=1, source_target_pairs={{0,1},{1,0},{2,3},{3,2},{4,5},{5,4},{6,7},{7,6},{8,9},{9,8},{10,11... | collective-permute-start | bytes 17915912 | tf_op jit(solution)/shard_map/ppermute | solution.py:487
  2.2 10.2 %collective-permute-start.1 = (bf16[6,192,128]{2,1,0:T(8,128)(2,1)S(1)}, bf16[6,192,128]{2,1,0:T(8,128)(2,1)S(1)}, u32[]{:S(2)}, u32[]{:S(2)}) collective-permute-start(bf16[6,192,128]{2,1,0:T(8,128)(2,1)S(1)} %get-tuple-element.21.refs_0_), channel_id=1, source_target_pairs={{0,2},{1,3},{2,0},{3,1},{4,6},{5,7},{6,4},{7,5},{8,10},{9,11},{10,... | collective-permute-start | bytes 884744 | tf_op jit(solution)/shard_map/ppermute | solution.py:488
  4.8 4.8 %copy-start = (s32[12,27]{1,0:T(8,128)S(1)}, s32[12,27]{1,0:T(8,128)}, u32[]{:S(2)}) copy-start(s32[12,27]{1,0:T(8,128)} %neighbours.1) | copy-start | bytes 3892
  4.8 10.9 %collective-permute-start.6 = (bf16[6,192,128]{2,1,0:T(8,128)(2,1)S(1)}, bf16[6,192,128]{2,1,0:T(8,128)(2,1)S(1)}, u32[]{:S(2)}, u32[]{:S(2)}) collective-permute-start(bf16[6,192,128]{2,1,0:T(8,128)(2,1)S(1)} %get-tuple-element.20), channel_id=1, source_target_pairs={{0,4},{4,0},{8,12},{12,8},{16,20},{20,16},{24,28},{28,24},{1,5},{5... | collective-permute-start | bytes 884744 | tf_op jit(solution)/shard_map/ppermute | solution.py:489
  12.5 8.8 %collective-permute-start.3 = (bf16[6,192,128]{2,1,0:T(8,128)(2,1)S(1)}, bf16[6,192,128]{2,1,0:T(8,128)(2,1)S(1)}, u32[]{:S(2)}, u32[]{:S(2)}) collective-permute-start(bf16[6,192,128]{2,1,0:T(8,128)(2,1)S(1)} %gate.4.refs_0_), channel_id=1, source_target_pairs={{0,4},{4,0},{8,12},{12,8},{16,20},{20,16},{24,28},{28,24},{1,5},{5... | collective-permute-start | bytes 884744 | tf_op jit(solution)/shard_map/ppermute | solution.py:493
  14.2 8.7 %collective-permute-start.2 = (bf16[6,192,128]{2,1,0:T(8,128)(2,1)S(1)}, bf16[6,192,128]{2,1,0:T(8,128)(2,1)S(1)}, u32[]{:S(2)}, u32[]{:S(2)}) collective-permute-start(bf16[6,192,128]{2,1,0:T(8,128)(2,1)S(1)} %get-tuple-element.20), channel_id=1, source_target_pairs={{0,2},{1,3},{2,0},{3,1},{4,6},{5,7},{6,4},{7,5},{8,10},{9,11},{10,... | collective-permute-start | bytes 884744 | tf_op jit(solution)/shard_map/ppermute | solution.py:488
  15.7 10.8 %collective-permute-start.7 = (bf16[6,192,128]{2,1,0:T(8,128)(2,1)S(1)}, bf16[6,192,128]{2,1,0:T(8,128)(2,1)S(1)}, u32[]{:S(2)}, u32[]{:S(2)}) collective-permute-start(bf16[6,192,128]{2,1,0:T(8,128)(2,1)S(1)} %collective-permute-done.6.refs_1_), channel_id=1, source_target_pairs={{0,8},{4,28},{8,16},{12,4},{16,24},{20,12},{24,0},{28,20},{1,9},{5... | collective-permute-start | bytes 884744 | tf_op jit(solution)/shard_map/ppermute | solution.py:494
  21.3 11.6 %collective-permute-start.5 = (bf16[6,192,128]{2,1,0:T(8,128)(2,1)S(1)}, bf16[6,192,128]{2,1,0:T(8,128)(2,1)S(1)}, u32[]{:S(2)}, u32[]{:S(2)}) collective-permute-start(bf16[6,192,128]{2,1,0:T(8,128)(2,1)S(1)} %collective-permute-done.3.refs_0_), channel_id=1, source_target_pairs={{0,8},{4,28},{8,16},{12,4},{16,24},{20,12},{24,0},{28,20},{1,9},{5... | collective-permute-start | bytes 884744 | tf_op jit(solution)/shard_map/ppermute | solution.py:495
  22.9 10.7 %collective-permute-start.4 = (bf16[6,192,128]{2,1,0:T(8,128)(2,1)S(1)}, bf16[6,192,128]{2,1,0:T(8,128)(2,1)S(1)}, u32[]{:S(2)}, u32[]{:S(2)}) collective-permute-start(bf16[6,192,128]{2,1,0:T(8,128)(2,1)S(1)} %collective-permute-done.2.refs_1_), channel_id=1, source_target_pairs={{0,4},{4,0},{8,12},{12,8},{16,20},{20,16},{24,28},{28,24},{1,5},{5... | collective-permute-start | bytes 884744 | tf_op jit(solution)/shard_map/ppermute | solution.py:493
  26.5 7.1 %collective-permute-start.8 = (bf16[6,192,128]{2,1,0:T(8,128)(2,1)S(1)}, bf16[6,192,128]{2,1,0:T(8,128)(2,1)S(1)}, u32[]{:S(2)}, u32[]{:S(2)}) collective-permute-start(bf16[6,192,128]{2,1,0:T(8,128)(2,1)S(1)} %collective-permute-done.7.refs_3_), channel_id=1, source_target_pairs={{0,2},{1,3},{2,0},{3,1},{4,6},{5,7},{6,4},{7,5},{8,10},{9,11},{10,... | collective-permute-start | bytes 884744 | tf_op jit(solution)/shard_map/ppermute | solution.py:495
  32.9 7.0 %collective-permute-start.10 = (bf16[6,192,128]{2,1,0:T(8,128)(2,1)S(1)}, bf16[6,192,128]{2,1,0:T(8,128)(2,1)S(1)}, u32[]{:S(2)}, u32[]{:S(2)}) collective-permute-start(bf16[6,192,128]{2,1,0:T(8,128)(2,1)S(1)} %gate.5.refs_2_), channel_id=1, source_target_pairs={{0,2},{1,3},{2,0},{3,1},{4,6},{5,7},{6,4},{7,5},{8,10},{9,11},{10,... | collective-permute-start | bytes 884744 | tf_op jit(solution)/shard_map/ppermute | solution.py:500
  33.6 6.7 %collective-permute-start.9 = (bf16[6,192,128]{2,1,0:T(8,128)(2,1)S(1)}, bf16[6,192,128]{2,1,0:T(8,128)(2,1)S(1)}, u32[]{:S(2)}, u32[]{:S(2)}) collective-permute-start(bf16[6,192,128]{2,1,0:T(8,128)(2,1)S(1)} %gate.6), channel_id=1, source_target_pairs={{0,4},{4,0},{8,12},{12,8},{16,20},{20,16},{24,28},{28,24},{1,5},{5... | collective-permute-start | bytes 884744 | tf_op jit(solution)/shard_map/ppermute | solution.py:499
  40.3 7.2 %collective-permute-start.11 = (s16[1168,128]{1,0:T(8,128)(2,1)S(1)}, s16[1168,128]{1,0:T(8,128)(2,1)S(1)}, u32[]{:S(2)}, u32[]{:S(2)}) collective-permute-start(s16[1168,128]{1,0:T(8,128)(2,1)S(1)} %gate.7.refs_7_), channel_id=1, source_target_pairs={{0,2},{1,3},{2,0},{3,1},{4,6},{5,7},{6,4},{7,5},{8,10},{9,11},{10,... | collective-permute-start | bytes 897032 | tf_op jit(solution)/shard_map/ppermute | solution.py:504
  48.4 3.6 %collective-permute-start.12 = (f32[2,128]{1,0:T(2,128)S(1)}, f32[2,128]{1,0:T(2,128)S(1)}, u32[]{:S(2)}, u32[]{:S(2)}) collective-permute-start(f32[2,128]{1,0:T(2,128)S(1)} %get-tuple-element.19), channel_id=1, source_target_pairs={{0,4},{4,0},{8,12},{12,8},{16,20},{20,16},{24,28},{28,24},{1,5},{5... | collective-permute-start | bytes 3080 | tf_op jit(solution)/shard_map/ppermute | solution.py:458
  52.1 5.4 %collective-permute-start.13 = (f32[2,128]{1,0:T(2,128)S(1)}, f32[2,128]{1,0:T(2,128)S(1)}, u32[]{:S(2)}, u32[]{:S(2)}) collective-permute-start(f32[2,128]{1,0:T(2,128)S(1)} %add.12), channel_id=1, source_target_pairs={{0,24},{4,28},{8,16},{12,20},{16,8},{20,12},{24,0},{28,4},{1,25},{... | collective-permute-start | bytes 3080 | tf_op jit(solution)/shard_map/ppermute | solution.py:461
  53.6 3.8 %collective-permute-start.14 = (f32[2,128]{1,0:T(2,128)S(1)}, f32[2,128]{1,0:T(2,128)S(1)}, u32[]{:S(2)}, u32[]{:S(2)}) collective-permute-start(f32[2,128]{1,0:T(2,128)S(1)} %add.12), channel_id=1, source_target_pairs={{0,8},{4,12},{8,0},{12,4},{16,24},{20,28},{24,16},{28,20},{1,9},{5... | collective-permute-start | bytes 3080 | tf_op jit(solution)/shard_map/ppermute | solution.py:461
  53.6 4.5 %collective-permute-start.15 = (f32[2,128]{1,0:T(2,128)S(1)}, f32[2,128]{1,0:T(2,128)S(1)}, u32[]{:S(2)}, u32[]{:S(2)}) collective-permute-start(f32[2,128]{1,0:T(2,128)S(1)} %add.12), channel_id=1, source_target_pairs={{0,16},{4,20},{8,24},{12,28},{16,0},{20,4},{24,8},{28,12},{1,17},{... | collective-permute-start | bytes 3080 | tf_op jit(solution)/shard_map/ppermute | solution.py:461
